TPU v7x, 32 devices: a whole 2x2x4 slice. The times are simulated.
32 devices in a mesh: section: 2 (over x), tensor: 4 (over y, core), dp: 4 (over z).
Axes of the slice: x: 2, y: 2, z: 4, core: 2. Of those that a mesh axis runs over, the one named last changes fastest.
Arguments:
- inputs: bfloat16 [8, 1024, 1280], P('dp', 'tensor'), may hold values from -6 to 6
- cotangent: bfloat16 [8, 1024, 1280], P('dp', 'tensor'), may hold values from -6 to 6
- gain_attn: float32 [2, 1280], P('section'), may hold values from 0.25 to 1.75
- w_query: bfloat16 [2, 1280, 1280], P('section', None, 'tensor'), may hold values from -0.15625 to 0.15625
- w_key: bfloat16 [2, 1280, 1280], P('section', None, 'tensor'), may hold values from -0.15625 to 0.15625
- w_value: bfloat16 [2, 1280, 1280], P('section', None, 'tensor'), may hold values from -0.15625 to 0.15625
- w_out: bfloat16 [2, 1280, 1280], P('section', 'tensor'), may hold values from -0.625 to 0.625
- dim_scale: float32 [2, 80], P('section'), may hold values from -1 to 1.5
- gain_mlp: float32 [2, 1280], P('section'), may hold values from 0.25 to 1.75
- w_up: bfloat16 [2, 1280, 1280], P('section', None, 'tensor'), may hold values from -0.15625 to 0.15625
- w_down: bfloat16 [2, 1280, 1280], P('section', 'tensor'), may hold values from -0.15625 to 0.15625
Outputs:
- layer_out: bfloat16 [2, 8, 1024, 1280], P('section', 'dp', 'tensor')
- input_grads: bfloat16 [2, 8, 1024, 1280], P('section', 'dp', 'tensor')
- grad_gain_attn: float32 [2, 1280], P('section')
- grad_query: float32 [2, 1280, 1280], P('section', 'dp', 'tensor')
- grad_key: float32 [2, 1280, 1280], P('section', 'dp', 'tensor')
- grad_value: float32 [2, 1280, 1280], P('section', 'dp', 'tensor')
- grad_out: float32 [2, 1280, 1280], P('section', 'tensor', 'dp')
- grad_scale: float32 [2, 80], P('section')
- gradient_feedforward_gain: float32 [2, 1280], P('section')
- grad_up: float32 [2, 1280, 1280], P('section', 'dp', 'tensor')
- grad_down: float32 [2, 1280, 1280], P('section', 'tensor', 'dp')
All inputs are finite; a program needn't handle non-finite values.
Results may differ from a plain program's by a relative error of at most 0.025.
The roundings to bfloat16 on the way count: a program that leaves them out, or rounds other values in their place, can miss the bound.
Values may be sent and summed in bfloat16 or wider, within the bound.
A program may use at most 192 MiB of HBM per device.

v0:
```python
import math

import jax
import jax.numpy as jnp
from jax import lax
from jax.sharding import PartitionSpec as P

EPS = 1e-06
LOG2E = 1.442695041
NEGATIVE = -1e30
CONTRACT_ROWS = (((0,), (0,)), ((), ()))
CONTRACT_LAST = (((1,), (1,)), ((), ()))


def from_behind(block, axis, distance):
    devices = range(lax.axis_size(axis))
    route = [(i - distance, i) for i in devices if i - distance in devices]
    return lax.ppermute(block, axis, route)


def norm_forward(hidden, gain):
    inverse = lax.rsqrt(jnp.mean(hidden * hidden, axis=1, keepdims=True) + EPS)
    return (hidden * inverse * gain, inverse)


def norm_backward(hidden, inverse, gain, grad_normed):
    unit = hidden * inverse
    grad_unit = grad_normed * gain
    grad_gain = jnp.sum(grad_normed * unit, axis=0)
    grad_hidden = inverse * (grad_unit - unit * jnp.mean(grad_unit * unit, axis=1, keepdims=True))
    return (grad_hidden, grad_gain)


def masked_scores(q_block, keys, start):
    block = q_block.shape[0]
    scores = jnp.einsum("qhd,khd->hqk", q_block, keys, preferred_element_type=jnp.float32)
    rows_at = start + lax.iota(jnp.int32, block)
    cols_at = lax.iota(jnp.int32, keys.shape[0])
    keep = rows_at[:, None] >= cols_at[None, :]
    return (jnp.where(keep[None], scores, NEGATIVE), keep)


def attend(queries, keys, values, block):
    starts = jnp.arange(queries.shape[0] // block, dtype=jnp.int32) * block

    def one_block(start):
        q_block = lax.dynamic_slice_in_dim(queries, start, block, 0)
        scores, keep = masked_scores(q_block, keys, start)
        top = jnp.max(scores, axis=2, keepdims=True)
        weights = jnp.exp(scores - top)
        total = jnp.sum(weights, axis=2, keepdims=True)
        probs = (weights / total).astype(jnp.bfloat16)
        mixed = jnp.einsum("hqk,khd->qhd", probs, values, preferred_element_type=jnp.float32)
        return (mixed, top + jnp.log(total))

    mixed, logsum = lax.map(one_block, starts)
    return (mixed.reshape(queries.shape).astype(jnp.bfloat16), logsum)


def attend_back(queries, keys, values, logsum, grad_mixed, block):
    starts = jnp.arange(queries.shape[0] // block, dtype=jnp.int32) * block

    def one_block(carry, inputs_here):
        start, block_sum = inputs_here
        grad_keys, grad_values = carry
        q_block = lax.dynamic_slice_in_dim(queries, start, block, 0)
        g_block = lax.dynamic_slice_in_dim(grad_mixed, start, block, 0)
        scores, keep = masked_scores(q_block, keys, start)
        probs = jnp.where(keep[None], jnp.exp(scores - block_sum), 0.0)
        grad_probs = jnp.einsum("qhd,khd->hqk", g_block, values, preferred_element_type=jnp.float32)
        grad_values = grad_values + jnp.einsum(
            "hqk,qhd->khd", probs.astype(jnp.bfloat16), g_block, preferred_element_type=jnp.float32
        )
        inner = jnp.sum(probs * grad_probs, axis=2, keepdims=True)
        grad_scores = (probs * (grad_probs - inner)).astype(jnp.bfloat16)
        grad_query = jnp.einsum(
            "hqk,khd->qhd", grad_scores, keys, preferred_element_type=jnp.float32
        )
        grad_keys = grad_keys + jnp.einsum(
            "hqk,qhd->khd", grad_scores, q_block, preferred_element_type=jnp.float32
        )
        return ((grad_keys, grad_values), grad_query)

    zeros = jnp.zeros(keys.shape, jnp.float32)
    (grad_keys, grad_values), grad_query = lax.scan(one_block, (zeros, zeros), (starts, logsum))
    return (grad_query.reshape(queries.shape), grad_keys, grad_values)


def body(
    inputs, cotangent, gain_attn, w_query, w_key, w_value, w_out, dim_scale, gain_mlp, w_up, w_down
):
    first_section = lax.axis_index("section") == 0
    micro, rows, width = inputs.shape
    length = rows * lax.axis_size("tensor")
    block = min(512, length)
    local = w_query.shape[2]
    head = dim_scale.shape[1]
    heads_here = local // head
    gain_one = gain_attn[0]
    gain_two = gain_mlp[0]
    w_in = jnp.concatenate([w_query[0], w_key[0], w_value[0]], axis=1)
    w_o = w_out[0]
    w_u = w_up[0]
    w_d = w_down[0]
    multiplier = LOG2E / math.sqrt(head)
    scale_vec = jnp.tile(multiplier * jax.nn.softplus(dim_scale[0]), heads_here)
    received = jnp.zeros((rows, width), jnp.bfloat16)
    records = []
    outputs = []
    for tick in range(micro + 1):
        own = inputs[min(tick, micro - 1)]
        entering = jnp.where(first_section, own, received)
        forward_hidden = entering.astype(jnp.float32)
        normed, forward_inverse_one = norm_forward(forward_hidden, gain_one)
        forward_normed_all = lax.all_gather(
            normed.astype(jnp.bfloat16), "tensor", axis=0, tiled=True
        )
        projected = jnp.dot(forward_normed_all, w_in, preferred_element_type=jnp.float32)
        attention_query_raw = projected[:, :local]
        attention_queries = (
            (attention_query_raw * scale_vec).astype(jnp.bfloat16).reshape(length, heads_here, head)
        )
        attention_keys = (
            projected[:, local : 2 * local].astype(jnp.bfloat16).reshape(length, heads_here, head)
        )
        attention_values = (
            projected[:, 2 * local :].astype(jnp.bfloat16).reshape(length, heads_here, head)
        )
        attention_mixed, attention_logsum = attend(
            attention_queries, attention_keys, attention_values, block
        )
        forward_mixed = attention_mixed.reshape(length, local)
        forward_middle = forward_hidden + lax.psum_scatter(
            jnp.dot(forward_mixed, w_o, preferred_element_type=jnp.float32),
            "tensor",
            scatter_dimension=0,
            tiled=True,
        )
        normed_two, forward_inverse_two = norm_forward(forward_middle, gain_two)
        forward_normed_two_all = lax.all_gather(
            normed_two.astype(jnp.bfloat16), "tensor", axis=0, tiled=True
        )
        forward_upward = jnp.dot(forward_normed_two_all, w_u, preferred_element_type=jnp.float32)
        forward_activated = jax.nn.silu(forward_upward).astype(jnp.bfloat16)
        computed_result = forward_middle + lax.psum_scatter(
            jnp.dot(forward_activated, w_d, preferred_element_type=jnp.float32),
            "tensor",
            scatter_dimension=0,
            tiled=True,
        )
        forward_record = (
            forward_hidden,
            forward_inverse_one,
            forward_normed_all,
            attention_query_raw,
            attention_queries,
            attention_keys,
            attention_values,
            forward_mixed,
            attention_logsum,
            forward_middle,
            forward_inverse_two,
            forward_normed_two_all,
            forward_upward,
            forward_activated,
        )
        computed_result, record = (computed_result, forward_record)
        sent = computed_result.astype(jnp.bfloat16)
        outputs.append(sent)
        records.append(record)
        if tick < micro:
            received = from_behind(sent, "section", 1)
    layer_out = jnp.where(first_section, jnp.stack(outputs[:micro]), jnp.stack(outputs[1:]))
    back_in = jnp.zeros((rows, width), jnp.float32)
    grad_list = []
    totals = None
    small_totals = None
    for step in range(micro + 1):
        if step < micro:
            from_loss = cotangent[micro - 1 - step].astype(jnp.float32)
        else:
            from_loss = jnp.zeros((rows, width), jnp.float32)
        upper = jnp.where(first_section, back_in, from_loss)
        (
            hidden,
            inverse_one,
            normed_all,
            query_raw,
            queries,
            keys,
            values,
            mixed,
            logsum,
            middle,
            inverse_two,
            normed_two_all,
            upward,
            activated,
        ) = records[micro - step]
        grad_branch_all = lax.all_gather(upper.astype(jnp.bfloat16), "tensor", axis=0, tiled=True)
        backward_grad_w_d = lax.dot_general(
            activated, grad_branch_all, CONTRACT_ROWS, preferred_element_type=jnp.float32
        )
        grad_act = lax.dot_general(
            grad_branch_all, w_d, CONTRACT_LAST, preferred_element_type=jnp.float32
        )
        sigma = jax.nn.sigmoid(upward)
        grad_upward = (grad_act * sigma * (1.0 + upward * (1.0 - sigma))).astype(jnp.bfloat16)
        backward_grad_w_u = lax.dot_general(
            normed_two_all, grad_upward, CONTRACT_ROWS, preferred_element_type=jnp.float32
        )
        grad_normed_two = lax.psum_scatter(
            lax.dot_general(grad_upward, w_u, CONTRACT_LAST, preferred_element_type=jnp.float32),
            "tensor",
            scatter_dimension=0,
            tiled=True,
        )
        grad_mid_norm, grad_gain_two = norm_backward(middle, inverse_two, gain_two, grad_normed_two)
        grad_middle = upper + grad_mid_norm
        grad_attn_all = lax.all_gather(
            grad_middle.astype(jnp.bfloat16), "tensor", axis=0, tiled=True
        )
        backward_gradient_output_weight = lax.dot_general(
            mixed, grad_attn_all, CONTRACT_ROWS, preferred_element_type=jnp.float32
        )
        grad_mixed = lax.dot_general(
            grad_attn_all, w_o, CONTRACT_LAST, preferred_element_type=jnp.float32
        )
        grad_mixed = grad_mixed.astype(jnp.bfloat16).reshape(length, heads_here, head)
        grad_scaled, grad_keys, grad_values = attend_back(
            queries, keys, values, logsum, grad_mixed, block
        )
        grad_scaled = grad_scaled.reshape(length, local)
        unbounded_scale = jnp.sum(
            (grad_scaled * query_raw).reshape(length, heads_here, head), axis=(0, 1)
        )
        grad_proj = jnp.concatenate(
            [
                (grad_scaled * scale_vec).astype(jnp.bfloat16),
                grad_keys.reshape(length, local).astype(jnp.bfloat16),
                grad_values.reshape(length, local).astype(jnp.bfloat16),
            ],
            axis=1,
        )
        backward_grad_w_in = lax.dot_general(
            normed_all, grad_proj, CONTRACT_ROWS, preferred_element_type=jnp.float32
        )
        grad_normed_one = lax.psum_scatter(
            lax.dot_general(grad_proj, w_in, CONTRACT_LAST, preferred_element_type=jnp.float32),
            "tensor",
            scatter_dimension=0,
            tiled=True,
        )
        grad_in_norm, grad_gain_one = norm_backward(hidden, inverse_one, gain_one, grad_normed_one)
        grad_input = grad_middle + grad_in_norm
        grad_input, big, small = (
            grad_input,
            (
                backward_grad_w_in,
                backward_gradient_output_weight,
                backward_grad_w_u,
                backward_grad_w_d,
            ),
            (grad_gain_one, grad_gain_two, unbounded_scale),
        )
        grad_sent = grad_input.astype(jnp.bfloat16)
        grad_list.append(grad_sent)
        if step < micro:
            back_in = from_behind(grad_sent, "section", -1).astype(jnp.float32)
        if totals is None:
            totals = big
            small_totals = small
        else:
            totals = jax.tree.map(jnp.add, totals, big)
            small_totals = jax.tree.map(jnp.add, small_totals, small)
    shares = (
        lax.psum_scatter(totals[0], "dp", scatter_dimension=0, tiled=True),
        lax.psum_scatter(totals[1], "dp", scatter_dimension=1, tiled=True),
        lax.psum_scatter(totals[2], "dp", scatter_dimension=0, tiled=True),
        lax.psum_scatter(totals[3], "dp", scatter_dimension=1, tiled=True),
    )
    gain_one_sum, gain_two_sum, scale_sum = lax.psum(small_totals, ("tensor", "dp"))
    grad_scale = scale_sum * multiplier * jax.nn.sigmoid(dim_scale[0])
    first_grads = jnp.stack([grad_list[micro - j] for j in range(micro)])
    second_grads = jnp.stack([grad_list[micro - 1 - j] for j in range(micro)])
    input_grads = jnp.where(first_section, first_grads, second_grads)
    grad_w_in, gradient_output_weight, grad_w_u, grad_w_d = shares
    grad_query = grad_w_in[:, :local]
    grad_key = grad_w_in[:, local : 2 * local]
    grad_value = grad_w_in[:, 2 * local :]
    return (
        layer_out[None],
        input_grads[None],
        gain_one_sum[None],
        grad_query[None],
        grad_key[None],
        grad_value[None],
        gradient_output_weight[None],
        grad_scale[None],
        gain_two_sum[None],
        grad_w_u[None],
        grad_w_d[None],
    )


def solution(mesh):
    in_specs = (
        P("dp", "tensor", None),
        P("dp", "tensor", None),
        P("section", None),
        P("section", None, "tensor"),
        P("section", None, "tensor"),
        P("section", None, "tensor"),
        P("section", "tensor", None),
        P("section", None),
        P("section", None),
        P("section", None, "tensor"),
        P("section", "tensor", None),
    )
    out_specs = (
        P("section", "dp", "tensor", None),
        P("section", "dp", "tensor", None),
        P("section", None),
        P("section", "dp", "tensor"),
        P("section", "dp", "tensor"),
        P("section", "dp", "tensor"),
        P("section", "tensor", "dp"),
        P("section", None),
        P("section", None),
        P("section", "dp", "tensor"),
        P("section", "tensor", "dp"),
    )
    return jax.shard_map(body, mesh=mesh, in_specs=in_specs, out_specs=out_specs, check_vma=False)
```

profile of v0, /device:TPU:0, one launch (start us, length us, event | category | flops | bytes accessed | tf_op | source)
XLA Modules:
  0.0 1664.4 jit_solution(8571743370235503399)
XLA Ops:
  11.9 28.2 %all-gather.13.cloned.1.call-done = bf16[1024,1280]{1,0:T(8,128)(2,1)} async-done(((bf16[256,1280]{1,0:T(8,128)(2,1)}), bf16[1024,1280]{1,0:T(8,128)(2,1)}) %all-gather.13.cloned.1.call-update) | async-done | bytes 2621456 | tf_op jit(solution)/shard_map/all_gather | solution.py:115
  74.9 50.9 %reduce-scatter.21.cloned.1.call-done = f32[256,1280]{1,0:T(8,128)} async-done(((f32[1024,1280]{1,0:T(8,128)}), f32[256,1280]{1,0:T(8,128)}) %reduce-scatter.21.cloned.1.call-update) | async-done | bytes 1310736 | tf_op jit(solution)/shard_map/reduce_scatter | solution.py:133
  128.7 25.5 %all-gather.15.cloned.1.call-done = bf16[1024,1280]{1,0:T(8,128)(2,1)} async-done(((bf16[256,1280]{1,0:T(8,128)(2,1)}), bf16[1024,1280]{1,0:T(8,128)(2,1)}) %all-gather.15.cloned.1.call-update) | async-done | bytes 2621456 | tf_op jit(solution)/shard_map/all_gather | solution.py:140
  162.2 51.5 %reduce-scatter.23.cloned.1.call-done = f32[256,1280]{1,0:T(8,128)} async-done(((f32[1024,1280]{1,0:T(8,128)}), f32[256,1280]{1,0:T(8,128)}) %reduce-scatter.23.cloned.1.call-update) | async-done | bytes 1310736 | tf_op jit(solution)/shard_map/reduce_scatter | solution.py:145
  235.2 26.7 %all-gather.17.cloned.1.call-done = bf16[1024,1280]{1,0:T(8,128)(2,1)} async-done(((bf16[256,1280]{1,0:T(8,128)(2,1)}), bf16[1024,1280]{1,0:T(8,128)(2,1)}) %all-gather.17.cloned.1.call-update) | async-done | bytes 2621456 | tf_op jit(solution)/shard_map/all_gather | solution.py:115
  296.5 51.5 %reduce-scatter.25.cloned.1.call-done = f32[256,1280]{1,0:T(8,128)} async-done(((f32[1024,1280]{1,0:T(8,128)}), f32[256,1280]{1,0:T(8,128)}) %reduce-scatter.25.cloned.1.call-update) | async-done | bytes 1310736 | tf_op jit(solution)/shard_map/reduce_scatter | solution.py:133
  351.1 25.3 %all-gather.19.cloned.1.call-done = bf16[1024,1280]{1,0:T(8,128)(2,1)} async-done(((bf16[256,1280]{1,0:T(8,128)(2,1)}), bf16[1024,1280]{1,0:T(8,128)(2,1)}) %all-gather.19.cloned.1.call-update) | async-done | bytes 2621456 | tf_op jit(solution)/shard_map/all_gather | solution.py:140
  384.3 51.5 %reduce-scatter.27.cloned.1.call-done = f32[256,1280]{1,0:T(8,128)} async-done(((f32[1024,1280]{1,0:T(8,128)}), f32[256,1280]{1,0:T(8,128)}) %reduce-scatter.27.cloned.1.call-update) | async-done | bytes 1310736 | tf_op jit(solution)/shard_map/reduce_scatter | solution.py:145
  457.3 26.7 %all-gather.21.cloned.1.call-done = bf16[1024,1280]{1,0:T(8,128)(2,1)} async-done(((bf16[256,1280]{1,0:T(8,128)(2,1)}), bf16[1024,1280]{1,0:T(8,128)(2,1)}) %all-gather.21.cloned.1.call-update) | async-done | bytes 2621456 | tf_op jit(solution)/shard_map/all_gather | solution.py:115
  518.1 51.5 %reduce-scatter.29.cloned.1.call-done = f32[256,1280]{1,0:T(8,128)} async-done(((f32[1024,1280]{1,0:T(8,128)}), f32[256,1280]{1,0:T(8,128)}) %reduce-scatter.29.cloned.1.call-update) | async-done | bytes 1310736 | tf_op jit(solution)/shard_map/reduce_scatter | solution.py:133
  634.1 51.5 %reduce-scatter.33.cloned.1.call-done = f32[256,1280]{1,0:T(8,128)} async-done(((f32[1024,1280]{1,0:T(8,128)}), f32[256,1280]{1,0:T(8,128)}) %reduce-scatter.33.cloned.1.call-update) | async-done | bytes 1310736 | tf_op jit(solution)/shard_map/reduce_scatter | solution.py:212
  689.4 25.6 %all-gather.27.cloned.1.call-done = bf16[1024,1280]{1,0:T(8,128)(2,1)} async-done(((bf16[256,1280]{1,0:T(8,128)(2,1)}), bf16[1024,1280]{1,0:T(8,128)(2,1)}) %all-gather.27.cloned.1.call-update) | async-done | bytes 2621456 | tf_op jit(solution)/shard_map/all_gather | solution.py:220
  720.3 75.3 %while.84 = (s32[]{:T(128)}, f32[1024,4,80]{0,2,1:T(8,128)S(1)}, f32[1024,4,80]{0,2,1:T(8,128)}, f32[2,512,4,80]{1,0,3,2:T(2,128)}, s32[2]{0:T(128)S(1)}, /*inde...) while((s32[]{:T(128)}, f32[1024,4,80]{0,2,1:T(8,128)S(1)}, ...), condition=%wide.region_28.29_spmd.clone, body=%wide.region_26.28_spmd.clone.sunk | while | flops 1711012352 | bytes 168620400 | solution.py:85
  813.0 46.2 %reduce-scatter.35.cloned.1.call-done = f32[256,1280]{1,0:T(8,128)} async-done(((f32[1024,1280]{1,0:T(8,128)}), f32[256,1280]{1,0:T(8,128)}) %reduce-scatter.35.cloned.1.call-update) | async-done | bytes 1310736 | tf_op jit(solution)/shard_map/reduce_scatter | solution.py:248
  861.5 51.6 %reduce-scatter.31.cloned.1.call-done = f32[256,1280]{1,0:T(8,128)} async-done(((f32[1024,1280]{1,0:T(8,128)}), f32[256,1280]{1,0:T(8,128)}) %reduce-scatter.31.cloned.1.call-update) | async-done | bytes 1310736 | tf_op jit(solution)/shard_map/reduce_scatter | solution.py:145
  970.7 51.5 %reduce-scatter.37.cloned.1.call-done = f32[256,1280]{1,0:T(8,128)} async-done(((f32[1024,1280]{1,0:T(8,128)}), f32[256,1280]{1,0:T(8,128)}) %reduce-scatter.37.cloned.1.call-update) | async-done | bytes 1310736 | tf_op jit(solution)/shard_map/reduce_scatter | solution.py:212
  1027.6 25.6 %all-gather.31.cloned.1.call-done = bf16[1024,1280]{1,0:T(8,128)(2,1)} async-done(((bf16[256,1280]{1,0:T(8,128)(2,1)}), bf16[1024,1280]{1,0:T(8,128)(2,1)}) %all-gather.31.cloned.1.call-update) | async-done | bytes 2621456 | tf_op jit(solution)/shard_map/all_gather | solution.py:220
  1058.5 75.2 %while.85 = (s32[]{:T(128)}, f32[1024,4,80]{0,2,1:T(8,128)S(1)}, f32[1024,4,80]{0,2,1:T(8,128)}, f32[2,512,4,80]{1,0,3,2:T(2,128)}, s32[2]{0:T(128)S(1)}, /*inde...) while((s32[]{:T(128)}, f32[1024,4,80]{0,2,1:T(8,128)S(1)}, ...), condition=%wide.region_35.36_spmd.clone, body=%wide.region_33.35_spmd.clone.sunk | while | flops 1711012352 | bytes 168620400 | solution.py:85
  1145.6 51.5 %reduce-scatter.39.cloned.1.call-done = f32[256,1280]{1,0:T(8,128)} async-done(((f32[1024,1280]{1,0:T(8,128)}), f32[256,1280]{1,0:T(8,128)}) %reduce-scatter.39.cloned.1.call-update) | async-done | bytes 1310736 | tf_op jit(solution)/shard_map/reduce_scatter | solution.py:248
  1252.4 51.5 %reduce-scatter.41.cloned.1.call-done = f32[256,1280]{1,0:T(8,128)} async-done(((f32[1024,1280]{1,0:T(8,128)}), f32[256,1280]{1,0:T(8,128)}) %reduce-scatter.41.cloned.1.call-update) | async-done | bytes 1310736 | tf_op jit(solution)/shard_map/reduce_scatter | solution.py:212
  1350.3 74.8 %while.86 = (s32[]{:T(128)}, f32[1024,4,80]{0,2,1:T(8,128)S(1)}, f32[1024,4,80]{0,2,1:T(8,128)}, f32[2,512,4,80]{1,0,3,2:T(2,128)}, s32[2]{0:T(128)S(1)}, /*inde...) while((s32[]{:T(128)}, f32[1024,4,80]{0,2,1:T(8,128)S(1)}, ...), condition=%wide.region_42.43_spmd.clone, body=%wide.region_40.42_spmd.clone.sunk | while | flops 1711012352 | bytes 168620400 | solution.py:85
  1463.5 70.0 %reduce-scatter.45.cloned.1.call-done = f32[320,960]{1,0:T(8,128)} async-done(((f32[1280,960]{1,0:T(8,128)}), f32[320,960]{1,0:T(8,128)}) %reduce-scatter.45.cloned.1.call-update) | async-done | bytes 1228816 | tf_op jit(solution)/shard_map/reduce_scatter | solution.py:277
  1536.2 51.8 %reduce-scatter.43.cloned.1.call-done = f32[256,1280]{1,0:T(8,128)} async-done(((f32[1024,1280]{1,0:T(8,128)}), f32[256,1280]{1,0:T(8,128)}) %reduce-scatter.43.cloned.1.call-update) | async-done | bytes 1310736 | tf_op jit(solution)/shard_map/reduce_scatter | solution.py:248
  1589.9 62.9 %all-reduce = (f32[1,1280]{1,0:T(1,128)}, f32[80]{0:T(128)S(1)}, f32[1,1280]{1,0:T(1,128)}) all-reduce(f32[1,1280]{1,0:T(1,128)S(1)} %broadcast_in_dim.168, f32[80]{0:T(128)S(1)} %add_add_fusion.3, f32[1,1280]{1,0:T(1,128)S(1)} %broadcast_in_dim.174), channel_id=1, replica_groups=mesh['section'=2,'tensor'=4,'dp'=4] {'tensor','dp'}, use_global_device_ids=true, to_apply=%region_48.49 | all-reduce | flops 2640 | bytes 21120 | tf_op jit(solution)/shard_map/psum | solution.py:282
  (670 shorter events, 759.5 us)
Async XLA Ops:
  11.7 114.1 %reduce-scatter.21.cloned.1.call-start = ((), (), s32[]{:S(2)}) async-start(), calls=%async_computation.17 | async-start | bytes 6553600 | tf_op jit(solution)/shard_map/reduce_scatter | solution.py:133
  128.5 85.2 %reduce-scatter.23.cloned.1.call-start = ((), (), s32[]{:S(2)}) async-start(), calls=%async_computation.19 | async-start | bytes 6553600 | tf_op jit(solution)/shard_map/reduce_scatter | solution.py:145
  162.1 99.8 %all-gather.17.cloned.1.call-start = ((), (), s32[]{:S(2)}) async-start(), calls=%async_computation.20 | async-start | bytes 3276800 | tf_op jit(solution)/shard_map/all_gather | solution.py:115
  235.2 112.8 %reduce-scatter.25.cloned.1.call-start = ((), (), s32[]{:S(2)}) async-start(), calls=%async_computation.21 | async-start | bytes 6553600 | tf_op jit(solution)/shard_map/reduce_scatter | solution.py:133
  350.6 85.1 %reduce-scatter.27.cloned.1.call-start = ((), (), s32[]{:S(2)}) async-start(), calls=%async_computation.23 | async-start | bytes 6553600 | tf_op jit(solution)/shard_map/reduce_scatter | solution.py:145
  384.2 99.8 %all-gather.21.cloned.1.call-start = ((), (), s32[]{:S(2)}) async-start(), calls=%async_computation.24 | async-start | bytes 3276800 | tf_op jit(solution)/shard_map/all_gather | solution.py:115
  457.3 112.4 %reduce-scatter.29.cloned.1.call-start = ((), (), s32[]{:S(2)}) async-start(), calls=%async_computation.25 | async-start | bytes 6553600 | tf_op jit(solution)/shard_map/reduce_scatter | solution.py:133
  518.0 80.1 %all-gather.23.cloned.1.call-start = ((), (), s32[]{:S(2)}) async-start(), calls=%async_computation.26 | async-start | bytes 3276800 | tf_op jit(solution)/shard_map/all_gather | solution.py:140
  574.7 110.8 %reduce-scatter.33.cloned.1.call-start = ((), (), s32[]{:S(2)}) async-start(), calls=%async_computation.29 | async-start | bytes 6553600 | tf_op jit(solution)/shard_map/reduce_scatter | solution.py:212
  634.0 81.0 %all-gather.27.cloned.1.call-start = ((), (), s32[]{:S(2)}) async-start(), calls=%async_computation.30 | async-start | bytes 3276800 | tf_op jit(solution)/shard_map/all_gather | solution.py:220
  689.3 169.8 %reduce-scatter.35.cloned.1.call-start = ((), (), s32[]{:S(2)}) async-start(), calls=%async_computation.31 | async-start | bytes 6553600 | tf_op jit(solution)/shard_map/reduce_scatter | solution.py:248
  807.6 105.5 %reduce-scatter.31.cloned.1.call-start = ((), (), s32[]{:S(2)}) async-start(), calls=%async_computation.27 | async-start | bytes 6553600 | tf_op jit(solution)/shard_map/reduce_scatter | solution.py:145
  812.9 150.0 %all-gather.29.cloned.1.call-start = ((), (), s32[]{:S(2)}) async-start(), calls=%async_computation.32 | async-start | bytes 3276800 | tf_op jit(solution)/shard_map/all_gather | solution.py:200
  938.1 84.1 %reduce-scatter.37.cloned.1.call-start = ((), (), s32[]{:S(2)}) async-start(), calls=%async_computation.33 | async-start | bytes 6553600 | tf_op jit(solution)/shard_map/reduce_scatter | solution.py:212
  970.6 82.6 %all-gather.31.cloned.1.call-start = ((), (), s32[]{:S(2)}) async-start(), calls=%async_computation.34 | async-start | bytes 3276800 | tf_op jit(solution)/shard_map/all_gather | solution.py:220
  1027.5 169.6 %reduce-scatter.39.cloned.1.call-start = ((), (), s32[]{:S(2)}) async-start(), calls=%async_computation.35 | async-start | bytes 6553600 | tf_op jit(solution)/shard_map/reduce_scatter | solution.py:248
  1145.5 98.8 %all-gather.33.cloned.1.call-start = ((), (), s32[]{:S(2)}) async-start(), calls=%async_computation.36 | async-start | bytes 3276800 | tf_op jit(solution)/shard_map/all_gather | solution.py:200
  1219.5 84.5 %reduce-scatter.41.cloned.1.call-start = ((), (), s32[]{:S(2)}) async-start(), calls=%async_computation.37 | async-start | bytes 6553600 | tf_op jit(solution)/shard_map/reduce_scatter | solution.py:212
  1252.4 85.2 %all-gather.35.cloned.1.call-start = ((), (), s32[]{:S(2)}) async-start(), calls=%async_computation.38 | async-start | bytes 3276800 | tf_op jit(solution)/shard_map/all_gather | solution.py:220
  1308.3 150.9 %reduce-scatter.51.cloned.1.call-start = ((), (), s32[]{:S(2)}) async-start(), calls=%async_computation.43 | async-start | bytes 2457600
  1319.3 142.1 %reduce-scatter.49.cloned.1.call-start = ((), (), s32[]{:S(2)}) async-start(), calls=%async_computation.42 | async-start | bytes 2457600
  1344.9 188.7 %reduce-scatter.45.cloned.1.call-start = ((), (), s32[]{:S(2)}) async-start(), calls=%async_computation.40 | async-start | bytes 6553600 | tf_op jit(solution)/shard_map/reduce_scatter | solution.py:277
  1439.3 148.7 %reduce-scatter.43.cloned.1.call-start = ((), (), s32[]{:S(2)}) async-start(), calls=%async_computation.39 | async-start | bytes 6553600 | tf_op jit(solution)/shard_map/reduce_scatter | solution.py:248
  1446.7 210.7 %reduce-scatter.47.cloned.1.call-start = ((), (), s32[]{:S(2)}) async-start(), calls=%async_computation.41 | async-start | bytes 2457600 | tf_op jit(solution)/shard_map/reduce_scatter | solution.py:279
  (178 other events, 6547.1 us)
Sparse Core Ops, SparseCore 0:
  11.8 28.2 all-gather.12
  74.4 51.3 reduce-scatter.20
  128.6 25.5 all-gather.14
  162.3 51.3 reduce-scatter.22
  235.3 26.5 all-gather.16
  296.5 51.3 reduce-scatter.24
  350.7 25.5 all-gather.18
  384.3 51.3 reduce-scatter.26
  457.4 26.5 all-gather.20
  518.2 51.3 reduce-scatter.28
  572.6 25.5 all-gather.22
  600.2 25.5 all-gather.24
  634.1 51.3 reduce-scatter.32
  807.7 51.3 reduce-scatter.34
  861.7 51.3 reduce-scatter.30
  970.8 51.3 reduce-scatter.36
  1145.6 51.3 reduce-scatter.38
  1252.5 51.3 reduce-scatter.40
  1308.4 25.5 all-gather.34
  1336.3 41.4 reduce-scatter.50
  1380.2 40.6 reduce-scatter.48
  1439.5 94.0 reduce-scatter.44
  1536.1 51.8 reduce-scatter.42
  1590.9 43.0 reduce-scatter.46
  (4 shorter events, 100.2 us)
where the time goes:
time: 1680 us; the launch traced here: 1660 us
  waiting for transfers between devices  1030 us (61%)
  matrix products  265 us (16%)
  local copies, waits for them, and re-layouts  149 us (9%)
  other arithmetic  109 us (6%)
  blocking collectives  62.9 us (4%)
  loops' own time  24.9 us (1%)
    reduce_scatter x3, waiting for transfers between devices, body(): lax.psum_scatter(jnp.dot(forward_activated, w_d, preferred_element_type=j...  155 us
    reduce_scatter x3, waiting for transfers between devices, body(): lax.psum_scatter(lax.dot_general(grad_upward, w_u, CONTRACT_LAST, preferr...  155 us
    reduce_scatter x3, waiting for transfers between devices, body(): lax.psum_scatter(jnp.dot(forward_mixed, w_o, preferred_element_type=jnp.f...  154 us
    reduce_scatter x3, waiting for transfers between devices, body(): lax.psum_scatter(lax.dot_general(grad_proj, w_in, CONTRACT_LAST, preferre...  150 us
    dynamic_update_slice x12, local copies, waits for them, and re-layouts, attend(): mixed, logsum = lax.map(one_block, starts)  85.4 us
    all_gather x3, waiting for transfers between devices, body(): lax.all_gather(normed.astype(jnp.bfloat16), 'tensor', axis=0, tiled=True)  81.6 us
    all_gather x3, waiting for transfers between devices, body(): lax.all_gather(normed_two.astype(jnp.bfloat16), 'tensor', axis=0, tiled=T...  74.1 us
    all_gather x3, waiting for transfers between devices, body(): lax.all_gather(upper.astype(jnp.bfloat16), 'tensor', axis=0, tiled=True)  73.1 us
  transfers between devices with their start and end apart: 32, of which 28 were waited for; matrix products, arithmetic and copies ran while one was open for 10% of the time, Pallas kernels for 0%

commit v1 on v0

v1 whole, which is shorter than its diff:
```python
import functools
import math

import jax
import jax.numpy as jnp
from jax import lax
from jax.experimental import pallas as pl
from jax.experimental.pallas import tpu as pltpu
from jax.sharding import PartitionSpec as P

EPS = 1e-06
LOG2E = 1.442695041
NEGATIVE = -1e30
BF16 = jnp.bfloat16
F32 = jnp.float32
MESH = pl.DeviceIdType.MESH
ANY = pl.BlockSpec(memory_space=pl.ANY)
VMEM = pl.BlockSpec(memory_space=pltpu.VMEM)
DMA = pltpu.SemaphoreType.DMA
MIB = 1 << 20
PIECES = 4


def plain(a, b):
    return jnp.dot(a, b, preferred_element_type=F32)


def by_last(a, b):
    return lax.dot_general(a, b, (((1,), (1,)), ((), ())), preferred_element_type=F32)


def by_first(a, b):
    return lax.dot_general(a, b, (((0,), (0,)), ((), ())), preferred_element_type=F32)


def other(index):
    return index + 1 - 2 * lax.rem(index, 2)


def remote(src, dst, send, receive, device):
    return pltpu.make_async_remote_copy(
        src_ref=src,
        dst_ref=dst,
        send_sem=send,
        recv_sem=receive,
        device_id=device,
        device_id_type=MESH,
    )


def greet(devices):
    barrier = pltpu.get_barrier_semaphore()
    for device in devices:
        pl.semaphore_signal(barrier, inc=1, device_id=device, device_id_type=MESH)
    pl.semaphore_wait(barrier, len(devices))


def inverse_rms(rows):
    return lax.rsqrt(jnp.mean(rows * rows, axis=1, keepdims=True) + EPS)


def forward_kernel(
    inputs, cotangent, w_in, w_o, w_u, w_d, gain_one, gain_two, scale,
    out_rows, h_out, n1_out, q_out, k_out, v_out, o_out, lse_out, m_out, n2_out, u_out, a_out,
    g_out, win_out, wo_out, wu_out, wd_out,
    land, win, wo, wu, wd, n1, q, k, v, o_heads, o, lse_cols, lse, ysend, yrecv, m, n2, u, a,
    zpart, zrecv, xout,
    own_sem, xs_sem, xr_sem, xfs_sem, xfr_sem, wys_sem, wyr_sem, wzs_sem, wzr_sem,
    ns_sem, nr_sem, nfs_sem, nfr_sem, ys_sem, yr_sem, zs_sem, zr_sem, os_sem, or_sem, save_sem,
):
    s, t, d = lax.axis_index("section"), lax.axis_index("tensor"), lax.axis_index("dp")
    blocks, rows, width = land.shape[1:]
    half = rows // 2
    local = w_o.shape[0]
    heads, _, head = q.shape
    per = heads // 2
    c, y = lax.rem(t, 2), t // 2
    core = (s, other(t), d)
    across = (s, lax.rem(t + 2, 4), d)
    diagonal = (s, other(lax.rem(t + 2, 4)), d)
    beside = (s, t, other(d))
    section = (1 - s, t, d)
    greet([core, across, diagonal, beside, section])

    mine = pl.ds(pl.multiple_of(c * half, half), half)
    theirs = pl.ds(pl.multiple_of((1 - c) * half, half), half)

    own = [
        pltpu.make_async_copy(w_in, win.at[0], own_sem.at[0]),
        pltpu.make_async_copy(w_o, wo.at[pl.ds(0, local)], own_sem.at[1]),
        pltpu.make_async_copy(w_u, wu.at[0], own_sem.at[2]),
        pltpu.make_async_copy(w_d, wd.at[pl.ds(0, local)], own_sem.at[3]),
    ]
    for copy in own:
        copy.start()

    def spread(source):
        for sequence in range(2):
            for part in range(2):
                target = 2 * sequence + part
                piece = pl.ds(part * half, half)
                src = source.at[sequence, piece]
                dst = land.at[0, t, piece]

                @pl.when(target == t)
                def _():
                    pltpu.make_async_copy(src, dst, xr_sem.at[t]).start()

                @pl.when(target != t)
                def _():
                    remote(src, dst, xs_sem.at[target], xr_sem.at[t], (s, target, d)).start()

    def gather_rows():
        for b in range(blocks):
            piece = land.at[0, b, mine]
            remote(piece, piece, xs_sem.at[b], xr_sem.at[b], core).wait_recv()
            remote(piece, piece, xfs_sem.at[b], xfr_sem.at[b], core).start()
        for b in range(blocks):
            piece = land.at[0, b, theirs]
            remote(piece, piece, xfs_sem.at[b], xfr_sem.at[b], core).wait_recv()

    parity = lax.rem(d, 2)
    step = width // 2 // PIECES
    in_pieces = [
        [pl.ds(pl.multiple_of(which * (width // 2) + i * step, step), step) for i in range(PIECES)]
        for which in (parity, 1 - parity)
    ]
    wide = [pl.ds(pl.multiple_of(w * (width // 2), width // 2), width // 2) for w in (parity, 1 - parity)]
    short = local // 2
    tall = [pl.ds(pl.multiple_of(w * short, short), short) for w in (parity, 1 - parity)]
    low = [pl.ds(pl.multiple_of(local + w * short, short), short) for w in (parity, 1 - parity)]

    def pieces(which):
        found = [(w_in.at[p], win.at[1, p]) for p in in_pieces[which]]
        found.append((w_o.at[tall[which]], wo.at[low[which]]))
        found.append((w_u.at[wide[which]], wu.at[1, wide[which]]))
        found.append((w_d.at[tall[which]], wd.at[low[which]]))
        return found

    sent, relayed = pieces(0), pieces(1)

    @pl.when(s == 0)
    def _():
        spread(inputs)

    for i, (src, dst) in enumerate(sent):
        remote(src, dst, wys_sem.at[i], wyr_sem.at[i], across).start()

    @pl.when(s == 1)
    def _():
        spread(cotangent)

    def relay(i):
        dst = sent[i][1]
        remote(dst, dst, wys_sem.at[i], wyr_sem.at[i], across).wait_recv()
        remote(dst, dst, wzs_sem.at[i], wzr_sem.at[i], beside).start()

    def arrived(i):
        dst = relayed[i][1]
        remote(dst, dst, wzs_sem.at[i], wzr_sem.at[i], beside).wait_recv()

    @pl.when(s == 0)
    def _():
        gather_rows()

    for i in range(PIECES):
        relay(i)
    own[0].wait()
    for i in range(PIECES):
        arrived(i)

    def save(kind, b, src, dst):
        pltpu.make_async_copy(src, dst, save_sem.at[kind, b]).start()

    causal = lax.broadcasted_iota(jnp.int32, (rows, rows), 0) >= lax.broadcasted_iota(
        jnp.int32, (rows, rows), 1
    )
    lane = lax.broadcasted_iota(jnp.int32, (rows, 128), 1)

    def attention(b, _):
        at = pl.ds(pl.multiple_of(b * rows, rows), rows)

        @pl.when(s == 1)
        def _():
            piece = land.at[1, b, mine]
            remote(piece, piece, ns_sem.at[b], nr_sem.at[b], core).wait_recv()
            remote(piece, piece, nfs_sem.at[b], nfr_sem.at[b], core).start()
            rest = land.at[1, b, theirs]
            remote(rest, rest, nfs_sem.at[b], nfr_sem.at[b], core).wait_recv()

        hidden = land[s, b].astype(F32)
        normed = (hidden * inverse_rms(hidden) * gain_one[...]).astype(BF16)
        n1[at] = normed
        for j in range(2):
            projected = plain(normed, win[j])
            for i in range(per):
                cut = slice(i * head, (i + 1) * head)
                q[j * per + i, at] = (projected[:, cut] * scale[...]).astype(BF16)
                k[j * per + i, at] = projected[:, local + i * head : local + (i + 1) * head].astype(
                    BF16
                )
                v[j * per + i, at] = projected[
                    :, 2 * local + i * head : 2 * local + (i + 1) * head
                ].astype(BF16)
        lse_cols[...] = jnp.zeros_like(lse_cols)
        for bb in range(blocks):

            @pl.when(b == bb)
            def _():
                def one(i, _):
                    qh = q[i, bb * rows : (bb + 1) * rows]
                    near = by_last(qh, k[i, bb * rows : (bb + 1) * rows])
                    near = jnp.where(causal, near, NEGATIVE)
                    top = jnp.max(near, axis=1, keepdims=True)
                    if bb:
                        far = by_last(qh, k[i, : bb * rows])
                        top = jnp.maximum(top, jnp.max(far, axis=1, keepdims=True))
                    near = jnp.exp(near - top)
                    total = jnp.sum(near, axis=1, keepdims=True)
                    mixed = plain(near.astype(BF16), v[i, bb * rows : (bb + 1) * rows])
                    if bb:
                        far = jnp.exp(far - top)
                        total = total + jnp.sum(far, axis=1, keepdims=True)
                        mixed = mixed + plain(far.astype(BF16), v[i, : bb * rows])
                    o_heads[i] = (mixed / total).astype(BF16)
                    lse_cols[...] = jnp.where(lane == i, top + jnp.log(total), lse_cols[...])
                    return 0

                lax.fori_loop(0, heads, one, 0, unroll=2)

        o[at] = jnp.concatenate([o_heads[i] for i in range(heads)], axis=1)
        lse[b] = jnp.transpose(lse_cols[...])[:heads]

        save(0, b, land.at[s, b], h_out.at[b])
        save(1, b, n1.at[at], n1_out.at[at])
        save(2, b, q.at[:, at], q_out.at[:, at])
        save(3, b, k.at[:, at], k_out.at[:, at])
        save(4, b, v.at[:, at], v_out.at[:, at])
        save(5, b, o.at[at], o_out.at[at])
        save(6, b, lse.at[b], lse_out.at[b])
        for i in range(3):

            @pl.when(b == blocks - 3 + i)
            def _():
                relay(PIECES + i)

        return 0

    lax.fori_loop(0, blocks, attention, 0)

    own[1].wait()
    arrived(PIECES)

    def project(b, _):
        at = pl.ds(pl.multiple_of(b * rows, rows), rows)
        ysend[b] = plain(o[at], wo[...]).astype(BF16)
        remote(ysend.at[b], yrecv.at[b], ys_sem.at[b], yr_sem.at[b], core).start()
        return 0

    lax.fori_loop(0, blocks, project, 0)

    own[2].wait()
    arrived(PIECES + 1)
    own[3].wait()
    arrived(PIECES + 2)
    weights = [(win, win_out), (wo, wo_out), (wu, wu_out), (wd, wd_out)]
    for i, (src, dst) in enumerate(weights):
        save(11, i, src, dst)

    def feed(b, _):
        at = pl.ds(pl.multiple_of(b * rows, rows), rows)
        remote(ysend.at[b], yrecv.at[b], ys_sem.at[b], yr_sem.at[b], core).wait_recv()
        middle = land[s, b].astype(F32) + (ysend[b].astype(F32) + yrecv[b].astype(F32))
        m[b] = middle
        normed = (middle * inverse_rms(middle) * gain_two[...]).astype(BF16)
        n2[at] = normed
        up = jnp.concatenate([plain(normed, wu[0]), plain(normed, wu[1])], axis=1)
        u[b] = up
        active = (up / (1.0 + jnp.exp(-up))).astype(BF16)
        a[at] = active
        zpart[b] = plain(active, wd[...])
        copy = remote(zpart.at[b, theirs], zrecv.at[b], zs_sem.at[b], zr_sem.at[b], core)
        copy.start()
        save(7, b, m.at[b], m_out.at[b])
        save(8, b, n2.at[at], n2_out.at[at])
        save(9, b, u.at[b], u_out.at[b])
        save(10, b, a.at[at], a_out.at[at])
        copy.wait_recv()
        xout[b] = (m[b, mine] + (zpart[b, mine] + zrecv[b])).astype(BF16)

        @pl.when(s == 0)
        def _():
            remote(xout.at[b], land.at[1, b, mine], ns_sem.at[b], nr_sem.at[b], section).start()

        place = out_rows.at[y, mine]

        @pl.when(b == t)
        def _():
            pltpu.make_async_copy(xout.at[b], place, or_sem.at[t]).start()

        @pl.when(b != t)
        def _():
            remote(xout.at[b], place, os_sem.at[b], or_sem.at[t], (s, b, d)).start()

        return 0

    lax.fori_loop(0, blocks, feed, 0)

    @pl.when(s == 1)
    def _():
        gather_rows()

    for b in range(blocks):
        pltpu.make_async_copy(land.at[0, b], g_out.at[b], save_sem.at[12, b]).start()

    for b in range(blocks):
        piece = land.at[0, b, mine]
        remote(piece, piece, xfs_sem.at[b], xfr_sem.at[b], core).wait_send()
        remote(ysend.at[b], yrecv.at[b], ys_sem.at[b], yr_sem.at[b], core).wait_send()
        remote(zpart.at[b, theirs], zrecv.at[b], zs_sem.at[b], zr_sem.at[b], core).wait_send()
        here = out_rows.at[b // 2, pl.ds((b % 2) * half, half)]
        remote(here, here, os_sem.at[b], or_sem.at[b], core).wait_recv()

        @pl.when(b != t)
        def _():
            remote(xout.at[b], here, os_sem.at[b], or_sem.at[b], core).wait_send()
            remote(piece, piece, xs_sem.at[b], xr_sem.at[b], core).wait_send()

        @pl.when(s == 0)
        def _():
            remote(xout.at[b], piece, ns_sem.at[b], nr_sem.at[b], section).wait_send()

        @pl.when(s == 1)
        def _():
            remote(piece, piece, nfs_sem.at[b], nfr_sem.at[b], core).wait_send()

    for i, (src, dst) in enumerate(sent):
        remote(src, dst, wys_sem.at[i], wyr_sem.at[i], across).wait_send()
        remote(dst, dst, wzs_sem.at[i], wzr_sem.at[i], beside).wait_send()
    for i, (src, dst) in enumerate(weights):
        pltpu.make_async_copy(src, dst, save_sem.at[11, i]).wait()
    for b in range(blocks):
        at = pl.ds(b * rows, rows)
        saved = [
            (land.at[s, b], h_out.at[b]),
            (n1.at[at], n1_out.at[at]),
            (q.at[:, at], q_out.at[:, at]),
            (k.at[:, at], k_out.at[:, at]),
            (v.at[:, at], v_out.at[:, at]),
            (o.at[at], o_out.at[at]),
            (lse.at[b], lse_out.at[b]),
            (m.at[b], m_out.at[b]),
            (n2.at[at], n2_out.at[at]),
            (u.at[b], u_out.at[b]),
            (a.at[at], a_out.at[at]),
        ]
        for kind, (src, dst) in enumerate(saved):
            pltpu.make_async_copy(src, dst, save_sem.at[kind, b]).wait()
        pltpu.make_async_copy(land.at[0, b], g_out.at[b], save_sem.at[12, b]).wait()


def forward(inputs, cotangent, w_in, w_o, w_u, w_d, gain_one, gain_two, scale, head):
    _, rows, width = inputs.shape
    local = w_o.shape[0]
    heads = 2 * local // head
    blocks = lax.axis_size("tensor")
    length = blocks * rows
    half = rows // 2
    shape = jax.ShapeDtypeStruct
    outs = [
        shape(inputs.shape, BF16),
        shape((blocks, rows, width), BF16),
        shape((length, width), BF16),
        shape((heads, length, head), BF16),
        shape((heads, length, head), BF16),
        shape((heads, length, head), BF16),
        shape((length, 2 * local), BF16),
        shape((blocks, heads, rows), F32),
        shape((blocks, rows, width), F32),
        shape((length, width), BF16),
        shape((blocks, rows, 2 * local), F32),
        shape((length, 2 * local), BF16),
        shape((blocks, rows, width), BF16),
        shape((2, width, 3 * local), BF16),
        shape((2 * local, width), BF16),
        shape((2, width, local), BF16),
        shape((2 * local, width), BF16),
    ]
    scratch = [
        pltpu.VMEM((2, blocks, rows, width), BF16),
        pltpu.VMEM((2, width, 3 * local), BF16),
        pltpu.VMEM((2 * local, width), BF16),
        pltpu.VMEM((2, width, local), BF16),
        pltpu.VMEM((2 * local, width), BF16),
        pltpu.VMEM((length, width), BF16),
        pltpu.VMEM((heads, length, head), BF16),
        pltpu.VMEM((heads, length, head), BF16),
        pltpu.VMEM((heads, length, head), BF16),
        pltpu.VMEM((heads, rows, head), BF16),
        pltpu.VMEM((length, 2 * local), BF16),
        pltpu.VMEM((rows, 128), F32),
        pltpu.VMEM((blocks, heads, rows), F32),
        pltpu.VMEM((blocks, rows, width), BF16),
        pltpu.VMEM((blocks, rows, width), BF16),
        pltpu.VMEM((blocks, rows, width), F32),
        pltpu.VMEM((length, width), BF16),
        pltpu.VMEM((blocks, rows, 2 * local), F32),
        pltpu.VMEM((length, 2 * local), BF16),
        pltpu.VMEM((blocks, rows, width), F32),
        pltpu.VMEM((blocks, half, width), F32),
        pltpu.VMEM((blocks, half, width), BF16),
        DMA((4,)),
        DMA((blocks,)),
        DMA((blocks,)),
        DMA((blocks,)),
        DMA((blocks,)),
        DMA((PIECES + 3,)),
        DMA((PIECES + 3,)),
        DMA((PIECES + 3,)),
        DMA((PIECES + 3,)),
        DMA((blocks,)),
        DMA((blocks,)),
        DMA((blocks,)),
        DMA((blocks,)),
        DMA((blocks,)),
        DMA((blocks,)),
        DMA((blocks,)),
        DMA((blocks,)),
        DMA((blocks,)),
        DMA((blocks,)),
        DMA((13, blocks)),
    ]
    return pl.pallas_call(
        forward_kernel,
        out_shape=outs,
        in_specs=[ANY] * 6 + [VMEM] * 3,
        out_specs=[ANY] * len(outs),
        scratch_shapes=scratch,
        compiler_params=pltpu.CompilerParams(
            collective_id=1, has_side_effects=True, vmem_limit_bytes=60 * MIB
        ),
        name="forward",
    )(inputs, cotangent, w_in, w_o, w_u, w_d, gain_one, gain_two, scale)


def backward_kernel(
    g_in, h_in, q_in, k_in, v_in, o_in, lse_in, m_in, u_in, win_in, wo_in, wu_in, wd_in,
    gain_one, gain_two, scale,
    out_rows, g_out, gu_out, gy_out, gp_out, dg1, dg2, ds,
    g, win, wo, wu, wd, h, q, k, v, o, lse, m, u, gu, gy, gp, ysend, yrecv, gm, go_heads, gq_heads,
    cols, delta, dk, dv, n1part, n1recv, xout,
    load_sem, w_sem, ns_sem, nr_sem, nfs_sem, nfr_sem, ys_sem, yr_sem, zs_sem, zr_sem, os_sem, or_sem,
    save_sem,
):
    s, t, d = lax.axis_index("section"), lax.axis_index("tensor"), lax.axis_index("dp")
    blocks, rows, width = g.shape
    half = rows // 2
    local = wu.shape[2]
    heads, _, head = q.shape
    per = heads // 2
    c, y = lax.rem(t, 2), t // 2
    core = (s, other(t), d)
    across = (s, lax.rem(t + 2, 4), d)
    diagonal = (s, other(lax.rem(t + 2, 4)), d)
    section = (1 - s, t, d)
    mine = pl.ds(pl.multiple_of(c * half, half), half)
    theirs = pl.ds(pl.multiple_of((1 - c) * half, half), half)

    weights = [(wd_in, wd), (wu_in, wu), (wo_in, wo), (win_in, win)]

    def loads(b):
        at = pl.ds(b * rows, rows)
        return [
            (u_in.at[b], u.at[b]),
            (m_in.at[b], m.at[b]),
            (o_in.at[at], o.at[at]),
            (q_in.at[:, at], q.at[:, at]),
            (k_in.at[:, at], k.at[:, at]),
            (v_in.at[:, at], v.at[:, at]),
            (lse_in.at[b], lse.at[b]),
            (h_in.at[b, mine], h.at[b]),
        ]

    for i, (src, dst) in enumerate(weights[:2]):
        pltpu.make_async_copy(src, dst, w_sem.at[i]).start()
    for kind, (src, dst) in enumerate(loads(blocks - 1)[:2]):
        pltpu.make_async_copy(src, dst, load_sem.at[kind, blocks - 1]).start()

    @pl.when(s == 1)
    def _():
        for b in reversed(range(blocks)):
            pltpu.make_async_copy(g_in.at[b], g.at[b], nr_sem.at[b]).start()

    for i, (src, dst) in enumerate(weights[2:]):
        pltpu.make_async_copy(src, dst, w_sem.at[2 + i]).start()
    for b in reversed(range(blocks)):
        for kind, (src, dst) in enumerate(loads(b)):
            if kind >= 2 or b < blocks - 1:
                pltpu.make_async_copy(src, dst, load_sem.at[kind, b]).start()

    greet([core, across, diagonal, section])

    dk[...] = jnp.zeros_like(dk)
    dv[...] = jnp.zeros_like(dv)
    dg1[...] = jnp.zeros_like(dg1)
    dg2[...] = jnp.zeros_like(dg2)
    ds[...] = jnp.zeros_like(ds)
    for i, (src, dst) in enumerate(weights):
        pltpu.make_async_copy(src, dst, w_sem.at[i]).wait()
    for b in range(blocks):
        for kind, (src, dst) in enumerate(loads(b)):
            if b != blocks - 1 or kind < 2:
                pass
            pltpu.make_async_copy(src, dst, load_sem.at[kind, b]).wait()

    causal = lax.broadcasted_iota(jnp.int32, (rows, rows), 0) <= lax.broadcasted_iota(
        jnp.int32, (rows, rows), 1
    )

    def save(kind, b, src, dst):
        pltpu.make_async_copy(src, dst, save_sem.at[kind, b]).start()

    def one_block(turn, _):
        b = blocks - 1 - turn
        at = pl.ds(pl.multiple_of(b * rows, rows), rows)

        @pl.when(s == 1)
        def _():
            pltpu.make_async_copy(g_in.at[b], g.at[b], nr_sem.at[b]).wait()

        @pl.when(s == 0)
        def _():
            piece = g.at[b, mine]
            remote(piece, piece, ns_sem.at[b], nr_sem.at[b], core).wait_recv()
            remote(piece, piece, nfs_sem.at[b], nfr_sem.at[b], core).start()
            rest = g.at[b, theirs]
            remote(rest, rest, nfs_sem.at[b], nfr_sem.at[b], core).wait_recv()

        save(0, b, g.at[b], g_out.at[at])
        grad = g[b]
        grad_act = by_last(grad, wd[...])
        up = u[b]
        sigma = 1.0 / (1.0 + jnp.exp(-up))
        grad_up = (grad_act * sigma * (1.0 + up * (1.0 - sigma))).astype(BF16)
        gu[at] = grad_up
        save(1, b, gu.at[at], gu_out.at[at])
        ysend[b] = (by_last(grad_up[:, :local], wu[0]) + by_last(grad_up[:, local:], wu[1])).astype(
            BF16
        )
        copy = remote(ysend.at[b], yrecv.at[b], ys_sem.at[b], yr_sem.at[b], core)
        copy.start()
        copy.wait_recv()
        grad_normed = ysend[b].astype(F32) + yrecv[b].astype(F32)
        middle = m[b]
        inverse = inverse_rms(middle)
        unit = middle * inverse
        grad_unit = grad_normed * gain_two[...]
        dg2[...] += jnp.sum(grad_normed * unit, axis=0, keepdims=True)
        grad_middle = grad.astype(F32) + inverse * (
            grad_unit - unit * jnp.mean(grad_unit * unit, axis=1, keepdims=True)
        )
        gm[...] = grad_middle
        grad_mid = grad_middle.astype(BF16)
        gy[at] = grad_mid
        save(2, b, gy.at[at], gy_out.at[at])
        grad_mixed = by_last(grad_mid, wo[...]).astype(BF16)
        both = grad_mixed.astype(F32) * o[at].astype(F32)
        lane = lax.broadcasted_iota(jnp.int32, (rows, 128), 1)
        found = jnp.zeros((rows, 128), F32)
        for i in range(heads):
            cut = slice(i * head, (i + 1) * head)
            go_heads[i] = grad_mixed[:, cut]
            found = jnp.where(lane == i, jnp.sum(both[:, cut], axis=1, keepdims=True), found)
        delta[...] = jnp.transpose(found)[:heads]
        for bb in range(blocks):

            @pl.when(b == bb)
            def _():
                def one(i, _):
                    qh = q[i, bb * rows : (bb + 1) * rows]
                    gh = go_heads[i]
                    offset = lse[bb, pl.ds(i, 1)]
                    inner = delta[pl.ds(i, 1)]
                    total = jnp.zeros((head, rows), F32)
                    for j in range(bb + 1):
                        cut = slice(j * rows, (j + 1) * rows)
                        kj = k[i, cut]
                        weight = jnp.exp(by_last(kj, qh) - offset)
                        if j == bb:
                            weight = jnp.where(causal, weight, 0.0)
                        grad_score = weight * (by_last(v[i, cut], gh) - inner)
                        grad_score = grad_score.astype(BF16)
                        dv[i, cut] += plain(weight.astype(BF16), gh)
                        dk[i, cut] += plain(grad_score, qh)
                        total = total + by_first(kj, grad_score)
                    gq_heads[i] = jnp.transpose(total)
                    return 0

                lax.fori_loop(0, heads, one, 0)

        for j in range(2):
            mine_heads = range(j * per, (j + 1) * per)
            grad_scaled = jnp.concatenate([gq_heads[i] for i in mine_heads], axis=1)
            queries = jnp.concatenate([q[i, at] for i in mine_heads], axis=1).astype(F32)
            ds[pl.ds(j, 1)] += jnp.sum(grad_scaled * queries, axis=0, keepdims=True)
            grads = [
                (grad_scaled * scale[...]).astype(BF16),
                jnp.concatenate([dk[i, at] for i in mine_heads], axis=1).astype(BF16),
                jnp.concatenate([dv[i, at] for i in mine_heads], axis=1).astype(BF16),
            ]
            gp[j, at] = jnp.concatenate(grads, axis=1)
        save(3, b, gp.at[:, at], gp_out.at[:, at])
        n1part[...] = by_last(gp[0, at], win[0]) + by_last(gp[1, at], win[1])
        copy = remote(n1part.at[theirs], n1recv.at[b], zs_sem.at[b], zr_sem.at[b], core)
        copy.start()
        copy.wait_recv()
        grad_normed = n1part[mine] + n1recv[b]
        hidden = h[b].astype(F32)
        inverse = inverse_rms(hidden)
        unit = hidden * inverse
        grad_unit = grad_normed * gain_one[...]
        dg1[...] += jnp.sum(grad_normed * unit, axis=0, keepdims=True)
        xout[b] = (
            gm[mine]
            + inverse * (grad_unit - unit * jnp.mean(grad_unit * unit, axis=1, keepdims=True))
        ).astype(BF16)

        @pl.when(s == 1)
        def _():
            remote(xout.at[b], g.at[b, mine], ns_sem.at[b], nr_sem.at[b], section).start()

        place = out_rows.at[y, mine]

        @pl.when(b == t)
        def _():
            pltpu.make_async_copy(xout.at[b], place, or_sem.at[t]).start()

        @pl.when(b != t)
        def _():
            remote(xout.at[b], place, os_sem.at[b], or_sem.at[t], (s, b, d)).start()

        copy.wait_send()
        return 0

    lax.fori_loop(0, blocks, one_block, 0)

    for b in range(blocks):
        at = pl.ds(b * rows, rows)
        piece = g.at[b, mine]
        remote(ysend.at[b], yrecv.at[b], ys_sem.at[b], yr_sem.at[b], core).wait_send()
        here = out_rows.at[b // 2, pl.ds((b % 2) * half, half)]
        remote(here, here, os_sem.at[b], or_sem.at[b], core).wait_recv()

        @pl.when(b != t)
        def _():
            remote(xout.at[b], here, os_sem.at[b], or_sem.at[b], core).wait_send()

        @pl.when(s == 1)
        def _():
            remote(xout.at[b], piece, ns_sem.at[b], nr_sem.at[b], section).wait_send()

        @pl.when(s == 0)
        def _():
            remote(piece, piece, nfs_sem.at[b], nfr_sem.at[b], core).wait_send()

        saved = [
            (g.at[b], g_out.at[at]),
            (gu.at[at], gu_out.at[at]),
            (gy.at[at], gy_out.at[at]),
            (gp.at[:, at], gp_out.at[:, at]),
        ]
        for kind, (src, dst) in enumerate(saved):
            pltpu.make_async_copy(src, dst, save_sem.at[kind, b]).wait()


def backward(saved, gain_one, gain_two, scale):
    g_in, h_in, q_in = saved[:3]
    win_in, wo_in, wu_in, wd_in = saved[9:]
    blocks, rows, width = g_in.shape
    heads, length, head = q_in.shape
    local = wu_in.shape[2]
    half = rows // 2
    shape = jax.ShapeDtypeStruct
    outs = [
        shape((2, rows, width), BF16),
        shape((length, width), BF16),
        shape((length, 2 * local), BF16),
        shape((length, width), BF16),
        shape((2, length, 3 * local), BF16),
        shape((1, width), F32),
        shape((1, width), F32),
        shape((2, local), F32),
    ]
    scratch = [
        pltpu.VMEM((blocks, rows, width), BF16),
        pltpu.VMEM(win_in.shape, BF16),
        pltpu.VMEM(wo_in.shape, BF16),
        pltpu.VMEM(wu_in.shape, BF16),
        pltpu.VMEM(wd_in.shape, BF16),
        pltpu.VMEM((blocks, half, width), BF16),
        pltpu.VMEM((heads, length, head), BF16),
        pltpu.VMEM((heads, length, head), BF16),
        pltpu.VMEM((heads, length, head), BF16),
        pltpu.VMEM((length, 2 * local), BF16),
        pltpu.VMEM((blocks, heads, rows), F32),
        pltpu.VMEM((blocks, rows, width), F32),
        pltpu.VMEM((blocks, rows, 2 * local), F32),
        pltpu.VMEM((length, 2 * local), BF16),
        pltpu.VMEM((length, width), BF16),
        pltpu.VMEM((2, length, 3 * local), BF16),
        pltpu.VMEM((blocks, rows, width), BF16),
        pltpu.VMEM((blocks, rows, width), BF16),
        pltpu.VMEM((rows, width), F32),
        pltpu.VMEM((heads, rows, head), BF16),
        pltpu.VMEM((heads, rows, head), F32),
        pltpu.VMEM((8, 128), F32),
        pltpu.VMEM((heads, rows), F32),
        pltpu.VMEM((heads, length, head), F32),
        pltpu.VMEM((heads, length, head), F32),
        pltpu.VMEM((rows, width), F32),
        pltpu.VMEM((blocks, half, width), F32),
        pltpu.VMEM((blocks, half, width), BF16),
        DMA((8, blocks)),
        DMA((4,)),
        DMA((blocks,)),
        DMA((blocks,)),
        DMA((blocks,)),
        DMA((blocks,)),
        DMA((blocks,)),
        DMA((blocks,)),
        DMA((blocks,)),
        DMA((blocks,)),
        DMA((blocks,)),
        DMA((blocks,)),
        DMA((4, blocks)),
    ]
    return pl.pallas_call(
        backward_kernel,
        out_shape=outs,
        in_specs=[ANY] * 13 + [VMEM] * 3,
        out_specs=[ANY] * 5 + [VMEM] * 3,
        scratch_shapes=scratch,
        compiler_params=pltpu.CompilerParams(
            collective_id=2, has_side_effects=True, vmem_limit_bytes=62 * MIB
        ),
        name="backward",
    )(*saved, gain_one, gain_two, scale)


def reduce_kernel(
    keep_in, give_in, out, keep, yrecv, right, left, sbuf,
    k_sem, ys_sem, yr_sem, rs_sem, rr_sem, ls_sem, lr_sem,
):
    s, t, d = lax.axis_index("section"), lax.axis_index("tensor"), lax.axis_index("dp")
    n, chunk, width = keep.shape
    groups = ys_sem.shape[1]
    step = width // groups
    across = (s, lax.rem(t + 2, 4), d)
    up = (s, t, lax.rem(d + 1, n))
    down = (s, t, lax.rem(d + n - 1, n))
    greet([across, up, down])

    def cut(i):
        return pl.ds(i * step, step)

    order = []
    for i in range((n + 1) // 2):
        order += [n - 1 - i, i] if n - 1 - i != i else [i]
    for e in order:
        pltpu.make_async_copy(keep_in.at[e], keep.at[e], k_sem.at[e]).start()
        for i in range(groups):
            remote(
                give_in.at[e, :, cut(i)],
                yrecv.at[e, :, cut(i)],
                ys_sem.at[e, i],
                yr_sem.at[e, i],
                across,
            ).start()

    def exchange(e, i):
        piece = yrecv.at[e, :, cut(i)]
        return remote(piece, piece, ys_sem.at[e, i], yr_sem.at[e, i], across)

    def to_right(e, i):
        return remote(
            sbuf.at[e, :, cut(i)], right.at[e, :, cut(i)], rs_sem.at[e, i], rr_sem.at[e, i], up
        )

    def to_left(e, i):
        return remote(
            sbuf.at[e, :, cut(i)], left.at[e, :, cut(i)], ls_sem.at[e, i], lr_sem.at[e, i], down
        )

    def paired(e, i):
        if i == 0:
            pltpu.make_async_copy(keep_in.at[e], keep.at[e], k_sem.at[e]).wait()
        exchange(e, i).wait_recv()
        lanes = slice(i * step, (i + 1) * step)
        return keep[e, :, lanes].astype(F32) + yrecv[e, :, lanes].astype(F32)

    for e in order:
        for i in range(groups):
            lanes = slice(i * step, (i + 1) * step)

            @pl.when(e > d)
            def _():
                out[:, lanes] = paired(e, i)

                @pl.when(d > 0)
                def _():
                    to_right(e, i).wait_recv()
                    out[:, lanes] += right[e, :, lanes].astype(F32)

                sbuf[e, :, lanes] = out[:, lanes].astype(BF16)
                to_right(e, i).start()

            @pl.when(e < d)
            def _():
                out[:, lanes] = paired(e, i)

                @pl.when(d < n - 1)
                def _():
                    to_left(e, i).wait_recv()
                    out[:, lanes] += left[e, :, lanes].astype(F32)

                sbuf[e, :, lanes] = out[:, lanes].astype(BF16)
                to_left(e, i).start()

    for e in order:
        for i in range(groups):
            lanes = slice(i * step, (i + 1) * step)

            @pl.when(e == d)
            def _():
                out[:, lanes] = paired(e, i)

                @pl.when(d > 0)
                def _():
                    to_right(e, i).wait_recv()
                    out[:, lanes] += right[e, :, lanes].astype(F32)

                @pl.when(d < n - 1)
                def _():
                    to_left(e, i).wait_recv()
                    out[:, lanes] += left[e, :, lanes].astype(F32)

    for e in order:
        for i in range(groups):
            exchange(e, i).wait_send()

            @pl.when(e > d)
            def _():
                to_right(e, i).wait_send()

            @pl.when(e < d)
            def _():
                to_left(e, i).wait_send()


def reduce(keep, give):
    n, chunk, width = keep.shape
    groups = 3
    return pl.pallas_call(
        reduce_kernel,
        out_shape=jax.ShapeDtypeStruct((chunk, width), F32),
        in_specs=[ANY] * 2,
        out_specs=VMEM,
        scratch_shapes=[pltpu.VMEM(keep.shape, BF16)] * 5 + [DMA((n,))] + [DMA((n, groups))] * 6,
        compiler_params=pltpu.CompilerParams(
            collective_id=3, has_side_effects=True, vmem_limit_bytes=60 * MIB
        ),
        name="reduce",
    )(keep, give)


def body(
    inputs, cotangent, gain_attn, w_query, w_key, w_value, w_out, dim_scale, gain_mlp, w_up, w_down
):
    local = w_query.shape[2]
    head = dim_scale.shape[1]
    width = inputs.shape[2]
    n = lax.axis_size("dp")
    w_in = jnp.concatenate([w_query[0], w_key[0], w_value[0]], axis=1)
    multiplier = LOG2E / math.sqrt(head)
    per_dim = multiplier * jax.nn.softplus(dim_scale)
    done = forward(
        inputs, cotangent, w_in, w_out[0], w_up[0], w_down[0], gain_attn, gain_mlp, per_dim, head
    )
    layer_out, h, n1, q, k, v, o, lse, m, n2, u, a, g, win, wo, wu, wd = done
    input_grads, g_all, gu, gy, gp, dg1, dg2, ds = backward(
        (g, h, q, k, v, o, lse, m, u, win, wo, wu, wd),
        gain_attn,
        gain_mlp,
        jnp.tile(per_dim, (1, local // head)),
    )

    def over_rows(a, b):
        return lax.dot_general(a, b, (((0,), (0,)), ((), ())), preferred_element_type=F32)

    parts = []
    for j in range(2):
        cut = slice(j * local, (j + 1) * local)
        parts.append(
            jnp.concatenate(
                [
                    over_rows(n1, gp[j]).astype(BF16),
                    over_rows(n2, gu[:, cut]).astype(BF16),
                    over_rows(gy, o[:, cut]).astype(BF16),
                    over_rows(g_all, a[:, cut]).astype(BF16),
                ],
                axis=1,
            ).reshape(n, width // n, 6 * local)
        )
    grads = reduce(*parts)
    first_core = lax.rem(lax.axis_index("tensor"), 2) == 0
    dg2 = jnp.where(first_core, dg2, 0.0)
    ds = jnp.sum(ds.reshape(-1, head), axis=0, keepdims=True)
    dg1, dg2, ds = lax.psum((dg1, dg2, ds), ("tensor", "dp"))
    grad_scale = ds / per_dim * multiplier * jax.nn.sigmoid(dim_scale)
    pieces = [grads[:, i * local : (i + 1) * local] for i in range(6)]
    return (
        layer_out[None],
        input_grads[None],
        dg1,
        pieces[0][None],
        pieces[1][None],
        pieces[2][None],
        pieces[4].T[None],
        grad_scale,
        dg2,
        pieces[3][None],
        pieces[5].T[None],
    )


def solution(mesh):
    in_specs = (
        P("dp", "tensor", None),
        P("dp", "tensor", None),
        P("section", None),
        P("section", None, "tensor"),
        P("section", None, "tensor"),
        P("section", None, "tensor"),
        P("section", "tensor", None),
        P("section", None),
        P("section", None),
        P("section", None, "tensor"),
        P("section", "tensor", None),
    )
    out_specs = (
        P("section", "dp", "tensor", None),
        P("section", "dp", "tensor", None),
        P("section", None),
        P("section", "dp", "tensor"),
        P("section", "dp", "tensor"),
        P("section", "dp", "tensor"),
        P("section", "tensor", "dp"),
        P("section", None),
        P("section", None),
        P("section", "dp", "tensor"),
        P("section", "tensor", "dp"),
    )
    return jax.shard_map(body, mesh=mesh, in_specs=in_specs, out_specs=out_specs, check_vma=False)
```

time: 1680 us -> 574 us (0.34)
  waiting for transfers between devices: 1030 us -> 0 us
  Pallas kernels: 0 us -> 420 us
  matrix products: 265 us -> 17.7 us
  local copies, waits for them, and re-layouts: 149 us -> 34.4 us
  other arithmetic: 109 us -> 25.2 us
  loops' own time: 24.9 us -> 0 us
    reduce_scatter x14 -> x0, waiting for transfers between devices: 683 us -> none  [the longest x3 155 us: body(): lax.psum_scatter(jnp.dot(forward_activated, w_d, preferred_element_type=j...]
    pallas_call x0 -> x3, Pallas kernels: none -> 420 us  [the longest x1 177 us: backward(): pl.pallas_call(backward_kernel, out_shape=outs, in_specs=[ANY] * 13 + [VM...]
    all_gather x12 -> x0, waiting for transfers between devices: 280 us -> none  [the longest x3 81.6 us: body(): lax.all_gather(normed.astype(jnp.bfloat16), 'tensor', axis=0, tiled=True)]
    dot_general x78 -> x8, matrix products: 265 us -> 17.7 us  [over_rows(): lax.dot_general(a, b, (((0,), (0,)), ((), ())), preferred_element_type=F32)]
    dynamic_update_slice x12 -> x0, local copies, waits for them, and re-layouts: 85.4 us -> none  [attend(): mixed, logsum = lax.map(one_block, starts)]
    ppermute x4 -> x0, waiting for transfers between devices: 62 us -> none  [from_behind(): return lax.ppermute(block, axis, route)]
    convert_element_type x31 -> x0, other arithmetic: 47.8 us -> none  [the longest x6 14.8 us: one_block(): grad_scores = (probs * (grad_probs - inner)).astype(jnp.bfloat16)]
    reduce_sum x24 -> x1, other arithmetic: 42.2 us -> 0.02 us  [body(): ds = jnp.sum(ds.reshape(-1, head), axis=0, keepdims=True)]
  transfers between devices with their start and end apart: 32 -> 0, of which waited for: 28 -> 0; matrix products, arithmetic and copies ran while one was open for 10% -> 0% of each run, Pallas kernels for 0% -> 0%
where the time goes in v1:
time: 574 us; the launch traced here: 565 us
  Pallas kernels  420 us (73%)
  blocking collectives  67.2 us (12%)
  local copies, waits for them, and re-layouts  34.4 us (6%)
  other arithmetic  25.2 us (4%)
  matrix products  17.7 us (3%)
    pallas_call x1, Pallas kernels, backward(): pl.pallas_call(backward_kernel, out_shape=outs, in_specs=[ANY] * 13 + [VM...  177 us
    pallas_call x1, Pallas kernels, forward(): pl.pallas_call(forward_kernel, out_shape=outs, in_specs=[ANY] * 6 + [VMEM...  124 us
    pallas_call x1, Pallas kernels, reduce(): pl.pallas_call(reduce_kernel, out_shape=jax.ShapeDtypeStruct((chunk, widt...  119 us
    psum x1, blocking collectives, body(): dg1, dg2, ds = lax.psum((dg1, dg2, ds), ('tensor', 'dp'))  67.2 us
    concatenate x2, other arithmetic, body(): jnp.concatenate([over_rows(n1, gp[j]).astype(BF16), over_rows(n2, gu[:, c...  21.5 us
    dot_general x8, matrix products, over_rows(): lax.dot_general(a, b, (((0,), (0,)), ((), ())), preferred_element_type=F32)  17.7 us
    concatenate x2, local copies, waits for them, and re-layouts, body(): jnp.concatenate([over_rows(n1, gp[j]).astype(BF16), over_rows(n2, gu[:, c...  16.1 us
    unnamed x40, local copies, waits for them, and re-layouts  14 us

profile of v1, /device:TPU:0, one launch (start us, length us, event | category | flops | bytes accessed | tf_op | source)
XLA Modules:
  0.0 565.5 jit_solution(4805020460947176341)
XLA Ops:
  0.6 1.6 copy.22
  2.2 1.6 copy.23
  3.8 1.6 copy.24
  5.3 2.5 pad_maximum_fusion.2.w_in
  7.9 2.2 copy.25
  10.6 124.3 %forward.1 = (bf16[2,256,1280]{2,1,0:T(8,128)(2,1)}, bf16[4,256,1280]{2,1,0:T(8,128)(2,1)}, bf16[1024,1280]{1,0:T(8,128)(2,1)}, bf16[8,1024,80]{2,1,0:T(8,128)(2...) custom-call(bf16[2,256,1280]{2,1,0:T(8,128)(2,1)} %inputs.1, ...), custom_call_target="tpu_custom_call" | custom-call | tf_op jit(solution)/shard_map/forward/pallas_call | solution.py:433
  135.6 176.6 %backward.1 = (bf16[2,256,1280]{2,1,0:T(8,128)(2,1)}, bf16[1024,1280]{1,0:T(8,128)(2,1)}, bf16[1024,640]{1,0:T(8,128)(2,1)}, bf16[1024,1280]{1,0:T(8,128)(2,1)},...) custom-call(bf16[4,256,1280]{2,1,0:T(8,128)(2,1)} %get-tuple-element.37.g_in, ...), custom_call_target="tpu_custom_call" | custom-call | tf_op jit(solution)/shard_map/backward/pallas_call | solution.py:737
  312.2 5.3 convolution_convert_fusion
  317.5 1.3 convolution_convert_fusion.4
  319.6 1.3 convolution_convert_fusion.3
  321.7 1.3 convolution_convert_fusion.2
  323.0 10.8 %pad_maximum_fusion.1 = bf16[1280,1920]{0,1:T(8,128)(2,1)} fusion(bf16[1280,320]{0,1:T(8,128)(2,1)S(1)} %convolution_convert_fusion.2, bf16[1280,320]{0,1:T(8,128)(2,1)S(1)} %convolution_convert_fusion.3, bf16[1280,320]{0,1:T(8,128)(2,1)S(1)} %convolution_convert_fusion.4, bf16[1280,960]{0,1:T(8,128)(2,1)S(1)} %convolution_convert_fusion), kind=kLoop, calls=%fused_computation.1 | loop fusion | flops 19660800 | bytes 9830400 | tf_op jit(solution)/shard_map/concatenate | solution.py:904
  333.8 8.1 %copy.27 = bf16[1280,1920]{1,0:T(8,128)(2,1)} copy(bf16[1280,1920]{0,1:T(8,128)(2,1)} %pad_maximum_fusion.1) | data formatting | bytes 9830400 | tf_op jit(solution)/shard_map/concatenate | solution.py:904
  341.9 5.3 convolution_convert_fusion.1
  347.3 1.1 convolution_convert_fusion.7
  349.0 1.1 convolution_convert_fusion.6
  350.7 1.1 convolution_convert_fusion.5
  351.9 10.7 %pad_maximum_fusion = bf16[1280,1920]{0,1:T(8,128)(2,1)} fusion(bf16[1280,320]{0,1:T(8,128)(2,1)S(1)} %convolution_convert_fusion.5, bf16[1280,320]{0,1:T(8,128)(2,1)S(1)} %convolution_convert_fusion.6, bf16[1280,320]{0,1:T(8,128)(2,1)S(1)} %convolution_convert_fusion.7, bf16[1280,960]{0,1:T(8,128)(2,1)S(1)} %convolution_convert_fusion.1), kind=kLoop, calls=%fused_computation | loop fusion | flops 19660800 | bytes 9830400 | tf_op jit(solution)/shard_map/concatenate | solution.py:904
  362.6 8.0 %copy.26 = bf16[1280,1920]{1,0:T(8,128)(2,1)} copy(bf16[1280,1920]{0,1:T(8,128)(2,1)} %pad_maximum_fusion) | data formatting | bytes 9830400 | tf_op jit(solution)/shard_map/concatenate | solution.py:904
  370.5 119.1 %reduce.1 = f32[320,1920]{1,0:T(8,128)} custom-call(bf16[4,320,1920]{2,1,0:T(8,128)(2,1)} %bitcast.44, bf16[4,320,1920]{2,1,0:T(8,128)(2,1)} %bitcast.43), custom_call_target="tpu_custom_call" | custom-call | tf_op jit(solution)/shard_map/reduce/pallas_call | solution.py:863
  489.6 3.6 slice_bitcast_fusion
  495.4 67.2 %all-reduce = (f32[1,1280]{1,0:T(1,128)}, f32[1,80]{1,0:T(1,128)S(1)}, f32[1,1280]{1,0:T(1,128)}) all-reduce(f32[1,1280]{1,0:T(1,128)S(1)} %copy-done.3, f32[1,80]{1,0:T(1,128)S(1)} %bitcast.53, f32[1,1280]{1,0:T(1,128)S(1)} %broadcast_select_fusion), channel_id=1, replica_groups=mesh['section'=2,'tensor'=4,'dp'=4] {'tensor','dp'}, use_global_device_ids=true, to_apply=%region_0.1 | all-reduce | flops 2640 | bytes 21120 | tf_op jit(solution)/shard_map/psum | solution.py:918
  563.1 1.1 copy.32
  564.2 1.1 copy.33
  (42 shorter events, 6.8 us)
Async XLA Ops:
  5.3 4.8 copy-start.15
  312.2 5.3 copy-start.6
  312.2 5.3 copy-start.13
  317.5 1.3 copy-start
  317.5 2.1 copy-start.10
  319.6 1.7 copy-start.8
  319.6 2.1 copy-start.12
  341.9 5.3 copy-start.7
  341.9 5.3 copy-start.14
  347.3 1.7 copy-start.11
  349.0 1.7 copy-start.9
  489.6 5.7 %copy-start.4 = (f32[1,1280]{1,0:T(1,128)S(1)}, f32[1,1280]{1,0:T(1,128)}, u32[]{:S(2)}) copy-start(f32[1,1280]{1,0:T(1,128)} %get-tuple-element.60) | copy-start | bytes 15364
  489.6 5.7 %copy-start.5 = (f32[2,320]{1,0:T(2,128)S(1)}, f32[2,320]{1,0:T(2,128)}, u32[]{:S(2)}) copy-start(f32[2,320]{1,0:T(2,128)} %get-tuple-element.59) | copy-start | bytes 7684
  489.6 5.8 %copy-start.3 = (f32[1,1280]{1,0:T(1,128)S(1)}, f32[1,1280]{1,0:T(1,128)}, u32[]{:S(2)}) copy-start(f32[1,1280]{1,0:T(1,128)} %get-tuple-element.51) | copy-start | bytes 15364
  489.6 73.5 %copy-start.1 = (bf16[2,256,1280]{2,1,0:T(8,128)(2,1)S(1)}, bf16[2,256,1280]{2,1,0:T(8,128)(2,1)}, u32[]{:S(2)}) copy-start(bf16[2,256,1280]{2,1,0:T(8,128)(2,1)} %get-tuple-element.36) | copy-start | bytes 3932164
  562.6 1.6 copy-start.2

commit v2 on v1

--- a/solution.py
+++ b/solution.py
@@ -747,130 +747,350 @@
     )(*saved, gain_one, gain_two, scale)
 
 
-def reduce_kernel(
-    keep_in, give_in, out, keep, yrecv, right, left, sbuf,
-    k_sem, ys_sem, yr_sem, rs_sem, rr_sem, ls_sem, lr_sem,
+def farthest_first(d, k, n):
+    found = 0
+    for i in range(n):
+        above = list(range(n - 1, i, -1))
+        below = list(range(i))
+        first, second = (above, below) if len(above) >= len(below) else (below, above)
+        lead = len(first) - len(second) - 1
+        order = first[: max(lead, 0)]
+        rest = first[max(lead, 0) :]
+        for j in range(max(len(rest), len(second))):
+            order += rest[j : j + 1] + second[j : j + 1]
+        order.append(i)
+        picked = 0
+        for j, e in enumerate(order):
+            picked = picked + jnp.where(k == j, e, 0)
+        found = found + jnp.where(d == i, picked, 0)
+    return found
+
+
+def gradient_kernel(
+    n1_in, n2_in, gy_in, g_in, gp_in, gu_in, o_in, a_in, small,
+    out, small_out,
+    x, xt, gp, gu, o, a, keep, give, yrecv, flow, last, keep_d, give_d, flow_k, flow_g, last_k, last_g,
+    yd, smalls, chain,
+    x_sem, g_sem, ys_sem, yr_sem, fs_sem, fr_sem, last_sem, ks_sem, kr_sem, gs_sem, gr_sem, last_d_sem,
+    yds_sem, ydr_sem, ss_sem, sr_sem, cs_sem, cr_sem,
 ):
     s, t, d = lax.axis_index("section"), lax.axis_index("tensor"), lax.axis_index("dp")
-    n, chunk, width = keep.shape
-    groups = ys_sem.shape[1]
-    step = width // groups
+    n, chunk, wide = keep.shape
+    local = keep_d.shape[2]
+    pieces = ys_sem.shape[1]
+    step = chunk // pieces
+    core = (s, other(t), d)
     across = (s, lax.rem(t + 2, 4), d)
+    diagonal = (s, other(lax.rem(t + 2, 4)), d)
     up = (s, t, lax.rem(d + 1, n))
     down = (s, t, lax.rem(d + n - 1, n))
-    greet([across, up, down])
-
-    def cut(i):
-        return pl.ds(i * step, step)
-
-    order = []
-    for i in range((n + 1) // 2):
-        order += [n - 1 - i, i] if n - 1 - i != i else [i]
-    for e in order:
-        pltpu.make_async_copy(keep_in.at[e], keep.at[e], k_sem.at[e]).start()
-        for i in range(groups):
-            remote(
-                give_in.at[e, :, cut(i)],
-                yrecv.at[e, :, cut(i)],
-                ys_sem.at[e, i],
-                yr_sem.at[e, i],
-                across,
-            ).start()
+
+    def load(i, source):
+        return pltpu.make_async_copy(source, x.at[i % 2], x_sem.at[i])
+
+    sources = [g_in, n1_in, n2_in, gy_in]
+    load(0, g_in).start()
+    operands = [(a_in, a), (gp_in, gp), (gu_in, gu), (o_in, o)]
+    pltpu.make_async_copy(a_in, a, g_sem.at[0]).start()
+    load(1, n1_in).start()
+    for i in range(1, 4):
+        pltpu.make_async_copy(operands[i][0], operands[i][1], g_sem.at[i]).start()
+
+    greet([core, across, diagonal, up, down])
+
+    partners = [core, across, diagonal]
+
+    def share(i):
+        return remote(small, smalls.at[i], ss_sem.at[i], sr_sem.at[i], partners[i])
+
+    for i in range(3):
+        share(i).start()
+
+    def turn(i):
+        load(i, sources[i]).wait()
+        turned = jnp.transpose(x[i % 2])
+        for e in range(n):
+            xt[i, e] = turned[e * chunk : (e + 1) * chunk]
+        if i + 2 < 4:
+            load(i + 2, sources[i + 2]).start()
+
+    def flow_piece(buffer, into, e, send, receive, device):
+        return remote(buffer.at[e], into.at[e], send.at[e], receive.at[e], device)
+
+    turn(0)
+    pltpu.make_async_copy(a_in, a, g_sem.at[0]).wait()
+
+    def down_product(e, _):
+        both = plain(xt[0, e], a[...])
+        keep_d[e] = both[:, :local].astype(BF16)
+        give_d[e] = both[:, local:].astype(BF16)
+        return 0
+
+    lax.fori_loop(0, n, down_product, 0)
+
+    line_d = [(keep_d, flow_k, last_k, ks_sem, kr_sem, 0), (give_d, flow_g, last_g, gs_sem, gr_sem, 1)]
+
+    def upstream_d(e, buffer, into, send, receive):
+        piece = into.at[e]
+        remote(piece, piece, send.at[e], receive.at[e], up).wait_recv()
+        buffer[e] = (buffer[e].astype(F32) + into[e].astype(F32)).astype(BF16)
+
+    def send_d(e, buffer, into, spare, send, receive, i):
+        @pl.when(e > d)
+        def _():
+            remote(buffer.at[e], into.at[e], send.at[e], receive.at[e], up).start()
+
+        @pl.when(e < d - 1)
+        def _():
+            remote(buffer.at[e], into.at[e], send.at[e], receive.at[e], down).start()
+
+        @pl.when(e == d - 1)
+        def _():
+            remote(buffer.at[e], spare, send.at[e], last_d_sem.at[i], down).start()
+
+    def ends(k, _):
+        e = farthest_first(d, k, n)
+        for buffer, into, spare, send, receive, i in line_d:
+
+            @pl.when(((d == 0) | (d == n - 1)) & (e != d))
+            def _():
+                send_d(e, buffer, into, spare, send, receive, i)
+
+        return 0
+
+    lax.fori_loop(0, n, ends, 0)
+
+    turn(1)
+    turn(2)
+    turn(3)
+    for i in range(1, 4):
+        pltpu.make_async_copy(operands[i][0], operands[i][1], g_sem.at[i]).wait()
 
     def exchange(e, i):
-        piece = yrecv.at[e, :, cut(i)]
-        return remote(piece, piece, ys_sem.at[e, i], yr_sem.at[e, i], across)
-
-    def to_right(e, i):
+        rows = pl.ds(i * step, step)
         return remote(
-            sbuf.at[e, :, cut(i)], right.at[e, :, cut(i)], rs_sem.at[e, i], rr_sem.at[e, i], up
+            give.at[e, rows], yrecv.at[e, rows], ys_sem.at[e, i], yr_sem.at[e, i], across
         )
 
-    def to_left(e, i):
-        return remote(
-            sbuf.at[e, :, cut(i)], left.at[e, :, cut(i)], ls_sem.at[e, i], lr_sem.at[e, i], down
-        )
-
-    def paired(e, i):
-        if i == 0:
-            pltpu.make_async_copy(keep_in.at[e], keep.at[e], k_sem.at[e]).wait()
-        exchange(e, i).wait_recv()
-        lanes = slice(i * step, (i + 1) * step)
-        return keep[e, :, lanes].astype(F32) + yrecv[e, :, lanes].astype(F32)
-
-    for e in order:
-        for i in range(groups):
-            lanes = slice(i * step, (i + 1) * step)
+    def products(k, _):
+        e = farthest_first(d, k, n)
+        ups = plain(xt[2, e], gu[...])
+        outs = plain(xt[3, e], o[...])
+        for j, target in ((1, give), (0, keep)):
+            cut = slice(j * local, (j + 1) * local)
+            target[e] = jnp.concatenate(
+                [
+                    plain(xt[1, e], gp[j]).astype(BF16),
+                    ups[:, cut].astype(BF16),
+                    outs[:, cut].astype(BF16),
+                ],
+                axis=1,
+            )
+            if j:
+                for i in range(pieces):
+                    exchange(e, i).start()
+        return 0
+
+    lax.fori_loop(0, n, products, 0)
+
+    for i in range(3):
+        share(i).wait_recv()
+    mine = small[...] + smalls[0] + (smalls[1] + smalls[2])
+    small_out[...] = mine
+
+    def link(i, device):
+        return remote(chain.at[i], chain.at[2 + i], cs_sem.at[i], cr_sem.at[i], device)
+
+    for i, first, final, device in ((0, d == 0, d == n - 1, up), (1, d == n - 1, d == 0, down)):
+        chain[i] = mine
+
+        @pl.when(jnp.logical_not(first))
+        def _():
+            link(i, device).wait_recv()
+            chain[i] = mine + chain[2 + i]
+            small_out[...] += chain[2 + i]
+
+        @pl.when(jnp.logical_not(final))
+        def _():
+            link(i, device).start()
+
+    def middle(k, _):
+        e = farthest_first(d, k, n)
+        for buffer, into, spare, send, receive, i in line_d:
+
+            @pl.when((d > 0) & (d < n - 1) & (e != d))
+            def _():
+                upstream_d(e, buffer, into, send, receive)
+                send_d(e, buffer, into, spare, send, receive, i)
+
+        return 0
+
+    lax.fori_loop(0, n, middle, 0)
+
+    def flows(k, _):
+        e = farthest_first(d, k, n)
+        for i in range(pieces):
+            at = pl.ds(i * step, step)
+
+            first = ((e > d) & (d == 0)) | ((e < d) & (d == n - 1))
+
+            @pl.when(e != d)
+            def _():
+                exchange(e, i).wait_recv()
+
+            @pl.when((e != d) & first)
+            def _():
+                keep[e, at] = (keep[e, at].astype(F32) + yrecv[e, at].astype(F32)).astype(BF16)
+
+            @pl.when((e != d) & jnp.logical_not(first))
+            def _():
+                piece = flow.at[e, at]
+                remote(piece, piece, fs_sem.at[e, i], fr_sem.at[e, i], up).wait_recv()
+                total = keep[e, at].astype(F32) + yrecv[e, at].astype(F32)
+                keep[e, at] = (total + flow[e, at].astype(F32)).astype(BF16)
+
+            src = keep.at[e, at]
 
             @pl.when(e > d)
             def _():
-                out[:, lanes] = paired(e, i)
-
-                @pl.when(d > 0)
-                def _():
-                    to_right(e, i).wait_recv()
-                    out[:, lanes] += right[e, :, lanes].astype(F32)
-
-                sbuf[e, :, lanes] = out[:, lanes].astype(BF16)
-                to_right(e, i).start()
-
-            @pl.when(e < d)
+                remote(src, flow.at[e, at], fs_sem.at[e, i], fr_sem.at[e, i], up).start()
+
+            @pl.when(e < d - 1)
             def _():
-                out[:, lanes] = paired(e, i)
-
-                @pl.when(d < n - 1)
-                def _():
-                    to_left(e, i).wait_recv()
-                    out[:, lanes] += left[e, :, lanes].astype(F32)
-
-                sbuf[e, :, lanes] = out[:, lanes].astype(BF16)
-                to_left(e, i).start()
-
-    for e in order:
-        for i in range(groups):
-            lanes = slice(i * step, (i + 1) * step)
-
-            @pl.when(e == d)
+                remote(src, flow.at[e, at], fs_sem.at[e, i], fr_sem.at[e, i], down).start()
+
+            @pl.when(e == d - 1)
             def _():
-                out[:, lanes] = paired(e, i)
-
-                @pl.when(d > 0)
-                def _():
-                    to_right(e, i).wait_recv()
-                    out[:, lanes] += right[e, :, lanes].astype(F32)
-
-                @pl.when(d < n - 1)
-                def _():
-                    to_left(e, i).wait_recv()
-                    out[:, lanes] += left[e, :, lanes].astype(F32)
-
-    for e in order:
-        for i in range(groups):
+                remote(src, last.at[at], fs_sem.at[e, i], last_sem.at[i], down).start()
+
+        return 0
+
+    lax.fori_loop(0, n, flows, 0)
+
+    for buffer, into, spare, send, receive, i in line_d:
+
+        @pl.when(d > 0)
+        def _():
+            upstream_d(d, buffer, into, send, receive)
+
+        @pl.when(d < n - 1)
+        def _():
+            remote(spare, spare, send.at[0], last_d_sem.at[i], down).wait_recv()
+            buffer[d] = (buffer[d].astype(F32) + spare[...].astype(F32)).astype(BF16)
+
+    crossing = remote(give_d.at[d], yd, yds_sem, ydr_sem, across)
+    crossing.start()
+    for i in range(pieces):
+        at = pl.ds(i * step, step)
+        exchange(d, i).wait_recv()
+        out[at, :wide] = keep[d, at].astype(F32) + yrecv[d, at].astype(F32)
+
+        @pl.when(d > 0)
+        def _():
+            piece = flow.at[d, at]
+            remote(piece, piece, fs_sem.at[d, i], fr_sem.at[d, i], up).wait_recv()
+            out[at, :wide] += flow[d, at].astype(F32)
+
+        @pl.when(d < n - 1)
+        def _():
+            piece = last.at[at]
+            remote(piece, piece, fs_sem.at[d, i], last_sem.at[i], down).wait_recv()
+            out[at, :wide] += last[at].astype(F32)
+
+    crossing.wait_recv()
+    out[:, wide:] = keep_d[d].astype(F32) + yd[...].astype(F32)
+
+    crossing.wait_send()
+    for i in range(3):
+        share(i).wait_send()
+
+    @pl.when(d < n - 1)
+    def _():
+        link(0, up).wait_send()
+
+    @pl.when(d > 0)
+    def _():
+        link(1, down).wait_send()
+
+    def drain(e, _):
+        for i in range(pieces):
             exchange(e, i).wait_send()
 
-            @pl.when(e > d)
-            def _():
-                to_right(e, i).wait_send()
-
-            @pl.when(e < d)
-            def _():
-                to_left(e, i).wait_send()
-
-
-def reduce(keep, give):
-    n, chunk, width = keep.shape
-    groups = 3
+        @pl.when(e != d)
+        def _():
+            for i in range(pieces):
+                piece = keep.at[e, pl.ds(i * step, step)]
+                remote(piece, piece, fs_sem.at[e, i], fr_sem.at[e, i], up).wait_send()
+            for buffer, into, spare, send, receive, i in line_d:
+                remote(buffer.at[e], buffer.at[e], send.at[e], receive.at[e], up).wait_send()
+
+        return 0
+
+    lax.fori_loop(0, n, drain, 0)
+
+
+def gradients(n1, n2, gy, g, gp, gu, o, a, small):
+    n = lax.axis_size("dp")
+    length, width = n1.shape
+    local = gp.shape[2] // 3
+    chunk = width // n
+    wide = 5 * local
+    pieces = 4 if chunk % 64 == 0 else 1
+    big = pltpu.VMEM((n, chunk, wide), BF16)
+    line = pltpu.VMEM((n, chunk, local), BF16)
     return pl.pallas_call(
-        reduce_kernel,
-        out_shape=jax.ShapeDtypeStruct((chunk, width), F32),
-        in_specs=[ANY] * 2,
-        out_specs=VMEM,
-        scratch_shapes=[pltpu.VMEM(keep.shape, BF16)] * 5 + [DMA((n,))] + [DMA((n, groups))] * 6,
+        gradient_kernel,
+        out_shape=[
+            jax.ShapeDtypeStruct((chunk, 6 * local), F32),
+            jax.ShapeDtypeStruct(small.shape, F32),
+        ],
+        in_specs=[ANY] * 8 + [VMEM],
+        out_specs=[VMEM, VMEM],
+        scratch_shapes=[
+            pltpu.VMEM((2, length, width), BF16),
+            pltpu.VMEM((4, n, chunk, length), BF16),
+            pltpu.VMEM(gp.shape, BF16),
+            pltpu.VMEM(gu.shape, BF16),
+            pltpu.VMEM(o.shape, BF16),
+            pltpu.VMEM(a.shape, BF16),
+            big,
+            big,
+            big,
+            big,
+            pltpu.VMEM((chunk, wide), BF16),
+            line,
+            line,
+            line,
+            line,
+            pltpu.VMEM((chunk, local), BF16),
+            pltpu.VMEM((chunk, local), BF16),
+            pltpu.VMEM((chunk, local), BF16),
+            pltpu.VMEM((3,) + small.shape, F32),
+            pltpu.VMEM((4,) + small.shape, F32),
+            DMA((4,)),
+            DMA((4,)),
+            DMA((n, pieces)),
+            DMA((n, pieces)),
+            DMA((n, pieces)),
+            DMA((n, pieces)),
+            DMA((pieces,)),
+            DMA((n,)),
+            DMA((n,)),
+            DMA((n,)),
+            DMA((n,)),
+            DMA((2,)),
+            DMA,
+            DMA,
+            DMA((3,)),
+            DMA((3,)),
+            DMA((2,)),
+            DMA((2,)),
+        ],
         compiler_params=pltpu.CompilerParams(
-            collective_id=3, has_side_effects=True, vmem_limit_bytes=60 * MIB
+            collective_id=3, has_side_effects=True, vmem_limit_bytes=62 * MIB
         ),
-        name="reduce",
-    )(keep, give)
+        name="gradients",
+    )(n1, n2, gy, g, gp, gu, o, a, small)
 
 
 def body(
@@ -879,7 +1099,6 @@
     local = w_query.shape[2]
     head = dim_scale.shape[1]
     width = inputs.shape[2]
-    n = lax.axis_size("dp")
     w_in = jnp.concatenate([w_query[0], w_key[0], w_value[0]], axis=1)
     multiplier = LOG2E / math.sqrt(head)
     per_dim = multiplier * jax.nn.softplus(dim_scale)
@@ -894,28 +1113,12 @@
         jnp.tile(per_dim, (1, local // head)),
     )
 
-    def over_rows(a, b):
-        return lax.dot_general(a, b, (((0,), (0,)), ((), ())), preferred_element_type=F32)
-
-    parts = []
-    for j in range(2):
-        cut = slice(j * local, (j + 1) * local)
-        parts.append(
-            jnp.concatenate(
-                [
-                    over_rows(n1, gp[j]).astype(BF16),
-                    over_rows(n2, gu[:, cut]).astype(BF16),
-                    over_rows(gy, o[:, cut]).astype(BF16),
-                    over_rows(g_all, a[:, cut]).astype(BF16),
-                ],
-                axis=1,
-            ).reshape(n, width // n, 6 * local)
-        )
-    grads = reduce(*parts)
     first_core = lax.rem(lax.axis_index("tensor"), 2) == 0
     dg2 = jnp.where(first_core, dg2, 0.0)
-    ds = jnp.sum(ds.reshape(-1, head), axis=0, keepdims=True)
-    dg1, dg2, ds = lax.psum((dg1, dg2, ds), ("tensor", "dp"))
+    small = jnp.concatenate([dg1, dg2, ds.reshape(1, -1)], axis=1)
+    grads, small = gradients(n1, n2, gy, g_all, gp, gu, o, a, small)
+    dg1, dg2 = small[:, :width], small[:, width : 2 * width]
+    ds = jnp.sum(small[:, 2 * width :].reshape(-1, head), axis=0, keepdims=True)
     grad_scale = ds / per_dim * multiplier * jax.nn.sigmoid(dim_scale)
     pieces = [grads[:, i * local : (i + 1) * local] for i in range(6)]
     return (

time: 574 us -> 444 us (0.77)
  blocking collectives: 67.2 us -> 0 us
  other arithmetic: 25.2 us -> 5.62 us
  matrix products: 17.7 us -> 0 us
  local copies, waits for them, and re-layouts: 34.4 us -> 16.7 us
    psum x1 -> x0, blocking collectives: 67.2 us -> none  [body(): dg1, dg2, ds = lax.psum((dg1, dg2, ds), ('tensor', 'dp'))]
    concatenate x2 -> x1, other arithmetic: 21.5 us -> 1.3 us  [body(): small = jnp.concatenate([dg1, dg2, ds.reshape(1, -1)], axis=1)]
    dot_general x8 -> x0, matrix products: 17.7 us -> none  [over_rows(): lax.dot_general(a, b, (((0,), (0,)), ((), ())), preferred_element_type=F32)]
    concatenate x2 -> x0, local copies, waits for them, and re-layouts: 16.1 us -> none  [body(): jnp.concatenate([over_rows(n1, gp[j]).astype(BF16), over_rows(n2, gu[:, c...]
    unnamed x40 -> x16, local copies, waits for them, and re-layouts: 14 us -> 11 us
where the time goes in v2:
time: 444 us; the launch traced here: 441 us
  Pallas kernels  418 us (94%)
  local copies, waits for them, and re-layouts  16.7 us (4%)
  other arithmetic  5.62 us (1%)
    pallas_call x1, Pallas kernels, backward(): pl.pallas_call(backward_kernel, out_shape=outs, in_specs=[ANY] * 13 + [VM...  176 us
    pallas_call x1, Pallas kernels, forward(): pl.pallas_call(forward_kernel, out_shape=outs, in_specs=[ANY] * 6 + [VMEM...  124 us
    pallas_call x1, Pallas kernels, gradients(): pl.pallas_call(gradient_kernel, out_shape=[jax.ShapeDtypeStruct((chunk, 6...  117 us
    unnamed x16, local copies, waits for them, and re-layouts  11 us

profile of v2, /device:TPU:0, one launch (start us, length us, event | category | flops | bytes accessed | tf_op | source)
XLA Modules:
  0.0 441.1 jit_solution(8185742964693549940)
XLA Ops:
  0.6 1.6 copy.22
  2.2 1.6 copy.23
  3.8 1.6 copy.24
  5.3 0.0 copy-start.3
  5.3 2.5 pad_maximum_fusion.w_in
  7.9 2.2 copy.25
  10.1 0.0 copy-done.3
  10.1 0.5 fusion.scale
  10.6 124.3 %forward.1 = (bf16[2,256,1280]{2,1,0:T(8,128)(2,1)}, bf16[4,256,1280]{2,1,0:T(8,128)(2,1)}, bf16[1024,1280]{1,0:T(8,128)(2,1)}, bf16[8,1024,80]{2,1,0:T(8,128)(2...) custom-call(bf16[2,256,1280]{2,1,0:T(8,128)(2,1)} %inputs.1, ...), custom_call_target="tpu_custom_call" | custom-call | tf_op jit(solution)/shard_map/forward/pallas_call | solution.py:433
  134.9 0.6 tile.13.scale
  135.5 176.4 %backward.1 = (bf16[2,256,1280]{2,1,0:T(8,128)(2,1)}, bf16[1024,1280]{1,0:T(8,128)(2,1)}, bf16[1024,640]{1,0:T(8,128)(2,1)}, bf16[1024,1280]{1,0:T(8,128)(2,1)},...) custom-call(bf16[4,256,1280]{2,1,0:T(8,128)(2,1)} %get-tuple-element.39.g_in, ...), custom_call_target="tpu_custom_call" | custom-call | tf_op jit(solution)/shard_map/backward/pallas_call | solution.py:737
  312.0 0.7 broadcast_select_fusion
  312.7 0.8 reshape.34
  313.4 1.3 pad_maximum_fusion.1.small
  314.7 117.3 %gradients.1 = (f32[320,1920]{1,0:T(8,128)}, f32[1,3200]{1,0:T(1,128)}) custom-call(bf16[1024,1280]{1,0:T(8,128)(2,1)} %get-tuple-element.53.n1_in, bf16[1024,1280]{1,0:T(8,128)(2,1)} %get-tuple-element.54.n2_in, bf16[1024,1280]{1,0:T(8,128)(2,1)} %get-tuple-element.55.gy_in, bf16[1024,1280]{1,0:T(8,128)(2,1)} %get-tuple-element.56.g_in, ...), custom_call_target="tpu_custom_call" | custom-call | tf_op jit(solution)/shard_map/gradients/pallas_call | solution.py:1041
  432.0 3.6 slice_bitcast_fusion
  435.7 1.0 copy.26
  436.7 1.0 copy.27
  437.7 0.6 fusion.1
  438.3 0.1 reshape.35
  438.4 0.5 divide_multiply_fusion
  438.9 1.1 copy.30
  440.0 0.0 copy-done.1
  440.0 1.1 copy.31
  (9 shorter events, 0.1 us)
Async XLA Ops:
  5.3 4.7 %copy-start.3 = (f32[1,80]{1,0:T(1,128)S(1)}, f32[1,80]{1,0:T(1,128)}, u32[]{:S(2)}) copy-start(f32[1,80]{1,0:T(1,128)} %param.18) | copy-start | bytes 964
  432.0 5.7 %copy-start.2 = (f32[1,3200]{1,0:T(1,128)S(1)}, f32[1,3200]{1,0:T(1,128)}, u32[]{:S(2)}) copy-start(f32[1,3200]{1,0:T(1,128)} %get-tuple-element.63) | copy-start | bytes 38404
  432.0 6.9 %copy-start = (bf16[2,256,1280]{2,1,0:T(8,128)(2,1)S(1)}, bf16[2,256,1280]{2,1,0:T(8,128)(2,1)}, u32[]{:S(2)}) copy-start(bf16[2,256,1280]{2,1,0:T(8,128)(2,1)} %get-tuple-element.38) | copy-start | bytes 3932164
  438.4 1.6 copy-start.1

commit v3 on v2

--- a/solution.py
+++ b/solution.py
@@ -60,12 +60,12 @@
 
 
 def forward_kernel(
-    inputs, cotangent, w_in, w_o, w_u, w_d, gain_one, gain_two, scale,
+    inputs, cotangent, w_q, w_k, w_v, w_o, w_u, w_d, gain_one, gain_two, scale,
     out_rows, h_out, n1_out, q_out, k_out, v_out, o_out, lse_out, m_out, n2_out, u_out, a_out,
     g_out, win_out, wo_out, wu_out, wd_out,
-    land, win, wo, wu, wd, n1, q, k, v, o_heads, o, lse_cols, lse, ysend, yrecv, m, n2, u, a,
+    land, win, wo, wu, wd, passing, n1, q, k, v, o_heads, o, lse_cols, lse, ysend, yrecv, m, n2, u, a,
     zpart, zrecv, xout,
-    own_sem, xs_sem, xr_sem, xfs_sem, xfr_sem, wys_sem, wyr_sem, wzs_sem, wzr_sem,
+    own_sem, ps_sem, pr_sem, xs_sem, xp_sem, xr_sem, xfs_sem, wys_sem, wyr_sem, wzs_sem, wzr_sem,
     ns_sem, nr_sem, nfs_sem, nfr_sem, ys_sem, yr_sem, zs_sem, zr_sem, os_sem, or_sem, save_sem,
 ):
     s, t, d = lax.axis_index("section"), lax.axis_index("tensor"), lax.axis_index("dp")
@@ -75,9 +75,11 @@
     heads, _, head = q.shape
     per = heads // 2
     c, y = lax.rem(t, 2), t // 2
-    core = (s, other(t), d)
-    across = (s, lax.rem(t + 2, 4), d)
-    diagonal = (s, other(lax.rem(t + 2, 4)), d)
+    t_core, t_across = other(t), lax.rem(t + 2, 4)
+    t_diagonal = other(t_across)
+    core = (s, t_core, d)
+    across = (s, t_across, d)
+    diagonal = (s, t_diagonal, d)
     beside = (s, t, other(d))
     section = (1 - s, t, d)
     greet([core, across, diagonal, beside, section])
@@ -85,89 +87,107 @@
     mine = pl.ds(pl.multiple_of(c * half, half), half)
     theirs = pl.ds(pl.multiple_of((1 - c) * half, half), half)
 
-    own = [
-        pltpu.make_async_copy(w_in, win.at[0], own_sem.at[0]),
-        pltpu.make_async_copy(w_o, wo.at[pl.ds(0, local)], own_sem.at[1]),
-        pltpu.make_async_copy(w_u, wu.at[0], own_sem.at[2]),
-        pltpu.make_async_copy(w_d, wd.at[pl.ds(0, local)], own_sem.at[3]),
-    ]
-    for copy in own:
-        copy.start()
-
-    def spread(source):
-        for sequence in range(2):
-            for part in range(2):
-                target = 2 * sequence + part
-                piece = pl.ds(part * half, half)
-                src = source.at[sequence, piece]
-                dst = land.at[0, t, piece]
-
-                @pl.when(target == t)
-                def _():
-                    pltpu.make_async_copy(src, dst, xr_sem.at[t]).start()
-
-                @pl.when(target != t)
-                def _():
-                    remote(src, dst, xs_sem.at[target], xr_sem.at[t], (s, target, d)).start()
-
-    def gather_rows():
-        for b in range(blocks):
-            piece = land.at[0, b, mine]
-            remote(piece, piece, xs_sem.at[b], xr_sem.at[b], core).wait_recv()
-            remote(piece, piece, xfs_sem.at[b], xfr_sem.at[b], core).start()
-        for b in range(blocks):
-            piece = land.at[0, b, theirs]
-            remote(piece, piece, xfs_sem.at[b], xfr_sem.at[b], core).wait_recv()
-
+    shards = [w_q, w_k, w_v, w_o, w_u, w_d]
+
+    def place(i, slot, start, size):
+        if i < 3:
+            return win.at[slot, pl.ds(pl.multiple_of(i * local + start, 16), size)]
+        return (wo, wu, wd)[i - 3].at[pl.ds(pl.multiple_of(slot * local + start, 16), size)]
+
+    short = local // 2
     parity = lax.rem(d, 2)
-    step = width // 2 // PIECES
-    in_pieces = [
-        [pl.ds(pl.multiple_of(which * (width // 2) + i * step, step), step) for i in range(PIECES)]
-        for which in (parity, 1 - parity)
-    ]
-    wide = [pl.ds(pl.multiple_of(w * (width // 2), width // 2), width // 2) for w in (parity, 1 - parity)]
-    short = local // 2
-    tall = [pl.ds(pl.multiple_of(w * short, short), short) for w in (parity, 1 - parity)]
-    low = [pl.ds(pl.multiple_of(local + w * short, short), short) for w in (parity, 1 - parity)]
-
-    def pieces(which):
-        found = [(w_in.at[p], win.at[1, p]) for p in in_pieces[which]]
-        found.append((w_o.at[tall[which]], wo.at[low[which]]))
-        found.append((w_u.at[wide[which]], wu.at[1, wide[which]]))
-        found.append((w_d.at[tall[which]], wd.at[low[which]]))
-        return found
-
-    sent, relayed = pieces(0), pieces(1)
+
+    def own(i):
+        return pltpu.make_async_copy(shards[i], place(i, 0, 0, local), own_sem.at[i])
+
+    def crossing(i):
+        start = pl.multiple_of(parity * short, short)
+        dst = place(i, 1, start, short)
+        return remote(
+            shards[i].at[pl.ds(start, short)], dst, wys_sem.at[i], wyr_sem.at[i], across
+        )
+
+    def beside_copy(i, which):
+        piece = place(i, 1, pl.multiple_of(which * short, short), short)
+        return remote(piece, piece, wzs_sem.at[i], wzr_sem.at[i], beside)
+
+    def relay(i):
+        crossing(i).wait_recv()
+        beside_copy(i, parity).start()
+
+    def arrived(i):
+        beside_copy(i, 1 - parity).wait_recv()
+
+    step = rows // PIECES
+
+    def passing_copy(i):
+        piece = pl.ds(i * step, step)
+        return remote(
+            inputs.at[1 - y, piece], passing.at[piece], ps_sem.at[i], pr_sem.at[i], across
+        )
+
+    def onward(i):
+        piece = pl.ds(i * step, step)
+        return remote(
+            passing.at[piece], land.at[0, t_across, piece], ps_sem.at[PIECES + i], xp_sem.at[i], section
+        )
+
+    def over(i):
+        piece = pl.ds(i * step, step)
+        return remote(
+            cotangent.at[1 - y, piece], land.at[0, t, piece], xs_sem.at[i], xp_sem.at[i], across
+        )
+
+    def local_rows(source):
+        pltpu.make_async_copy(source.at[y], land.at[0, t], xr_sem.at[t]).start()
+        remote(source.at[y], land.at[0, t], xs_sem.at[PIECES], xr_sem.at[t], core).start()
+
+    def block_wait(b):
+        piece = land.at[0, b]
+        remote(piece, piece, xs_sem.at[PIECES], xr_sem.at[b], core).wait_recv()
+
+    def far_rows():
+        for i in range(PIECES):
+            piece = land.at[0, t_across, pl.ds(i * step, step)]
+            remote(piece, piece, xfs_sem, xp_sem.at[i], core).wait_recv()
+        piece = land.at[0, t_across]
+        remote(piece, piece, xfs_sem, xr_sem.at[t_across], core).start()
+        block_wait(t_diagonal)
+
+    def near_rows():
+        block_wait(t)
+        block_wait(t_core)
+
+    for i in range(3):
+        own(i).start()
 
     @pl.when(s == 0)
     def _():
-        spread(inputs)
-
-    for i, (src, dst) in enumerate(sent):
-        remote(src, dst, wys_sem.at[i], wyr_sem.at[i], across).start()
+        local_rows(inputs)
 
     @pl.when(s == 1)
     def _():
-        spread(cotangent)
-
-    def relay(i):
-        dst = sent[i][1]
-        remote(dst, dst, wys_sem.at[i], wyr_sem.at[i], across).wait_recv()
-        remote(dst, dst, wzs_sem.at[i], wzr_sem.at[i], beside).start()
-
-    def arrived(i):
-        dst = relayed[i][1]
-        remote(dst, dst, wzs_sem.at[i], wzr_sem.at[i], beside).wait_recv()
-
-    @pl.when(s == 0)
+        for i in range(PIECES):
+            passing_copy(i).start()
+
+    for i in range(6):
+        crossing(i).start()
+    for i in range(3, 6):
+        own(i).start()
+
+    @pl.when(s == 1)
     def _():
-        gather_rows()
-
-    for i in range(PIECES):
-        relay(i)
-    own[0].wait()
-    for i in range(PIECES):
-        arrived(i)
+        local_rows(cotangent)
+        for i in range(PIECES):
+            over(i).start()
+        for i in range(PIECES):
+            passing_copy(i).wait_recv()
+            onward(i).start()
+        for i in range(6):
+            relay(i)
+
+    for i in range(3):
+        own(i).wait()
 
     def save(kind, b, src, dst):
         pltpu.make_async_copy(src, dst, save_sem.at[kind, b]).start()
@@ -177,10 +197,32 @@
     )
     lane = lax.broadcasted_iota(jnp.int32, (rows, 128), 1)
 
-    def attention(b, _):
+    def attention(turn, _):
+        b = jnp.where(s == 0, lax.rem(turn, blocks), turn // 2)
+        j = jnp.where(s == 0, turn // blocks, lax.rem(turn, 2))
         at = pl.ds(pl.multiple_of(b * rows, rows), rows)
 
-        @pl.when(s == 1)
+        @pl.when((s == 0) & (turn == 0))
+        def _():
+            near_rows()
+
+        @pl.when((s == 0) & (turn == 2 * (1 - y)))
+        def _():
+            relay(0)
+            relay(1)
+            far_rows()
+
+        @pl.when((s == 0) & (turn == blocks))
+        def _():
+            for i in range(3):
+                arrived(i)
+
+        @pl.when((s == 1) & (turn == 0))
+        def _():
+            for i in range(3):
+                arrived(i)
+
+        @pl.when((s == 1) & (j == 0))
         def _():
             piece = land.at[1, b, mine]
             remote(piece, piece, ns_sem.at[b], nr_sem.at[b], core).wait_recv()
@@ -188,68 +230,68 @@
             rest = land.at[1, b, theirs]
             remote(rest, rest, nfs_sem.at[b], nfr_sem.at[b], core).wait_recv()
 
-        hidden = land[s, b].astype(F32)
-        normed = (hidden * inverse_rms(hidden) * gain_one[...]).astype(BF16)
-        n1[at] = normed
-        for j in range(2):
-            projected = plain(normed, win[j])
-            for i in range(per):
-                cut = slice(i * head, (i + 1) * head)
-                q[j * per + i, at] = (projected[:, cut] * scale[...]).astype(BF16)
-                k[j * per + i, at] = projected[:, local + i * head : local + (i + 1) * head].astype(
-                    BF16
-                )
-                v[j * per + i, at] = projected[
-                    :, 2 * local + i * head : 2 * local + (i + 1) * head
-                ].astype(BF16)
-        lse_cols[...] = jnp.zeros_like(lse_cols)
+        @pl.when(j == 0)
+        def _():
+            hidden = land[s, b].astype(F32)
+            n1[at] = (hidden * inverse_rms(hidden) * gain_one[...]).astype(BF16)
+            lse_cols[b] = jnp.zeros(lse_cols.shape[1:], F32)
+            save(0, b, land.at[s, b], h_out.at[b])
+            save(1, b, n1.at[at], n1_out.at[at])
+
+        projected = by_last(n1[at], win[j])
+        first = j * per
+        for i in range(per):
+            cut = i * head
+            q[first + i, at] = (projected[:, cut : cut + head] * scale[...]).astype(BF16)
+            cut += local
+            k[first + i, at] = projected[:, cut : cut + head].astype(BF16)
+            cut += local
+            v[first + i, at] = projected[:, cut : cut + head].astype(BF16)
         for bb in range(blocks):
 
             @pl.when(b == bb)
             def _():
-                def one(i, _):
-                    qh = q[i, bb * rows : (bb + 1) * rows]
-                    near = by_last(qh, k[i, bb * rows : (bb + 1) * rows])
+                for i in range(per):
+                    hd = first + i
+                    qh = q[hd, bb * rows : (bb + 1) * rows]
+                    near = by_last(qh, k[hd, bb * rows : (bb + 1) * rows])
                     near = jnp.where(causal, near, NEGATIVE)
                     top = jnp.max(near, axis=1, keepdims=True)
                     if bb:
-                        far = by_last(qh, k[i, : bb * rows])
+                        far = by_last(qh, k[hd, : bb * rows])
                         top = jnp.maximum(top, jnp.max(far, axis=1, keepdims=True))
                     near = jnp.exp(near - top)
                     total = jnp.sum(near, axis=1, keepdims=True)
-                    mixed = plain(near.astype(BF16), v[i, bb * rows : (bb + 1) * rows])
+                    mixed = plain(near.astype(BF16), v[hd, bb * rows : (bb + 1) * rows])
                     if bb:
                         far = jnp.exp(far - top)
                         total = total + jnp.sum(far, axis=1, keepdims=True)
-                        mixed = mixed + plain(far.astype(BF16), v[i, : bb * rows])
-                    o_heads[i] = (mixed / total).astype(BF16)
-                    lse_cols[...] = jnp.where(lane == i, top + jnp.log(total), lse_cols[...])
-                    return 0
-
-                lax.fori_loop(0, heads, one, 0, unroll=2)
-
-        o[at] = jnp.concatenate([o_heads[i] for i in range(heads)], axis=1)
-        lse[b] = jnp.transpose(lse_cols[...])[:heads]
-
-        save(0, b, land.at[s, b], h_out.at[b])
-        save(1, b, n1.at[at], n1_out.at[at])
-        save(2, b, q.at[:, at], q_out.at[:, at])
-        save(3, b, k.at[:, at], k_out.at[:, at])
-        save(4, b, v.at[:, at], v_out.at[:, at])
-        save(5, b, o.at[at], o_out.at[at])
-        save(6, b, lse.at[b], lse_out.at[b])
-        for i in range(3):
-
-            @pl.when(b == blocks - 3 + i)
+                        mixed = mixed + plain(far.astype(BF16), v[hd, : bb * rows])
+                    o_heads[hd, bb * rows : (bb + 1) * rows] = (mixed / total).astype(BF16)
+                    lse_cols[bb] = jnp.where(lane == hd, top + jnp.log(total), lse_cols[bb])
+
+        @pl.when(j == 1)
+        def _():
+            o[at] = jnp.concatenate([o_heads[i, at] for i in range(heads)], axis=1)
+            lse[b] = jnp.transpose(lse_cols[b])[:heads]
+            save(2, b, q.at[:, at], q_out.at[:, at])
+            save(3, b, k.at[:, at], k_out.at[:, at])
+            save(4, b, v.at[:, at], v_out.at[:, at])
+            save(5, b, o.at[at], o_out.at[at])
+            save(6, b, lse.at[b], lse_out.at[b])
+
+        for i, when in ((2, 2), (3, 4), (4, 5), (5, 7)):
+
+            @pl.when((s == 0) & (turn == when))
             def _():
-                relay(PIECES + i)
+                relay(i)
 
         return 0
 
-    lax.fori_loop(0, blocks, attention, 0)
-
-    own[1].wait()
-    arrived(PIECES)
+    lax.fori_loop(0, 2 * blocks, attention, 0)
+
+    own(3).wait()
+    arrived(3)
 
     def project(b, _):
         at = pl.ds(pl.multiple_of(b * rows, rows), rows)
@@ -259,10 +301,9 @@
 
     lax.fori_loop(0, blocks, project, 0)
 
-    own[2].wait()
-    arrived(PIECES + 1)
-    own[3].wait()
-    arrived(PIECES + 2)
+    for i in range(4, 6):
+        own(i).wait()
+        arrived(i)
     weights = [(win, win_out), (wo, wo_out), (wu, wu_out), (wd, wd_out)]
     for i, (src, dst) in enumerate(weights):
         save(11, i, src, dst)
@@ -274,7 +315,7 @@
         m[b] = middle
         normed = (middle * inverse_rms(middle) * gain_two[...]).astype(BF16)
         n2[at] = normed
-        up = jnp.concatenate([plain(normed, wu[0]), plain(normed, wu[1])], axis=1)
+        up = by_last(normed, wu[...])
         u[b] = up
         active = (up / (1.0 + jnp.exp(-up))).astype(BF16)
         a[at] = active
@@ -292,15 +333,15 @@
         def _():
             remote(xout.at[b], land.at[1, b, mine], ns_sem.at[b], nr_sem.at[b], section).start()
 
-        place = out_rows.at[y, mine]
+        spot = out_rows.at[y, mine]
 
         @pl.when(b == t)
         def _():
-            pltpu.make_async_copy(xout.at[b], place, or_sem.at[t]).start()
+            pltpu.make_async_copy(xout.at[b], spot, or_sem.at[t]).start()
 
         @pl.when(b != t)
         def _():
-            remote(xout.at[b], place, os_sem.at[b], or_sem.at[t], (s, b, d)).start()
+            remote(xout.at[b], spot, os_sem.at[b], or_sem.at[t], (s, b, d)).start()
 
         return 0
 
@@ -308,14 +349,25 @@
 
     @pl.when(s == 1)
     def _():
-        gather_rows()
+        near_rows()
+        far_rows()
 
     for b in range(blocks):
         pltpu.make_async_copy(land.at[0, b], g_out.at[b], save_sem.at[12, b]).start()
 
+    block = land.at[0, t]
+    remote(block, block, xs_sem.at[PIECES], xr_sem.at[t], core).wait_send()
+    remote(block, block, xfs_sem, xr_sem.at[t], core).wait_send()
+
+    @pl.when(s == 1)
+    def _():
+        for i in range(PIECES):
+            passing_copy(i).wait_send()
+            onward(i).wait_send()
+            over(i).wait_send()
+
     for b in range(blocks):
         piece = land.at[0, b, mine]
-        remote(piece, piece, xfs_sem.at[b], xfr_sem.at[b], core).wait_send()
         remote(ysend.at[b], yrecv.at[b], ys_sem.at[b], yr_sem.at[b], core).wait_send()
         remote(zpart.at[b, theirs], zrecv.at[b], zs_sem.at[b], zr_sem.at[b], core).wait_send()
         here = out_rows.at[b // 2, pl.ds((b % 2) * half, half)]
@@ -324,7 +376,6 @@
         @pl.when(b != t)
         def _():
             remote(xout.at[b], here, os_sem.at[b], or_sem.at[b], core).wait_send()
-            remote(piece, piece, xs_sem.at[b], xr_sem.at[b], core).wait_send()
 
         @pl.when(s == 0)
         def _():
@@ -334,9 +385,9 @@
         def _():
             remote(piece, piece, nfs_sem.at[b], nfr_sem.at[b], core).wait_send()
 
-    for i, (src, dst) in enumerate(sent):
-        remote(src, dst, wys_sem.at[i], wyr_sem.at[i], across).wait_send()
-        remote(dst, dst, wzs_sem.at[i], wzr_sem.at[i], beside).wait_send()
+    for i in range(6):
+        crossing(i).wait_send()
+        beside_copy(i, parity).wait_send()
     for i, (src, dst) in enumerate(weights):
         pltpu.make_async_copy(src, dst, save_sem.at[11, i]).wait()
     for b in range(blocks):
@@ -359,14 +410,15 @@
         pltpu.make_async_copy(land.at[0, b], g_out.at[b], save_sem.at[12, b]).wait()
 
 
-def forward(inputs, cotangent, w_in, w_o, w_u, w_d, gain_one, gain_two, scale, head):
+def forward(inputs, cotangent, shards, gain_one, gain_two, scale, head):
     _, rows, width = inputs.shape
-    local = w_o.shape[0]
+    local = shards[0].shape[0]
     heads = 2 * local // head
     blocks = lax.axis_size("tensor")
     length = blocks * rows
     half = rows // 2
     shape = jax.ShapeDtypeStruct
+    weights = [(2, 3 * local, width), (2 * local, width), (2 * local, width), (2 * local, width)]
     outs = [
         shape(inputs.shape, BF16),
         shape((blocks, rows, width), BF16),
@@ -381,24 +433,18 @@
         shape((blocks, rows, 2 * local), F32),
         shape((length, 2 * local), BF16),
         shape((blocks, rows, width), BF16),
-        shape((2, width, 3 * local), BF16),
-        shape((2 * local, width), BF16),
-        shape((2, width, local), BF16),
-        shape((2 * local, width), BF16),
-    ]
-    scratch = [
-        pltpu.VMEM((2, blocks, rows, width), BF16),
-        pltpu.VMEM((2, width, 3 * local), BF16),
-        pltpu.VMEM((2 * local, width), BF16),
-        pltpu.VMEM((2, width, local), BF16),
-        pltpu.VMEM((2 * local, width), BF16),
+    ] + [shape(w, BF16) for w in weights]
+    scratch = [pltpu.VMEM((2, blocks, rows, width), BF16)]
+    scratch += [pltpu.VMEM(w, BF16) for w in weights]
+    scratch += [
+        pltpu.VMEM((rows, width), BF16),
         pltpu.VMEM((length, width), BF16),
         pltpu.VMEM((heads, length, head), BF16),
         pltpu.VMEM((heads, length, head), BF16),
         pltpu.VMEM((heads, length, head), BF16),
-        pltpu.VMEM((heads, rows, head), BF16),
+        pltpu.VMEM((heads, length, head), BF16),
         pltpu.VMEM((length, 2 * local), BF16),
-        pltpu.VMEM((rows, 128), F32),
+        pltpu.VMEM((blocks, rows, 128), F32),
         pltpu.VMEM((blocks, heads, rows), F32),
         pltpu.VMEM((blocks, rows, width), BF16),
         pltpu.VMEM((blocks, rows, width), BF16),
@@ -409,38 +455,30 @@
         pltpu.VMEM((blocks, rows, width), F32),
         pltpu.VMEM((blocks, half, width), F32),
         pltpu.VMEM((blocks, half, width), BF16),
-        DMA((4,)),
+        DMA((6,)),
+        DMA((2 * PIECES,)),
+        DMA((PIECES,)),
+        DMA((PIECES + 1,)),
+        DMA((PIECES,)),
         DMA((blocks,)),
-        DMA((blocks,)),
-        DMA((blocks,)),
-        DMA((blocks,)),
-        DMA((PIECES + 3,)),
-        DMA((PIECES + 3,)),
-        DMA((PIECES + 3,)),
-        DMA((PIECES + 3,)),
-        DMA((blocks,)),
-        DMA((blocks,)),
-        DMA((blocks,)),
-        DMA((blocks,)),
-        DMA((blocks,)),
-        DMA((blocks,)),
-        DMA((blocks,)),
-        DMA((blocks,)),
-        DMA((blocks,)),
-        DMA((blocks,)),
-        DMA((13, blocks)),
+        DMA,
+        DMA((6,)),
+        DMA((6,)),
+        DMA((6,)),
+        DMA((6,)),
     ]
+    scratch += [DMA((blocks,))] * 10 + [DMA((13, blocks))]
     return pl.pallas_call(
         forward_kernel,
         out_shape=outs,
-        in_specs=[ANY] * 6 + [VMEM] * 3,
+        in_specs=[ANY] * 8 + [VMEM] * 3,
         out_specs=[ANY] * len(outs),
         scratch_shapes=scratch,
         compiler_params=pltpu.CompilerParams(
-            collective_id=1, has_side_effects=True, vmem_limit_bytes=60 * MIB
+            collective_id=1, has_side_effects=True, vmem_limit_bytes=62 * MIB
         ),
         name="forward",
-    )(inputs, cotangent, w_in, w_o, w_u, w_d, gain_one, gain_two, scale)
+    )(inputs, cotangent, *shards, gain_one, gain_two, scale)
 
 
 def backward_kernel(
@@ -448,14 +486,14 @@
     gain_one, gain_two, scale,
     out_rows, g_out, gu_out, gy_out, gp_out, dg1, dg2, ds,
     g, win, wo, wu, wd, h, q, k, v, o, lse, m, u, gu, gy, gp, ysend, yrecv, gm, go_heads, gq_heads,
-    cols, delta, dk, dv, n1part, n1recv, xout,
+    delta, dk, dv, n1part, n1recv, xout,
     load_sem, w_sem, ns_sem, nr_sem, nfs_sem, nfr_sem, ys_sem, yr_sem, zs_sem, zr_sem, os_sem, or_sem,
     save_sem,
 ):
     s, t, d = lax.axis_index("section"), lax.axis_index("tensor"), lax.axis_index("dp")
     blocks, rows, width = g.shape
     half = rows // 2
-    local = wu.shape[2]
+    local = wu.shape[0] // 2
     heads, _, head = q.shape
     per = heads // 2
     c, y = lax.rem(t, 2), t // 2
@@ -468,9 +506,12 @@
 
     weights = [(wd_in, wd), (wu_in, wu), (wo_in, wo), (win_in, win)]
 
-    def loads(b):
-        at = pl.ds(b * rows, rows)
-        return [
+    def weight(i):
+        return pltpu.make_async_copy(*weights[i], w_sem.at[i])
+
+    def load(kind, b):
+        at = pl.ds(pl.multiple_of(b * rows, rows), rows)
+        src, dst = [
             (u_in.at[b], u.at[b]),
             (m_in.at[b], m.at[b]),
             (o_in.at[at], o.at[at]),
@@ -479,24 +520,38 @@
             (v_in.at[:, at], v.at[:, at]),
             (lse_in.at[b], lse.at[b]),
             (h_in.at[b, mine], h.at[b]),
-        ]
-
-    for i, (src, dst) in enumerate(weights[:2]):
-        pltpu.make_async_copy(src, dst, w_sem.at[i]).start()
-    for kind, (src, dst) in enumerate(loads(blocks - 1)[:2]):
-        pltpu.make_async_copy(src, dst, load_sem.at[kind, blocks - 1]).start()
+        ][kind]
+        return pltpu.make_async_copy(src, dst, load_sem.at[kind, b])
+
+    def incoming(b):
+        return pltpu.make_async_copy(g_in.at[b], g.at[b], nr_sem.at[b])
+
+    last = blocks - 1
 
     @pl.when(s == 1)
     def _():
-        for b in reversed(range(blocks)):
-            pltpu.make_async_copy(g_in.at[b], g.at[b], nr_sem.at[b]).start()
-
-    for i, (src, dst) in enumerate(weights[2:]):
-        pltpu.make_async_copy(src, dst, w_sem.at[2 + i]).start()
-    for b in reversed(range(blocks)):
-        for kind, (src, dst) in enumerate(loads(b)):
-            if kind >= 2 or b < blocks - 1:
-                pltpu.make_async_copy(src, dst, load_sem.at[kind, b]).start()
+        incoming(last).start()
+
+    weight(0).start()
+    load(0, last).start()
+    weight(1).start()
+    load(1, last).start()
+    weight(2).start()
+    for kind in range(2, 7):
+        load(kind, last).start()
+    for b in reversed(range(last)):
+        load(4, b).start()
+        load(5, b).start()
+    weight(3).start()
+    load(7, last).start()
+    for b in reversed(range(last)):
+        for kind in (0, 1, 2, 3, 6, 7):
+            load(kind, b).start()
+
+    @pl.when(s == 1)
+    def _():
+        for b in reversed(range(last)):
+            incoming(b).start()
 
     greet([core, across, diagonal, section])
 
@@ -505,28 +560,22 @@
     dg1[...] = jnp.zeros_like(dg1)
     dg2[...] = jnp.zeros_like(dg2)
     ds[...] = jnp.zeros_like(ds)
-    for i, (src, dst) in enumerate(weights):
-        pltpu.make_async_copy(src, dst, w_sem.at[i]).wait()
-    for b in range(blocks):
-        for kind, (src, dst) in enumerate(loads(b)):
-            if b != blocks - 1 or kind < 2:
-                pass
-            pltpu.make_async_copy(src, dst, load_sem.at[kind, b]).wait()
 
     causal = lax.broadcasted_iota(jnp.int32, (rows, rows), 0) <= lax.broadcasted_iota(
         jnp.int32, (rows, rows), 1
     )
+    lane = lax.broadcasted_iota(jnp.int32, (rows, 128), 1)
 
     def save(kind, b, src, dst):
         pltpu.make_async_copy(src, dst, save_sem.at[kind, b]).start()
 
     def one_block(turn, _):
-        b = blocks - 1 - turn
+        b = last - turn
         at = pl.ds(pl.multiple_of(b * rows, rows), rows)
 
         @pl.when(s == 1)
         def _():
-            pltpu.make_async_copy(g_in.at[b], g.at[b], nr_sem.at[b]).wait()
+            incoming(b).wait()
 
         @pl.when(s == 0)
         def _():
@@ -536,6 +585,12 @@
             rest = g.at[b, theirs]
             remote(rest, rest, nfs_sem.at[b], nfr_sem.at[b], core).wait_recv()
 
+        @pl.when(turn == 0)
+        def _():
+            weight(0).wait()
+            weight(1).wait()
+
+        load(0, b).wait()
         save(0, b, g.at[b], g_out.at[at])
         grad = g[b]
         grad_act = by_last(grad, wd[...])
@@ -544,11 +599,21 @@
         grad_up = (grad_act * sigma * (1.0 + up * (1.0 - sigma))).astype(BF16)
         gu[at] = grad_up
         save(1, b, gu.at[at], gu_out.at[at])
-        ysend[b] = (by_last(grad_up[:, :local], wu[0]) + by_last(grad_up[:, local:], wu[1])).astype(
-            BF16
-        )
+        ysend[b] = plain(grad_up, wu[...]).astype(BF16)
         copy = remote(ysend.at[b], yrecv.at[b], ys_sem.at[b], yr_sem.at[b], core)
         copy.start()
+        load(1, b).wait()
+
+        @pl.when(turn == 0)
+        def _():
+            weight(2).wait()
+            weight(3).wait()
+            for bb in range(blocks):
+                load(4, bb).wait()
+                load(5, bb).wait()
+
+        for kind in (2, 3, 6, 7):
+            load(kind, b).wait()
         copy.wait_recv()
         grad_normed = ysend[b].astype(F32) + yrecv[b].astype(F32)
         middle = m[b]
@@ -565,7 +630,6 @@
         save(2, b, gy.at[at], gy_out.at[at])
         grad_mixed = by_last(grad_mid, wo[...]).astype(BF16)
         both = grad_mixed.astype(F32) * o[at].astype(F32)
-        lane = lax.broadcasted_iota(jnp.int32, (rows, 128), 1)
         found = jnp.zeros((rows, 128), F32)
         for i in range(heads):
             cut = slice(i * head, (i + 1) * head)
@@ -576,27 +640,31 @@
 
             @pl.when(b == bb)
             def _():
-                def one(i, _):
-                    qh = q[i, bb * rows : (bb + 1) * rows]
-                    gh = go_heads[i]
-                    offset = lse[bb, pl.ds(i, 1)]
-                    inner = delta[pl.ds(i, 1)]
-                    total = jnp.zeros((head, rows), F32)
-                    for j in range(bb + 1):
-                        cut = slice(j * rows, (j + 1) * rows)
-                        kj = k[i, cut]
-                        weight = jnp.exp(by_last(kj, qh) - offset)
-                        if j == bb:
-                            weight = jnp.where(causal, weight, 0.0)
-                        grad_score = weight * (by_last(v[i, cut], gh) - inner)
-                        grad_score = grad_score.astype(BF16)
-                        dv[i, cut] += plain(weight.astype(BF16), gh)
-                        dk[i, cut] += plain(grad_score, qh)
-                        total = total + by_first(kj, grad_score)
-                    gq_heads[i] = jnp.transpose(total)
+                def group(first, _):
+                    for j in range(per):
+                        i = first * per + j
+                        qh = q[i, bb * rows : (bb + 1) * rows]
+                        gh = go_heads[i]
+                        offset = lse[bb, pl.ds(i, 1)]
+                        inner = delta[pl.ds(i, 1)]
+                        total = None
+                        for lo, hi in ((bb * rows, (bb + 1) * rows), (0, bb * rows)):
+                            if lo == hi:
+                                continue
+                            kj = k[i, lo:hi]
+                            weight = jnp.exp(by_last(kj, qh) - offset)
+                            if lo == bb * rows and hi > lo and hi == (bb + 1) * rows:
+                                weight = jnp.where(causal, weight, 0.0)
+                            grad_score = weight * (by_last(v[i, lo:hi], gh) - inner)
+                            grad_score = grad_score.astype(BF16)
+                            dv[i, lo:hi] += plain(weight.astype(BF16), gh)
+                            dk[i, lo:hi] += plain(grad_score, qh)
+                            part = by_first(kj, grad_score)
+                            total = part if total is None else total + part
+                        gq_heads[i] = jnp.transpose(total)
                     return 0
 
-                lax.fori_loop(0, heads, one, 0)
+                lax.fori_loop(0, 2, group, 0)
 
         for j in range(2):
             mine_heads = range(j * per, (j + 1) * per)
@@ -610,14 +678,14 @@
             ]
             gp[j, at] = jnp.concatenate(grads, axis=1)
         save(3, b, gp.at[:, at], gp_out.at[:, at])
-        n1part[...] = by_last(gp[0, at], win[0]) + by_last(gp[1, at], win[1])
+        n1part[...] = plain(gp[0, at], win[0]) + plain(gp[1, at], win[1])
         copy = remote(n1part.at[theirs], n1recv.at[b], zs_sem.at[b], zr_sem.at[b], core)
         copy.start()
-        copy.wait_recv()
-        grad_normed = n1part[mine] + n1recv[b]
         hidden = h[b].astype(F32)
         inverse = inverse_rms(hidden)
         unit = hidden * inverse
+        copy.wait_recv()
+        grad_normed = n1part[mine] + n1recv[b]
         grad_unit = grad_normed * gain_one[...]
         dg1[...] += jnp.sum(grad_normed * unit, axis=0, keepdims=True)
         xout[b] = (
@@ -629,15 +697,15 @@
         def _():
             remote(xout.at[b], g.at[b, mine], ns_sem.at[b], nr_sem.at[b], section).start()
 
-        place = out_rows.at[y, mine]
+        spot = out_rows.at[y, mine]
 
         @pl.when(b == t)
         def _():
-            pltpu.make_async_copy(xout.at[b], place, or_sem.at[t]).start()
+            pltpu.make_async_copy(xout.at[b], spot, or_sem.at[t]).start()
 
         @pl.when(b != t)
         def _():
-            remote(xout.at[b], place, os_sem.at[b], or_sem.at[t], (s, b, d)).start()
+            remote(xout.at[b], spot, os_sem.at[b], or_sem.at[t], (s, b, d)).start()
 
         copy.wait_send()
         return 0
@@ -678,7 +746,7 @@
     win_in, wo_in, wu_in, wd_in = saved[9:]
     blocks, rows, width = g_in.shape
     heads, length, head = q_in.shape
-    local = wu_in.shape[2]
+    local = wu_in.shape[0] // 2
     half = rows // 2
     shape = jax.ShapeDtypeStruct
     outs = [
@@ -713,7 +781,6 @@
         pltpu.VMEM((rows, width), F32),
         pltpu.VMEM((heads, rows, head), BF16),
         pltpu.VMEM((heads, rows, head), F32),
-        pltpu.VMEM((8, 128), F32),
         pltpu.VMEM((heads, rows), F32),
         pltpu.VMEM((heads, length, head), F32),
         pltpu.VMEM((heads, length, head), F32),
@@ -722,18 +789,8 @@
         pltpu.VMEM((blocks, half, width), BF16),
         DMA((8, blocks)),
         DMA((4,)),
-        DMA((blocks,)),
-        DMA((blocks,)),
-        DMA((blocks,)),
-        DMA((blocks,)),
-        DMA((blocks,)),
-        DMA((blocks,)),
-        DMA((blocks,)),
-        DMA((blocks,)),
-        DMA((blocks,)),
-        DMA((blocks,)),
-        DMA((4, blocks)),
     ]
+    scratch += [DMA((blocks,))] * 10 + [DMA((4, blocks))]
     return pl.pallas_call(
         backward_kernel,
         out_shape=outs,
@@ -1099,11 +1156,11 @@
     local = w_query.shape[2]
     head = dim_scale.shape[1]
     width = inputs.shape[2]
-    w_in = jnp.concatenate([w_query[0], w_key[0], w_value[0]], axis=1)
+    shards = (w_query[0].T, w_key[0].T, w_value[0].T, w_out[0], w_up[0].T, w_down[0])
     multiplier = LOG2E / math.sqrt(head)
     per_dim = multiplier * jax.nn.softplus(dim_scale)
     done = forward(
-        inputs, cotangent, w_in, w_out[0], w_up[0], w_down[0], gain_attn, gain_mlp, per_dim, head
+        inputs, cotangent, shards, gain_attn, gain_mlp, per_dim, head
     )
     layer_out, h, n1, q, k, v, o, lse, m, n2, u, a, g, win, wo, wu, wd = done
     input_grads, g_all, gu, gy, gp, dg1, dg2, ds = backward(

time: 444 us -> 386 us (0.87)
  Pallas kernels: 418 us -> 368 us
  local copies, waits for them, and re-layouts: 16.7 us -> 9.76 us
    pallas_call x1, Pallas kernels: 176 us -> 150 us  [backward(): pl.pallas_call(backward_kernel, out_shape=outs, in_specs=[ANY] * 13 + [VM...]
    pallas_call x1, Pallas kernels: 124 us -> 101 us  [forward(): pl.pallas_call(forward_kernel, out_shape=outs, in_specs=[ANY] * 8 + [VMEM...]
    unnamed x16 -> x12, local copies, waits for them, and re-layouts: 11 us -> 4.12 us
where the time goes in v3:
time: 386 us; the launch traced here: 383 us
  Pallas kernels  368 us (95%)
  local copies, waits for them, and re-layouts  9.76 us (3%)
    pallas_call x1, Pallas kernels, backward(): pl.pallas_call(backward_kernel, out_shape=outs, in_specs=[ANY] * 13 + [VM...  150 us
    pallas_call x1, Pallas kernels, gradients(): pl.pallas_call(gradient_kernel, out_shape=[jax.ShapeDtypeStruct((chunk, 6...  117 us
    pallas_call x1, Pallas kernels, forward(): pl.pallas_call(forward_kernel, out_shape=outs, in_specs=[ANY] * 8 + [VMEM...  101 us

profile of v3, /device:TPU:0, one launch (start us, length us, event | category | flops | bytes accessed | tf_op | source)
XLA Modules:
  0.0 382.7 jit_solution(17887652992422620155)
XLA Ops:
  0.6 1.2 fusion.scale
  1.8 0.0 copy-start.3
  1.8 101.5 %forward.1 = (bf16[2,256,1280]{2,1,0:T(8,128)(2,1)}, bf16[4,256,1280]{2,1,0:T(8,128)(2,1)}, bf16[1024,1280]{1,0:T(8,128)(2,1)}, bf16[8,1024,80]{2,1,0:T(8,128)(2...) custom-call(bf16[2,256,1280]{2,1,0:T(8,128)(2,1)} %inputs.1, ...), custom_call_target="tpu_custom_call" | custom-call | tf_op jit(solution)/shard_map/forward/pallas_call | solution.py:471
  103.3 0.0 copy-done.3
  103.3 0.6 tile.13.scale
  104.0 150.0 %backward.1 = (bf16[2,256,1280]{2,1,0:T(8,128)(2,1)}, bf16[1024,1280]{1,0:T(8,128)(2,1)}, bf16[1024,640]{1,0:T(8,128)(2,1)}, bf16[1024,1280]{1,0:T(8,128)(2,1)},...) custom-call(bf16[4,256,1280]{2,1,0:T(8,128)(2,1)} %get-tuple-element.39.g_in, ...), custom_call_target="tpu_custom_call" | custom-call | tf_op jit(solution)/shard_map/backward/pallas_call | solution.py:794
  254.0 0.7 broadcast_select_fusion
  254.7 0.8 reshape.34
  255.4 1.3 pad_maximum_fusion.small
  256.7 117.0 %gradients.1 = (f32[320,1920]{1,0:T(8,128)}, f32[1,3200]{1,0:T(1,128)}) custom-call(bf16[1024,1280]{1,0:T(8,128)(2,1)} %get-tuple-element.53.n1_in, bf16[1024,1280]{1,0:T(8,128)(2,1)} %get-tuple-element.54.n2_in, bf16[1024,1280]{1,0:T(8,128)(2,1)} %get-tuple-element.55.gy_in, bf16[1024,1280]{1,0:T(8,128)(2,1)} %get-tuple-element.56.g_in, ...), custom_call_target="tpu_custom_call" | custom-call | tf_op jit(solution)/shard_map/gradients/pallas_call | solution.py:1098
  373.8 0.0 copy-start.2
  373.8 3.5 slice_bitcast_fusion
  377.3 0.0 copy-start
  377.3 1.0 copy.22
  378.3 1.0 copy.23
  379.3 0.0 copy-done.2
  379.3 0.6 fusion.1
  379.9 0.1 reshape.35
  380.0 0.0 copy-start.1
  380.0 0.5 divide_multiply_fusion
  380.6 0.0 copy-done
  380.6 1.1 copy.26
  381.6 0.0 copy-done.1
  381.6 1.1 copy.27
  (4 shorter events, 0.1 us)
Async XLA Ops:
  1.8 101.5 %copy-start.3 = (f32[1,80]{1,0:T(1,128)S(1)}, f32[1,80]{1,0:T(1,128)}, u32[]{:S(2)}) copy-start(f32[1,80]{1,0:T(1,128)} %param.18) | copy-start | bytes 964
  373.8 5.5 %copy-start.2 = (f32[1,3200]{1,0:T(1,128)S(1)}, f32[1,3200]{1,0:T(1,128)}, u32[]{:S(2)}) copy-start(f32[1,3200]{1,0:T(1,128)} %get-tuple-element.63) | copy-start | bytes 38404
  377.3 3.3 copy-start
  380.0 1.6 copy-start.1

commit v4 on v3

--- a/solution.py
+++ b/solution.py
@@ -55,18 +55,24 @@
     pl.semaphore_wait(barrier, len(devices))
 
 
+def per_dim(raw):
+    grown = jnp.maximum(raw, 0.0) + jnp.log(1.0 + jnp.exp(-jnp.abs(raw)))
+    return (LOG2E / math.sqrt(raw.shape[1])) * grown
+
+
 def inverse_rms(rows):
     return lax.rsqrt(jnp.mean(rows * rows, axis=1, keepdims=True) + EPS)
 
 
 def forward_kernel(
     inputs, cotangent, w_q, w_k, w_v, w_o, w_u, w_d, gain_one, gain_two, scale,
-    out_rows, h_out, n1_out, q_out, k_out, v_out, o_out, lse_out, m_out, n2_out, u_out, a_out,
+    x_out, h_out, n1_out, q_out, k_out, v_out, o_out, lse_out, m_out, n2_out, u_out, a_out,
     g_out, win_out, wo_out, wu_out, wd_out,
-    land, win, wo, wu, wd, passing, n1, q, k, v, o_heads, o, lse_cols, lse, ysend, yrecv, m, n2, u, a,
-    zpart, zrecv, xout,
+    land, win, wo, wu, wd, passing, down_a, down_b, n1, q, k, v, o_heads, o, lse_cols, lse, ysend, yrecv,
+    m, n2, u, a, zpart, zrecv, xout,
     own_sem, ps_sem, pr_sem, xs_sem, xp_sem, xr_sem, xfs_sem, wys_sem, wyr_sem, wzs_sem, wzr_sem,
-    ns_sem, nr_sem, nfs_sem, nfr_sem, ys_sem, yr_sem, zs_sem, zr_sem, os_sem, or_sem, save_sem,
+    das_sem, dar_sem, dbs_sem, dbr_sem, dcs_sem, dcr_sem,
+    ns_sem, nr_sem, nfs_sem, nfr_sem, ys_sem, yr_sem, zs_sem, zr_sem, save_sem,
 ):
     s, t, d = lax.axis_index("section"), lax.axis_index("tensor"), lax.axis_index("dp")
     blocks, rows, width = land.shape[1:]
@@ -94,21 +100,24 @@
             return win.at[slot, pl.ds(pl.multiple_of(i * local + start, 16), size)]
         return (wo, wu, wd)[i - 3].at[pl.ds(pl.multiple_of(slot * local + start, 16), size)]
 
-    short = local // 2
+    short = local // 4
     parity = lax.rem(d, 2)
 
     def own(i):
         return pltpu.make_async_copy(shards[i], place(i, 0, 0, local), own_sem.at[i])
 
+    def strip(i, which):
+        return pl.multiple_of(which * 2 * short + i % 2 * short, 16)
+
     def crossing(i):
-        start = pl.multiple_of(parity * short, short)
-        dst = place(i, 1, start, short)
+        start = strip(i, parity)
+        dst = place(i // 2, 1, start, short)
         return remote(
-            shards[i].at[pl.ds(start, short)], dst, wys_sem.at[i], wyr_sem.at[i], across
+            shards[i // 2].at[pl.ds(start, short)], dst, wys_sem.at[i], wyr_sem.at[i], across
         )
 
     def beside_copy(i, which):
-        piece = place(i, 1, pl.multiple_of(which * short, short), short)
+        piece = place(i // 2, 1, strip(i, which), short)
         return remote(piece, piece, wzs_sem.at[i], wzr_sem.at[i], beside)
 
     def relay(i):
@@ -117,6 +126,27 @@
 
     def arrived(i):
         beside_copy(i, 1 - parity).wait_recv()
+
+    quarter = local // PIECES
+
+    def down_piece(buffer, i):
+        return buffer.at[pl.ds(i * quarter, quarter)]
+
+    def down_first(i):
+        return remote(
+            down_piece(w_d, i), down_piece(down_a, i), das_sem.at[i], dar_sem.at[i], section
+        )
+
+    def down_second(i):
+        return remote(
+            down_piece(down_a, i), down_piece(down_b, i), dbs_sem.at[i], dbr_sem.at[i], across
+        )
+
+    def down_third(i):
+        return remote(
+            down_piece(down_b, i), wd.at[pl.ds(local + i * quarter, quarter)],
+            dcs_sem.at[i], dcr_sem.at[i], section,
+        )
 
     step = rows // PIECES
 
@@ -163,26 +193,35 @@
 
     @pl.when(s == 0)
     def _():
+        for i in range(10):
+            crossing(i).start()
         local_rows(inputs)
+        for i in range(PIECES):
+            down_first(i).start()
 
     @pl.when(s == 1)
     def _():
         for i in range(PIECES):
             passing_copy(i).start()
-
-    for i in range(6):
-        crossing(i).start()
+        local_rows(cotangent)
+
     for i in range(3, 6):
         own(i).start()
 
     @pl.when(s == 1)
     def _():
-        local_rows(cotangent)
+        for i in range(PIECES):
+            passing_copy(i).wait_recv()
+            onward(i).start()
+            down_first(i).wait_recv()
+            down_second(i).start()
+        for i in range(12):
+            crossing(i).start()
         for i in range(PIECES):
             over(i).start()
         for i in range(PIECES):
-            passing_copy(i).wait_recv()
-            onward(i).start()
+            down_second(i).wait_recv()
+            down_third(i).start()
         for i in range(6):
             relay(i)
 
@@ -197,6 +236,8 @@
     )
     lane = lax.broadcasted_iota(jnp.int32, (rows, 128), 1)
 
+    factor = per_dim(scale[...])
+
     def attention(turn, _):
         b = jnp.where(s == 0, lax.rem(turn, blocks), turn // 2)
         j = jnp.where(s == 0, turn // blocks, lax.rem(turn, 2))
@@ -208,18 +249,20 @@
 
         @pl.when((s == 0) & (turn == 2 * (1 - y)))
         def _():
-            relay(0)
-            relay(1)
+            for i in range(4):
+                relay(i)
             far_rows()
 
         @pl.when((s == 0) & (turn == blocks))
         def _():
-            for i in range(3):
+            relay(6)
+            relay(7)
+            for i in range(6):
                 arrived(i)
 
         @pl.when((s == 1) & (turn == 0))
         def _():
-            for i in range(3):
+            for i in range(6):
                 arrived(i)
 
         @pl.when((s == 1) & (j == 0))
@@ -242,7 +285,7 @@
         first = j * per
         for i in range(per):
             cut = i * head
-            q[first + i, at] = (projected[:, cut : cut + head] * scale[...]).astype(BF16)
+            q[first + i, at] = (projected[:, cut : cut + head] * factor).astype(BF16)
             cut += local
             k[first + i, at] = projected[:, cut : cut + head].astype(BF16)
             cut += local
@@ -280,18 +323,25 @@
             save(5, b, o.at[at], o_out.at[at])
             save(6, b, lse.at[b], lse_out.at[b])
 
-        for i, when in ((2, 2), (3, 4), (4, 5), (5, 7)):
+        for i, when in ((4, 2), (5, 3), (8, 4), (9, 5)):
 
             @pl.when((s == 0) & (turn == when))
             def _():
                 relay(i)
 
+        for i in range(6):
+
+            @pl.when((s == 1) & (turn == i))
+            def _():
+                relay(6 + i)
+
         return 0
 
     lax.fori_loop(0, 2 * blocks, attention, 0)
 
     own(3).wait()
-    arrived(3)
+    arrived(6)
+    arrived(7)
 
     def project(b, _):
         at = pl.ds(pl.multiple_of(b * rows, rows), rows)
@@ -301,9 +351,21 @@
 
     lax.fori_loop(0, blocks, project, 0)
 
-    for i in range(4, 6):
-        own(i).wait()
-        arrived(i)
+    own(4).wait()
+    own(5).wait()
+    arrived(8)
+    arrived(9)
+
+    @pl.when(s == 0)
+    def _():
+        for i in range(PIECES):
+            down_third(i).wait_recv()
+
+    @pl.when(s == 1)
+    def _():
+        arrived(10)
+        arrived(11)
+
     weights = [(win, win_out), (wo, wo_out), (wu, wu_out), (wd, wd_out)]
     for i, (src, dst) in enumerate(weights):
         save(11, i, src, dst)
@@ -333,16 +395,7 @@
         def _():
             remote(xout.at[b], land.at[1, b, mine], ns_sem.at[b], nr_sem.at[b], section).start()
 
-        spot = out_rows.at[y, mine]
-
-        @pl.when(b == t)
-        def _():
-            pltpu.make_async_copy(xout.at[b], spot, or_sem.at[t]).start()
-
-        @pl.when(b != t)
-        def _():
-            remote(xout.at[b], spot, os_sem.at[b], or_sem.at[t], (s, b, d)).start()
-
+        save(13, b, xout.at[b], x_out.at[b])
         return 0
 
     lax.fori_loop(0, blocks, feed, 0)
@@ -365,17 +418,21 @@
             passing_copy(i).wait_send()
             onward(i).wait_send()
             over(i).wait_send()
+            down_second(i).wait_send()
+            down_third(i).wait_send()
+        for i in range(10, 12):
+            crossing(i).wait_send()
+            beside_copy(i, parity).wait_send()
+
+    @pl.when(s == 0)
+    def _():
+        for i in range(PIECES):
+            down_first(i).wait_send()
 
     for b in range(blocks):
         piece = land.at[0, b, mine]
         remote(ysend.at[b], yrecv.at[b], ys_sem.at[b], yr_sem.at[b], core).wait_send()
         remote(zpart.at[b, theirs], zrecv.at[b], zs_sem.at[b], zr_sem.at[b], core).wait_send()
-        here = out_rows.at[b // 2, pl.ds((b % 2) * half, half)]
-        remote(here, here, os_sem.at[b], or_sem.at[b], core).wait_recv()
-
-        @pl.when(b != t)
-        def _():
-            remote(xout.at[b], here, os_sem.at[b], or_sem.at[b], core).wait_send()
 
         @pl.when(s == 0)
         def _():
@@ -385,7 +442,7 @@
         def _():
             remote(piece, piece, nfs_sem.at[b], nfr_sem.at[b], core).wait_send()
 
-    for i in range(6):
+    for i in range(10):
         crossing(i).wait_send()
         beside_copy(i, parity).wait_send()
     for i, (src, dst) in enumerate(weights):
@@ -408,6 +465,7 @@
         for kind, (src, dst) in enumerate(saved):
             pltpu.make_async_copy(src, dst, save_sem.at[kind, b]).wait()
         pltpu.make_async_copy(land.at[0, b], g_out.at[b], save_sem.at[12, b]).wait()
+        pltpu.make_async_copy(xout.at[b], x_out.at[b], save_sem.at[13, b]).wait()
 
 
 def forward(inputs, cotangent, shards, gain_one, gain_two, scale, head):
@@ -420,7 +478,7 @@
     shape = jax.ShapeDtypeStruct
     weights = [(2, 3 * local, width), (2 * local, width), (2 * local, width), (2 * local, width)]
     outs = [
-        shape(inputs.shape, BF16),
+        shape((blocks, half, width), BF16),
         shape((blocks, rows, width), BF16),
         shape((length, width), BF16),
         shape((heads, length, head), BF16),
@@ -438,6 +496,8 @@
     scratch += [pltpu.VMEM(w, BF16) for w in weights]
     scratch += [
         pltpu.VMEM((rows, width), BF16),
+        pltpu.VMEM((local, width), BF16),
+        pltpu.VMEM((local, width), BF16),
         pltpu.VMEM((length, width), BF16),
         pltpu.VMEM((heads, length, head), BF16),
         pltpu.VMEM((heads, length, head), BF16),
@@ -462,12 +522,8 @@
         DMA((PIECES,)),
         DMA((blocks,)),
         DMA,
-        DMA((6,)),
-        DMA((6,)),
-        DMA((6,)),
-        DMA((6,)),
     ]
-    scratch += [DMA((blocks,))] * 10 + [DMA((13, blocks))]
+    scratch += [DMA((12,))] * 4 + [DMA((PIECES,))] * 6 + [DMA((blocks,))] * 8 + [DMA((14, blocks))]
     return pl.pallas_call(
         forward_kernel,
         out_shape=outs,
@@ -482,13 +538,13 @@
 
 
 def backward_kernel(
-    g_in, h_in, q_in, k_in, v_in, o_in, lse_in, m_in, u_in, win_in, wo_in, wu_in, wd_in,
+    g_in, h_in, q_in, k_in, v_in, o_in, lse_in, m_in, u_in, win_in, wo_in, wu_in, wd_in, x_in,
     gain_one, gain_two, scale,
-    out_rows, g_out, gu_out, gy_out, gp_out, dg1, dg2, ds,
+    x_rows, out_rows, final, g_out, gu_out, gy_out, gp_out, dg1, dg2, ds,
     g, win, wo, wu, wd, h, q, k, v, o, lse, m, u, gu, gy, gp, ysend, yrecv, gm, go_heads, gq_heads,
     delta, dk, dv, n1part, n1recv, xout,
     load_sem, w_sem, ns_sem, nr_sem, nfs_sem, nfr_sem, ys_sem, yr_sem, zs_sem, zr_sem, os_sem, or_sem,
-    save_sem,
+    xs_sem, xr_sem, save_sem,
 ):
     s, t, d = lax.axis_index("section"), lax.axis_index("tensor"), lax.axis_index("dp")
     blocks, rows, width = g.shape
@@ -536,24 +592,22 @@
     load(0, last).start()
     weight(1).start()
     load(1, last).start()
-    weight(2).start()
-    for kind in range(2, 7):
-        load(kind, last).start()
-    for b in reversed(range(last)):
-        load(4, b).start()
-        load(5, b).start()
-    weight(3).start()
-    load(7, last).start()
-    for b in reversed(range(last)):
-        for kind in (0, 1, 2, 3, 6, 7):
-            load(kind, b).start()
-
-    @pl.when(s == 1)
-    def _():
-        for b in reversed(range(last)):
-            incoming(b).start()
 
     greet([core, across, diagonal, section])
+
+    spot = out_rows.at[y, mine]
+
+    def owner_copy(b, src, dst, send, receive, act):
+        @pl.when(b == t)
+        def _():
+            act(pltpu.make_async_copy(src, dst, receive.at[t]))
+
+        @pl.when(b != t)
+        def _():
+            act(remote(src, dst, send.at[b], receive.at[t], (s, b, d)))
+
+    for b in range(blocks):
+        owner_copy(b, x_in.at[b], x_rows.at[y, mine], xs_sem, xr_sem, lambda copy: copy.start())
 
     dk[...] = jnp.zeros_like(dk)
     dv[...] = jnp.zeros_like(dv)
@@ -564,12 +618,20 @@
     causal = lax.broadcasted_iota(jnp.int32, (rows, rows), 0) <= lax.broadcasted_iota(
         jnp.int32, (rows, rows), 1
     )
-    lane = lax.broadcasted_iota(jnp.int32, (rows, 128), 1)
+    factor = jnp.concatenate([per_dim(scale[...])] * per, axis=1)
+    width_two = heads * head
+    row_head = lax.broadcasted_iota(jnp.int32, (heads, width_two), 0)
+    start = row_head * head
+    place = lax.broadcasted_iota(jnp.int32, (heads, width_two), 1)
+    member = jnp.where((place >= start) & (place < start + head), 1.0, 0.0)
 
     def save(kind, b, src, dst):
         pltpu.make_async_copy(src, dst, save_sem.at[kind, b]).start()
 
-    def one_block(turn, _):
+    def neighbours_sum(b):
+        return remote(ysend.at[b], yrecv.at[b], ys_sem.at[b], yr_sem.at[b], core)
+
+    def up_part(turn):
         b = last - turn
         at = pl.ds(pl.multiple_of(b * rows, rows), rows)
 
@@ -588,7 +650,6 @@
         @pl.when(turn == 0)
         def _():
             weight(0).wait()
-            weight(1).wait()
 
         load(0, b).wait()
         save(0, b, g.at[b], g_out.at[at])
@@ -598,23 +659,27 @@
         sigma = 1.0 / (1.0 + jnp.exp(-up))
         grad_up = (grad_act * sigma * (1.0 + up * (1.0 - sigma))).astype(BF16)
         gu[at] = grad_up
+
+        @pl.when(turn == 0)
+        def _():
+            weight(1).wait()
+            weight(2).start()
+            for kind in (2, 3, 6):
+                load(kind, last).start()
+            for bb in reversed(range(blocks)):
+                load(4, bb).start()
+                load(5, bb).start()
+
         save(1, b, gu.at[at], gu_out.at[at])
         ysend[b] = plain(grad_up, wu[...]).astype(BF16)
-        copy = remote(ysend.at[b], yrecv.at[b], ys_sem.at[b], yr_sem.at[b], core)
-        copy.start()
+        neighbours_sum(b).start()
+
+    def one_block(turn, _):
+        b = last - turn
+        at = pl.ds(pl.multiple_of(b * rows, rows), rows)
         load(1, b).wait()
-
-        @pl.when(turn == 0)
-        def _():
-            weight(2).wait()
-            weight(3).wait()
-            for bb in range(blocks):
-                load(4, bb).wait()
-                load(5, bb).wait()
-
-        for kind in (2, 3, 6, 7):
-            load(kind, b).wait()
-        copy.wait_recv()
+        neighbours_sum(b).wait_recv()
+        grad = g[b]
         grad_normed = ysend[b].astype(F32) + yrecv[b].astype(F32)
         middle = m[b]
         inverse = inverse_rms(middle)
@@ -628,14 +693,44 @@
         grad_mid = grad_middle.astype(BF16)
         gy[at] = grad_mid
         save(2, b, gy.at[at], gy_out.at[at])
+
+        @pl.when(turn == 0)
+        def _():
+            weight(2).wait()
+            weight(3).start()
+            load(7, last).start()
+
+        load(2, b).wait()
         grad_mixed = by_last(grad_mid, wo[...]).astype(BF16)
         both = grad_mixed.astype(F32) * o[at].astype(F32)
-        found = jnp.zeros((rows, 128), F32)
+        delta[...] = lax.dot_general(
+            member,
+            both,
+            (((1,), (1,)), ((), ())),
+            precision=lax.Precision.HIGHEST,
+            preferred_element_type=F32,
+        )
         for i in range(heads):
-            cut = slice(i * head, (i + 1) * head)
-            go_heads[i] = grad_mixed[:, cut]
-            found = jnp.where(lane == i, jnp.sum(both[:, cut], axis=1, keepdims=True), found)
-        delta[...] = jnp.transpose(found)[:heads]
+            go_heads[i] = grad_mixed[:, i * head : (i + 1) * head]
+
+        @pl.when(turn == 0)
+        def _():
+            for bb in range(blocks):
+                load(4, bb).wait()
+                load(5, bb).wait()
+
+        load(3, b).wait()
+        load(6, b).wait()
+
+        @pl.when(turn < last)
+        def _():
+            for kind in (0, 1, 2, 3, 6, 7):
+                load(kind, b - 1).start()
+
+        @pl.when((turn < last) & (s == 1))
+        def _():
+            incoming(b - 1).start()
+
         for bb in range(blocks):
 
             @pl.when(b == bb)
@@ -672,15 +767,26 @@
             queries = jnp.concatenate([q[i, at] for i in mine_heads], axis=1).astype(F32)
             ds[pl.ds(j, 1)] += jnp.sum(grad_scaled * queries, axis=0, keepdims=True)
             grads = [
-                (grad_scaled * scale[...]).astype(BF16),
+                (grad_scaled * factor).astype(BF16),
                 jnp.concatenate([dk[i, at] for i in mine_heads], axis=1).astype(BF16),
                 jnp.concatenate([dv[i, at] for i in mine_heads], axis=1).astype(BF16),
             ]
             gp[j, at] = jnp.concatenate(grads, axis=1)
         save(3, b, gp.at[:, at], gp_out.at[:, at])
+
+        @pl.when(turn == 0)
+        def _():
+            weight(3).wait()
+
         n1part[...] = plain(gp[0, at], win[0]) + plain(gp[1, at], win[1])
         copy = remote(n1part.at[theirs], n1recv.at[b], zs_sem.at[b], zr_sem.at[b], core)
         copy.start()
+
+        @pl.when(turn < last)
+        def _():
+            up_part(turn + 1)
+
+        load(7, b).wait()
         hidden = h[b].astype(F32)
         inverse = inverse_rms(hidden)
         unit = hidden * inverse
@@ -697,29 +803,37 @@
         def _():
             remote(xout.at[b], g.at[b, mine], ns_sem.at[b], nr_sem.at[b], section).start()
 
-        spot = out_rows.at[y, mine]
-
-        @pl.when(b == t)
-        def _():
-            pltpu.make_async_copy(xout.at[b], spot, or_sem.at[t]).start()
-
-        @pl.when(b != t)
-        def _():
-            remote(xout.at[b], spot, os_sem.at[b], or_sem.at[t], (s, b, d)).start()
+        @pl.when(b > 0)
+        def _():
+            owner_copy(b, xout.at[b], spot, os_sem, or_sem, lambda copy: copy.start())
+
+        @pl.when(b == 0)
+        def _():
+            save(4, 0, xout.at[0], final)
 
         copy.wait_send()
         return 0
 
+    up_part(jnp.int32(0))
     lax.fori_loop(0, blocks, one_block, 0)
 
     for b in range(blocks):
         at = pl.ds(b * rows, rows)
         piece = g.at[b, mine]
         remote(ysend.at[b], yrecv.at[b], ys_sem.at[b], yr_sem.at[b], core).wait_send()
-        here = out_rows.at[b // 2, pl.ds((b % 2) * half, half)]
-        remote(here, here, os_sem.at[b], or_sem.at[b], core).wait_recv()
+        here = x_rows.at[b // 2, pl.ds((b % 2) * half, half)]
+        remote(here, here, xs_sem.at[b], xr_sem.at[b], core).wait_recv()
 
         @pl.when(b != t)
+        def _():
+            remote(x_in.at[b], here, xs_sem.at[b], xr_sem.at[b], core).wait_send()
+
+        @pl.when(t > 0)
+        def _():
+            here = out_rows.at[b // 2, pl.ds((b % 2) * half, half)]
+            remote(here, here, os_sem.at[b], or_sem.at[b], core).wait_recv()
+
+        @pl.when((b != t) & (b > 0))
         def _():
             remote(xout.at[b], here, os_sem.at[b], or_sem.at[b], core).wait_send()
 
@@ -739,11 +853,12 @@
         ]
         for kind, (src, dst) in enumerate(saved):
             pltpu.make_async_copy(src, dst, save_sem.at[kind, b]).wait()
+    pltpu.make_async_copy(xout.at[0], final, save_sem.at[4, 0]).wait()
 
 
 def backward(saved, gain_one, gain_two, scale):
     g_in, h_in, q_in = saved[:3]
-    win_in, wo_in, wu_in, wd_in = saved[9:]
+    win_in, wo_in, wu_in, wd_in = saved[9:13]
     blocks, rows, width = g_in.shape
     heads, length, head = q_in.shape
     local = wu_in.shape[0] // 2
@@ -751,6 +866,8 @@
     shape = jax.ShapeDtypeStruct
     outs = [
         shape((2, rows, width), BF16),
+        shape((2, rows, width), BF16),
+        shape((half, width), BF16),
         shape((length, width), BF16),
         shape((length, 2 * local), BF16),
         shape((length, width), BF16),
@@ -790,12 +907,12 @@
         DMA((8, blocks)),
         DMA((4,)),
     ]
-    scratch += [DMA((blocks,))] * 10 + [DMA((4, blocks))]
+    scratch += [DMA((blocks,))] * 12 + [DMA((5, blocks))]
     return pl.pallas_call(
         backward_kernel,
         out_shape=outs,
-        in_specs=[ANY] * 13 + [VMEM] * 3,
-        out_specs=[ANY] * 5 + [VMEM] * 3,
+        in_specs=[ANY] * 14 + [VMEM] * 3,
+        out_specs=[ANY] * 7 + [VMEM] * 3,
         scratch_shapes=scratch,
         compiler_params=pltpu.CompilerParams(
             collective_id=2, has_side_effects=True, vmem_limit_bytes=62 * MIB
@@ -824,34 +941,47 @@
 
 
 def gradient_kernel(
-    n1_in, n2_in, gy_in, g_in, gp_in, gu_in, o_in, a_in, small,
-    out, small_out,
-    x, xt, gp, gu, o, a, keep, give, yrecv, flow, last, keep_d, give_d, flow_k, flow_g, last_k, last_g,
-    yd, smalls, chain,
-    x_sem, g_sem, ys_sem, yr_sem, fs_sem, fr_sem, last_sem, ks_sem, kr_sem, gs_sem, gr_sem, last_d_sem,
-    yds_sem, ydr_sem, ss_sem, sr_sem, cs_sem, cr_sem,
+    n1_in, n2_in, gy_in, g_in, gp_in, gu_in, o_in, a_in, final, rows_in, dg1, dg2, ds, dim_scale,
+    out_q, out_k, out_v, out_u, out_o, out_d, rows_out, out_g1, out_g2, out_s,
+    x, xt, gp, gu, o, a,
+    keep_a, give_a, yrecv_a, flow_a, last_a, keep_b, give_b, yrecv_b, flow_b, last_b,
+    line, flow_d, last_d, rest, yd, small, smalls, chain,
+    x_sem, g_sem, ys_sem, yr_sem, fs_sem, fr_sem, last_sem, ds_sem, dr_sem, last_d_sem,
+    yds_sem, ydr_sem, ss_sem, sr_sem, cs_sem, cr_sem, es_sem, er_sem,
 ):
     s, t, d = lax.axis_index("section"), lax.axis_index("tensor"), lax.axis_index("dp")
-    n, chunk, wide = keep.shape
-    local = keep_d.shape[2]
-    pieces = ys_sem.shape[1]
+    n, chunk, _ = keep_a.shape
+    local = a.shape[1] // 2
+    split = yd.shape[1]
+    width = dg1.shape[1]
+    pieces = ys_sem.shape[2]
     step = chunk // pieces
     core = (s, other(t), d)
     across = (s, lax.rem(t + 2, 4), d)
     diagonal = (s, other(lax.rem(t + 2, 4)), d)
     up = (s, t, lax.rem(d + 1, n))
     down = (s, t, lax.rem(d + n - 1, n))
-
-    def load(i, source):
-        return pltpu.make_async_copy(source, x.at[i % 2], x_sem.at[i])
+    c, y = lax.rem(t, 2), t // 2
 
     sources = [g_in, n1_in, n2_in, gy_in]
-    load(0, g_in).start()
     operands = [(a_in, a), (gp_in, gp), (gu_in, gu), (o_in, o)]
-    pltpu.make_async_copy(a_in, a, g_sem.at[0]).start()
-    load(1, n1_in).start()
+
+    def load(i):
+        return pltpu.make_async_copy(sources[i], x.at[i % 2], x_sem.at[i])
+
+    def operand(i):
+        return pltpu.make_async_copy(*operands[i], g_sem.at[i])
+
+    load(0).start()
+    operand(0).start()
+    load(1).start()
     for i in range(1, 4):
-        pltpu.make_async_copy(operands[i][0], operands[i][1], g_sem.at[i]).start()
+        operand(i).start()
+
+    small[0:1, :width] = dg1[...]
+    small[0:1, width : 2 * width] = jnp.where(c == 0, dg2[...], 0.0)
+    small[0:1, 2 * width : 2 * width + local] = ds[0:1]
+    small[0:1, 2 * width + 384 : 2 * width + 384 + local] = ds[1:2]
 
     greet([core, across, diagonal, up, down])
 
@@ -864,136 +994,146 @@
         share(i).start()
 
     def turn(i):
-        load(i, sources[i]).wait()
+        load(i).wait()
         turned = jnp.transpose(x[i % 2])
         for e in range(n):
             xt[i, e] = turned[e * chunk : (e + 1) * chunk]
         if i + 2 < 4:
-            load(i + 2, sources[i + 2]).start()
-
-    def flow_piece(buffer, into, e, send, receive, device):
-        return remote(buffer.at[e], into.at[e], send.at[e], receive.at[e], device)
+            load(i + 2).start()
+
+    groups = [(keep_a, give_a, yrecv_a, flow_a, last_a), (keep_b, give_b, yrecv_b, flow_b, last_b)]
+
+    def exchange(which, e, i):
+        _, give, yrecv, _, _ = groups[which]
+        rows = pl.ds(i * step, step)
+        return remote(
+            give.at[e, rows], yrecv.at[e, rows], ys_sem.at[which, e, i], yr_sem.at[which, e, i], across
+        )
+
+    def send_all(which, e):
+        for i in range(pieces):
+            exchange(which, e, i).start()
+
+    def send_d(e):
+        src = line.at[e]
+
+        @pl.when(e > d)
+        def _():
+            remote(src, flow_d.at[e], ds_sem.at[e], dr_sem.at[e], up).start()
+
+        @pl.when(e < d - 1)
+        def _():
+            remote(src, flow_d.at[e], ds_sem.at[e], dr_sem.at[e], down).start()
+
+        @pl.when(e == d - 1)
+        def _():
+            remote(src, last_d, ds_sem.at[e], last_d_sem, down).start()
+
+    def upstream_d(e):
+        piece = flow_d.at[e]
+        remote(piece, piece, ds_sem.at[e], dr_sem.at[e], up).wait_recv()
+        line[e] = (line[e].astype(F32) + flow_d[e].astype(F32)).astype(BF16)
 
     turn(0)
-    pltpu.make_async_copy(a_in, a, g_sem.at[0]).wait()
-
-    def down_product(e, _):
-        both = plain(xt[0, e], a[...])
-        keep_d[e] = both[:, :local].astype(BF16)
-        give_d[e] = both[:, local:].astype(BF16)
+    operand(0).wait()
+
+    def down_product(k, _):
+        e = farthest_first(d, k, n)
+        both = plain(xt[0, e], a[...]).astype(BF16)
+        line[e] = jnp.concatenate([both[:, :split], both[:, local : local + split]], axis=1)
+        for j in range(2):
+            rest[j, e] = both[:, j * local + split : (j + 1) * local]
+
+        @pl.when(((d == 0) | (d == n - 1)) & (e != d))
+        def _():
+            send_d(e)
+
         return 0
 
     lax.fori_loop(0, n, down_product, 0)
 
-    line_d = [(keep_d, flow_k, last_k, ks_sem, kr_sem, 0), (give_d, flow_g, last_g, gs_sem, gr_sem, 1)]
-
-    def upstream_d(e, buffer, into, send, receive):
-        piece = into.at[e]
-        remote(piece, piece, send.at[e], receive.at[e], up).wait_recv()
-        buffer[e] = (buffer[e].astype(F32) + into[e].astype(F32)).astype(BF16)
-
-    def send_d(e, buffer, into, spare, send, receive, i):
-        @pl.when(e > d)
-        def _():
-            remote(buffer.at[e], into.at[e], send.at[e], receive.at[e], up).start()
-
-        @pl.when(e < d - 1)
-        def _():
-            remote(buffer.at[e], into.at[e], send.at[e], receive.at[e], down).start()
-
-        @pl.when(e == d - 1)
-        def _():
-            remote(buffer.at[e], spare, send.at[e], last_d_sem.at[i], down).start()
-
-    def ends(k, _):
+    turn(1)
+    operand(1).wait()
+
+    def in_product(k, _):
         e = farthest_first(d, k, n)
-        for buffer, into, spare, send, receive, i in line_d:
-
-            @pl.when(((d == 0) | (d == n - 1)) & (e != d))
-            def _():
-                send_d(e, buffer, into, spare, send, receive, i)
-
+        for j, target in ((1, give_a), (0, keep_a)):
+            target[e] = jnp.concatenate(
+                [plain(xt[1, e], gp[j]).astype(BF16), rest[j, e]], axis=1
+            )
+            if j:
+                send_all(0, e)
         return 0
 
-    lax.fori_loop(0, n, ends, 0)
-
-    turn(1)
+    lax.fori_loop(0, n, in_product, 0)
+
     turn(2)
     turn(3)
-    for i in range(1, 4):
-        pltpu.make_async_copy(operands[i][0], operands[i][1], g_sem.at[i]).wait()
-
-    def exchange(e, i):
-        rows = pl.ds(i * step, step)
-        return remote(
-            give.at[e, rows], yrecv.at[e, rows], ys_sem.at[e, i], yr_sem.at[e, i], across
-        )
-
-    def products(k, _):
+    operand(2).wait()
+    operand(3).wait()
+
+    def other_product(k, _):
         e = farthest_first(d, k, n)
         ups = plain(xt[2, e], gu[...])
         outs = plain(xt[3, e], o[...])
-        for j, target in ((1, give), (0, keep)):
+        for j, target in ((1, give_b), (0, keep_b)):
             cut = slice(j * local, (j + 1) * local)
-            target[e] = jnp.concatenate(
-                [
-                    plain(xt[1, e], gp[j]).astype(BF16),
-                    ups[:, cut].astype(BF16),
-                    outs[:, cut].astype(BF16),
-                ],
-                axis=1,
-            )
+            target[e] = jnp.concatenate([ups[:, cut], outs[:, cut]], axis=1).astype(BF16)
             if j:
-                for i in range(pieces):
-                    exchange(e, i).start()
+                send_all(1, e)
         return 0
 
-    lax.fori_loop(0, n, products, 0)
+    lax.fori_loop(0, n, other_product, 0)
+
+    half = final.shape[0]
+    owner = (s, 0, d)
+    spot = rows_out.at[y, pl.ds(pl.multiple_of(c * half, half), half)]
+
+    @pl.when(t == 0)
+    def _():
+        pltpu.make_async_copy(final, spot, er_sem.at[0]).start()
+
+    @pl.when(t != 0)
+    def _():
+        remote(final, spot, es_sem, er_sem.at[t], owner).start()
 
     for i in range(3):
         share(i).wait_recv()
     mine = small[...] + smalls[0] + (smalls[1] + smalls[2])
-    small_out[...] = mine
 
     def link(i, device):
         return remote(chain.at[i], chain.at[2 + i], cs_sem.at[i], cr_sem.at[i], device)
 
-    for i, first, final, device in ((0, d == 0, d == n - 1, up), (1, d == n - 1, d == 0, down)):
+    smalls[0] = mine
+    for i, opens, closes, device in ((0, d == 0, d == n - 1, up), (1, d == n - 1, d == 0, down)):
         chain[i] = mine
 
-        @pl.when(jnp.logical_not(first))
+        @pl.when(jnp.logical_not(opens))
         def _():
             link(i, device).wait_recv()
             chain[i] = mine + chain[2 + i]
-            small_out[...] += chain[2 + i]
-
-        @pl.when(jnp.logical_not(final))
+            smalls[0] += chain[2 + i]
+
+        @pl.when(jnp.logical_not(closes))
         def _():
             link(i, device).start()
 
-    def middle(k, _):
+    def middle(k):
         e = farthest_first(d, k, n)
-        for buffer, into, spare, send, receive, i in line_d:
-
-            @pl.when((d > 0) & (d < n - 1) & (e != d))
-            def _():
-                upstream_d(e, buffer, into, send, receive)
-                send_d(e, buffer, into, spare, send, receive, i)
-
-        return 0
-
-    lax.fori_loop(0, n, middle, 0)
-
-    def flows(k, _):
+
+        @pl.when((d > 0) & (d < n - 1) & (e != d))
+        def _():
+            upstream_d(e)
+            send_d(e)
+
+    def flows(which, k):
         e = farthest_first(d, k, n)
+        keep, give, yrecv, flow, last = groups[which]
+        send, receive = fs_sem.at[which], fr_sem.at[which]
         for i in range(pieces):
             at = pl.ds(i * step, step)
-
+            exchange(which, e, i).wait_recv()
             first = ((e > d) & (d == 0)) | ((e < d) & (d == n - 1))
-
-            @pl.when(e != d)
-            def _():
-                exchange(e, i).wait_recv()
 
             @pl.when((e != d) & first)
             def _():
@@ -1002,7 +1142,7 @@
             @pl.when((e != d) & jnp.logical_not(first))
             def _():
                 piece = flow.at[e, at]
-                remote(piece, piece, fs_sem.at[e, i], fr_sem.at[e, i], up).wait_recv()
+                remote(piece, piece, send.at[e, i], receive.at[e, i], up).wait_recv()
                 total = keep[e, at].astype(F32) + yrecv[e, at].astype(F32)
                 keep[e, at] = (total + flow[e, at].astype(F32)).astype(BF16)
 
@@ -1010,52 +1150,101 @@
 
             @pl.when(e > d)
             def _():
-                remote(src, flow.at[e, at], fs_sem.at[e, i], fr_sem.at[e, i], up).start()
+                remote(src, flow.at[e, at], send.at[e, i], receive.at[e, i], up).start()
 
             @pl.when(e < d - 1)
             def _():
-                remote(src, flow.at[e, at], fs_sem.at[e, i], fr_sem.at[e, i], down).start()
+                remote(src, flow.at[e, at], send.at[e, i], receive.at[e, i], down).start()
 
             @pl.when(e == d - 1)
             def _():
-                remote(src, last.at[at], fs_sem.at[e, i], last_sem.at[i], down).start()
-
+                remote(src, last.at[at], send.at[e, i], last_sem.at[which, i], down).start()
+
+    def flows_in(k, _):
+        middle(k)
+        flows(0, k)
         return 0
 
-    lax.fori_loop(0, n, flows, 0)
-
-    for buffer, into, spare, send, receive, i in line_d:
+    def flows_other(k, _):
+        flows(1, k)
+        return 0
+
+    lax.fori_loop(0, n, flows_in, 0)
+
+    @pl.when(d > 0)
+    def _():
+        upstream_d(d)
+
+    @pl.when(d < n - 1)
+    def _():
+        remote(last_d, last_d, ds_sem.at[0], last_d_sem, down).wait_recv()
+        line[d] = (line[d].astype(F32) + last_d[...].astype(F32)).astype(BF16)
+
+    crossing = remote(line.at[d, :, pl.ds(split, split)], yd, yds_sem, ydr_sem, across)
+    crossing.start()
+
+    lax.fori_loop(0, n, flows_other, 0)
+
+    def landed(which, i):
+        keep, _, yrecv, flow, last = groups[which]
+        at = pl.ds(i * step, step)
 
         @pl.when(d > 0)
         def _():
-            upstream_d(d, buffer, into, send, receive)
+            piece = flow.at[d, at]
+            remote(
+                piece, piece, fs_sem.at[which, d, i], fr_sem.at[which, d, i], up
+            ).wait_recv()
 
         @pl.when(d < n - 1)
         def _():
-            remote(spare, spare, send.at[0], last_d_sem.at[i], down).wait_recv()
-            buffer[d] = (buffer[d].astype(F32) + spare[...].astype(F32)).astype(BF16)
-
-    crossing = remote(give_d.at[d], yd, yds_sem, ydr_sem, across)
-    crossing.start()
+            piece = last.at[at]
+            remote(
+                piece, piece, fs_sem.at[which, d, i], last_sem.at[which, i], down
+            ).wait_recv()
+
+        above = jnp.where(d > 0, flow[d, at].astype(F32), 0.0)
+        below = jnp.where(d < n - 1, last[at].astype(F32), 0.0)
+        return (keep[d, at].astype(F32) + yrecv[d, at].astype(F32)) + (above + below)
+
+    rests = []
     for i in range(pieces):
         at = pl.ds(i * step, step)
-        exchange(d, i).wait_recv()
-        out[at, :wide] = keep[d, at].astype(F32) + yrecv[d, at].astype(F32)
-
-        @pl.when(d > 0)
-        def _():
-            piece = flow.at[d, at]
-            remote(piece, piece, fs_sem.at[d, i], fr_sem.at[d, i], up).wait_recv()
-            out[at, :wide] += flow[d, at].astype(F32)
-
-        @pl.when(d < n - 1)
-        def _():
-            piece = last.at[at]
-            remote(piece, piece, fs_sem.at[d, i], last_sem.at[i], down).wait_recv()
-            out[at, :wide] += last[at].astype(F32)
-
+        total = landed(0, i)
+        for j, ref in enumerate((out_q, out_k, out_v)):
+            ref[at] = total[:, j * local : (j + 1) * local]
+        rests.append(total[:, 3 * local :])
     crossing.wait_recv()
-    out[:, wide:] = keep_d[d].astype(F32) + yd[...].astype(F32)
+    most = line[d, :, :split].astype(F32) + yd[...].astype(F32)
+    out_d[...] = jnp.transpose(jnp.concatenate([most, jnp.concatenate(rests, axis=0)], axis=1))
+    found = smalls[0]
+    out_g1[...] = found[0:1, :width]
+    out_g2[...] = found[0:1, width : 2 * width]
+    head = dim_scale.shape[1]
+    scale = jnp.zeros((1, head), F32)
+    for j in range(2):
+        for i in range(local // head):
+            start = 2 * width + j * 384 + i * head
+            scale = scale + found[0:1, start : start + head]
+    raw = dim_scale[...]
+    grown = jnp.maximum(raw, 0.0) + jnp.log(1.0 + jnp.exp(-jnp.abs(raw)))
+    out_s[...] = scale / grown * (1.0 / (1.0 + jnp.exp(-raw)))
+    totals = []
+    for i in range(pieces):
+        total = landed(1, i)
+        out_u[pl.ds(i * step, step)] = total[:, :local]
+        totals.append(total[:, local:])
+    out_o[...] = jnp.transpose(jnp.concatenate(totals, axis=0))
+
+    @pl.when(t == 0)
+    def _():
+        for i in range(4):
+            piece = rows_out.at[i // 2, pl.ds(i % 2 * half, half)]
+            remote(piece, piece, es_sem, er_sem.at[i], owner).wait_recv()
+
+    @pl.when(t != 0)
+    def _():
+        remote(final, spot, es_sem, er_sem.at[t], owner).wait_send()
 
     crossing.wait_send()
     for i in range(3):
@@ -1070,39 +1259,51 @@
         link(1, down).wait_send()
 
     def drain(e, _):
-        for i in range(pieces):
-            exchange(e, i).wait_send()
+        for which in range(2):
+            for i in range(pieces):
+                exchange(which, e, i).wait_send()
 
         @pl.when(e != d)
         def _():
-            for i in range(pieces):
-                piece = keep.at[e, pl.ds(i * step, step)]
-                remote(piece, piece, fs_sem.at[e, i], fr_sem.at[e, i], up).wait_send()
-            for buffer, into, spare, send, receive, i in line_d:
-                remote(buffer.at[e], buffer.at[e], send.at[e], receive.at[e], up).wait_send()
+            for which in range(2):
+                for i in range(pieces):
+                    piece = groups[which][0].at[e, pl.ds(i * step, step)]
+                    remote(
+                        piece, piece, fs_sem.at[which, e, i], fr_sem.at[which, e, i], up
+                    ).wait_send()
+            remote(line.at[e], line.at[e], ds_sem.at[e], dr_sem.at[e], up).wait_send()
 
         return 0
 
     lax.fori_loop(0, n, drain, 0)
 
 
-def gradients(n1, n2, gy, g, gp, gu, o, a, small):
+def gradients(n1, n2, gy, g, gp, gu, o, a, final, rows, dg1, dg2, ds, dim_scale):
     n = lax.axis_size("dp")
     length, width = n1.shape
     local = gp.shape[2] // 3
     chunk = width // n
-    wide = 5 * local
     pieces = 4 if chunk % 64 == 0 else 1
-    big = pltpu.VMEM((n, chunk, wide), BF16)
-    line = pltpu.VMEM((n, chunk, local), BF16)
+    small = (1, 2 * width + 768)
+
+    def lines(columns):
+        return [pltpu.VMEM((n, chunk, columns), BF16)] * 4 + [pltpu.VMEM((chunk, columns), BF16)]
+
+    split = local // 128 * 128
+    line = pltpu.VMEM((n, chunk, 2 * split), BF16)
     return pl.pallas_call(
         gradient_kernel,
-        out_shape=[
-            jax.ShapeDtypeStruct((chunk, 6 * local), F32),
-            jax.ShapeDtypeStruct(small.shape, F32),
+        out_shape=[jax.ShapeDtypeStruct((chunk, local), F32)] * 4
+        + [jax.ShapeDtypeStruct((local, chunk), F32)] * 2
+        + [
+            jax.ShapeDtypeStruct(rows.shape, BF16),
+            jax.ShapeDtypeStruct(dg1.shape, F32),
+            jax.ShapeDtypeStruct(dg2.shape, F32),
+            jax.ShapeDtypeStruct(dim_scale.shape, F32),
         ],
-        in_specs=[ANY] * 8 + [VMEM],
-        out_specs=[VMEM, VMEM],
+        in_specs=[ANY] * 10 + [VMEM] * 4,
+        out_specs=[VMEM] * 6 + [ANY] + [VMEM] * 3,
+        input_output_aliases={9: 6},
         scratch_shapes=[
             pltpu.VMEM((2, length, width), BF16),
             pltpu.VMEM((4, n, chunk, length), BF16),
@@ -1110,74 +1311,61 @@
             pltpu.VMEM(gu.shape, BF16),
             pltpu.VMEM(o.shape, BF16),
             pltpu.VMEM(a.shape, BF16),
-            big,
-            big,
-            big,
-            big,
-            pltpu.VMEM((chunk, wide), BF16),
-            line,
-            line,
-            line,
-            line,
-            pltpu.VMEM((chunk, local), BF16),
-            pltpu.VMEM((chunk, local), BF16),
-            pltpu.VMEM((chunk, local), BF16),
-            pltpu.VMEM((3,) + small.shape, F32),
-            pltpu.VMEM((4,) + small.shape, F32),
+        ]
+        + lines(4 * local - split)
+        + lines(2 * local)
+        + [line] * 2
+        + [
+            pltpu.VMEM((chunk, 2 * split), BF16),
+            pltpu.VMEM((2, n, chunk, local - split), BF16),
+            pltpu.VMEM((chunk, split), BF16),
+            pltpu.VMEM(small, F32),
+            pltpu.VMEM((3,) + small, F32),
+            pltpu.VMEM((4,) + small, F32),
             DMA((4,)),
             DMA((4,)),
-            DMA((n, pieces)),
-            DMA((n, pieces)),
-            DMA((n, pieces)),
-            DMA((n, pieces)),
-            DMA((pieces,)),
+        ]
+        + [DMA((2, n, pieces))] * 4
+        + [
+            DMA((2, pieces)),
             DMA((n,)),
             DMA((n,)),
-            DMA((n,)),
-            DMA((n,)),
-            DMA((2,)),
+            DMA,
             DMA,
             DMA,
             DMA((3,)),
             DMA((3,)),
             DMA((2,)),
             DMA((2,)),
+            DMA,
+            DMA((4,)),
         ],
         compiler_params=pltpu.CompilerParams(
             collective_id=3, has_side_effects=True, vmem_limit_bytes=62 * MIB
         ),
         name="gradients",
-    )(n1, n2, gy, g, gp, gu, o, a, small)
+    )(n1, n2, gy, g, gp, gu, o, a, final, rows, dg1, dg2, ds, dim_scale)
 
 
 def body(
     inputs, cotangent, gain_attn, w_query, w_key, w_value, w_out, dim_scale, gain_mlp, w_up, w_down
 ):
-    local = w_query.shape[2]
     head = dim_scale.shape[1]
-    width = inputs.shape[2]
     shards = (w_query[0].T, w_key[0].T, w_value[0].T, w_out[0], w_up[0].T, w_down[0])
-    multiplier = LOG2E / math.sqrt(head)
-    per_dim = multiplier * jax.nn.softplus(dim_scale)
     done = forward(
-        inputs, cotangent, shards, gain_attn, gain_mlp, per_dim, head
+        inputs, cotangent, shards, gain_attn, gain_mlp, dim_scale, head
     )
-    layer_out, h, n1, q, k, v, o, lse, m, n2, u, a, g, win, wo, wu, wd = done
-    input_grads, g_all, gu, gy, gp, dg1, dg2, ds = backward(
-        (g, h, q, k, v, o, lse, m, u, win, wo, wu, wd),
+    x_halves, h, n1, q, k, v, o, lse, m, n2, u, a, g, win, wo, wu, wd = done
+    layer_out, input_grads, final, g_all, gu, gy, gp, dg1, dg2, ds = backward(
+        (g, h, q, k, v, o, lse, m, u, win, wo, wu, wd, x_halves),
         gain_attn,
         gain_mlp,
-        jnp.tile(per_dim, (1, local // head)),
+        dim_scale,
     )
 
-    first_core = lax.rem(lax.axis_index("tensor"), 2) == 0
-    dg2 = jnp.where(first_core, dg2, 0.0)
-    small = jnp.concatenate([dg1, dg2, ds.reshape(1, -1)], axis=1)
-    grads, small = gradients(n1, n2, gy, g_all, gp, gu, o, a, small)
-    dg1, dg2 = small[:, :width], small[:, width : 2 * width]
-    ds = jnp.sum(small[:, 2 * width :].reshape(-1, head), axis=0, keepdims=True)
-    grad_scale = ds / per_dim * multiplier * jax.nn.sigmoid(dim_scale)
-    pieces = [grads[:, i * local : (i + 1) * local] for i in range(6)]
+    *pieces, input_grads, dg1, dg2, grad_scale = gradients(
+        n1, n2, gy, g_all, gp, gu, o, a, final, input_grads, dg1, dg2, ds, dim_scale
+    )
     return (
         layer_out[None],
         input_grads[None],
@@ -1185,11 +1373,11 @@
         pieces[0][None],
         pieces[1][None],
         pieces[2][None],
-        pieces[4].T[None],
+        pieces[4][None],
         grad_scale,
         dg2,
         pieces[3][None],
-        pieces[5].T[None],
+        pieces[5][None],
     )
 
 

time: 386 us -> 348 us (0.902)
  Pallas kernels: 368 us -> 338 us
    pallas_call x2, Pallas kernels: 267 us -> 244 us  [the longest x1 125 us: backward(): pl.pallas_call(backward_kernel, out_shape=outs, in_specs=[ANY] * 14 + [VM...]
    pallas_call x1, Pallas kernels: 101 us -> 93.4 us  [forward(): pl.pallas_call(forward_kernel, out_shape=outs, in_specs=[ANY] * 8 + [VMEM...]
    unnamed x12 -> x33, local copies, waits for them, and re-layouts: 4.12 us -> 9.24 us
where the time goes in v4:
time: 348 us
  Pallas kernels  338 us (97%)
  local copies, waits for them, and re-layouts  9.24 us (3%)
    pallas_call x1, Pallas kernels, backward(): pl.pallas_call(backward_kernel, out_shape=outs, in_specs=[ANY] * 14 + [VM...  125 us
    pallas_call x1, Pallas kernels, gradients(): pl.pallas_call(gradient_kernel, out_shape=[jax.ShapeDtypeStruct((chunk, l...  119 us
    pallas_call x1, Pallas kernels, forward(): pl.pallas_call(forward_kernel, out_shape=outs, in_specs=[ANY] * 8 + [VMEM...  93.4 us
    unnamed x33, local copies, waits for them, and re-layouts  9.24 us

profile of v4, /device:TPU:0, one launch (start us, length us, event | category | flops | bytes accessed | tf_op | source)
XLA Modules:
  0.0 347.5 jit_solution(1919323649859473820)
XLA Ops:
  0.6 93.4 %forward.1 = (bf16[4,128,1280]{2,1,0:T(8,128)(2,1)}, bf16[4,256,1280]{2,1,0:T(8,128)(2,1)}, bf16[1024,1280]{1,0:T(8,128)(2,1)}, bf16[8,1024,80]{2,1,0:T(8,128)(2...) custom-call(bf16[2,256,1280]{2,1,0:T(8,128)(2,1)} %inputs.1, ...), custom_call_target="tpu_custom_call" | custom-call | tf_op jit(solution)/shard_map/forward/pallas_call | solution.py:527
  94.1 125.5 %backward.1 = (bf16[2,256,1280]{2,1,0:T(8,128)(2,1)}, bf16[2,256,1280]{2,1,0:T(8,128)(2,1)}, bf16[128,1280]{1,0:T(8,128)(2,1)}, bf16[1024,1280]{1,0:T(8,128)(2,1...) custom-call(bf16[4,256,1280]{2,1,0:T(8,128)(2,1)} %get-tuple-element, ...), custom_call_target="tpu_custom_call" | custom-call | tf_op jit(solution)/shard_map/backward/pallas_call | solution.py:911
  219.6 0.0 copy-start.1
  219.6 118.7 %gradients.1 = (f32[320,320]{1,0:T(8,128)}, f32[320,320]{1,0:T(8,128)}, f32[320,320]{1,0:T(8,128)}, f32[320,320]{1,0:T(8,128)}, f32[320,320]{1,0:T(8,128)}, /*in...) custom-call(bf16[1024,1280]{1,0:T(8,128)(2,1)} %get-tuple-element.63, ...), custom_call_target="tpu_custom_call", output_to_operand_aliasing={{6}: (9, {})} | custom-call | tf_op jit(solution)/shard_map/gradients/pallas_call | solution.py:1294
  338.2 0.0 copy-start
  338.2 0.0 copy-done.1
  338.3 1.1 copy.35
  339.3 0.7 copy-done
  340.0 1.1 copy.36
  341.1 0.0 copy-done.9
  341.1 0.6 copy.37
  341.7 0.0 copy-done.7
  341.7 0.8 copy.38
  342.5 0.0 copy-done.6
  342.5 0.8 copy.39
  343.3 0.0 copy-done.5
  343.3 0.8 copy.40
  344.0 0.0 copy-done.4
  344.0 0.8 copy.41
  344.8 0.0 copy-done.10
  344.8 0.5 copy.42
  345.3 0.6 copy.43
  345.9 0.8 copy.44
  346.7 0.8 copy.45
  (12 shorter events, 0.0 us)
Async XLA Ops:
  219.6 118.7 %copy-start.1 = (bf16[2,256,1280]{2,1,0:T(8,128)(2,1)S(1)}, bf16[2,256,1280]{2,1,0:T(8,128)(2,1)}, u32[]{:S(2)}) copy-start(bf16[2,256,1280]{2,1,0:T(8,128)(2,1)} %get-tuple-element.62) | copy-start | bytes 3932164
  338.2 1.8 copy-start
  340.0 1.1 copy-start.9
  340.0 1.7 copy-start.7
  340.0 2.4 copy-start.6
  341.1 2.2 copy-start.5
  341.1 3.0 copy-start.4
  342.5 2.4 copy-start.10
  342.5 2.9 copy-start.8
  342.5 3.5 copy-start.3
  343.3 3.5 copy-start.2

commit v5 on v4

--- a/solution.py
+++ b/solution.py
@@ -388,6 +388,19 @@
         save(8, b, n2.at[at], n2_out.at[at])
         save(9, b, u.at[b], u_out.at[b])
         save(10, b, a.at[at], a_out.at[at])
+
+        @pl.when(s == 0)
+        def _():
+            finish(b)
+
+        @pl.when((s == 1) & (b > 0))
+        def _():
+            finish(b - 1)
+
+        return 0
+
+    def finish(b):
+        copy = remote(zpart.at[b, theirs], zrecv.at[b], zs_sem.at[b], zr_sem.at[b], core)
         copy.wait_recv()
         xout[b] = (m[b, mine] + (zpart[b, mine] + zrecv[b])).astype(BF16)
 
@@ -396,9 +409,13 @@
             remote(xout.at[b], land.at[1, b, mine], ns_sem.at[b], nr_sem.at[b], section).start()
 
         save(13, b, xout.at[b], x_out.at[b])
-        return 0
 
     lax.fori_loop(0, blocks, feed, 0)
+
+    @pl.when(s == 1)
+    def _():
+        finish(blocks - 1)
+
 
     @pl.when(s == 1)
     def _():
@@ -593,7 +610,9 @@
     weight(1).start()
     load(1, last).start()
 
-    greet([core, across, diagonal, section])
+    barrier = pltpu.get_barrier_semaphore()
+    for device in (core, across, diagonal, section):
+        pl.semaphore_signal(barrier, inc=1, device_id=device, device_id_type=MESH)
 
     spot = out_rows.at[y, mine]
 
@@ -606,11 +625,6 @@
         def _():
             act(remote(src, dst, send.at[b], receive.at[t], (s, b, d)))
 
-    for b in range(blocks):
-        owner_copy(b, x_in.at[b], x_rows.at[y, mine], xs_sem, xr_sem, lambda copy: copy.start())
-
-    dk[...] = jnp.zeros_like(dk)
-    dv[...] = jnp.zeros_like(dv)
     dg1[...] = jnp.zeros_like(dg1)
     dg2[...] = jnp.zeros_like(dg2)
     ds[...] = jnp.zeros_like(ds)
@@ -639,6 +653,10 @@
         def _():
             incoming(b).wait()
 
+        @pl.when(turn == 0)
+        def _():
+            pl.semaphore_wait(barrier, 4)
+
         @pl.when(s == 0)
         def _():
             piece = g.at[b, mine]
@@ -673,6 +691,13 @@
         save(1, b, gu.at[at], gu_out.at[at])
         ysend[b] = plain(grad_up, wu[...]).astype(BF16)
         neighbours_sum(b).start()
+
+        @pl.when(turn == 0)
+        def _():
+            for bb in range(blocks):
+                owner_copy(
+                    bb, x_in.at[bb], x_rows.at[y, mine], xs_sem, xr_sem, lambda copy: copy.start()
+                )
 
     def one_block(turn, _):
         b = last - turn
@@ -752,8 +777,14 @@
                                 weight = jnp.where(causal, weight, 0.0)
                             grad_score = weight * (by_last(v[i, lo:hi], gh) - inner)
                             grad_score = grad_score.astype(BF16)
-                            dv[i, lo:hi] += plain(weight.astype(BF16), gh)
-                            dk[i, lo:hi] += plain(grad_score, qh)
+                            more_v = plain(weight.astype(BF16), gh)
+                            more_k = plain(grad_score, qh)
+                            if bb == last:
+                                dv[i, lo:hi] = more_v
+                                dk[i, lo:hi] = more_k
+                            else:
+                                dv[i, lo:hi] += more_v
+                                dk[i, lo:hi] += more_k
                             part = by_first(kj, grad_score)
                             total = part if total is None else total + part
                         gq_heads[i] = jnp.transpose(total)
@@ -942,12 +973,12 @@
 
 def gradient_kernel(
     n1_in, n2_in, gy_in, g_in, gp_in, gu_in, o_in, a_in, final, rows_in, dg1, dg2, ds, dim_scale,
-    out_q, out_k, out_v, out_u, out_o, out_d, rows_out, out_g1, out_g2, out_s,
-    x, xt, gp, gu, o, a,
+    q_out, k_out, v_out, u_out, o_out, d_out, rows_out, out_g1, out_g2, out_s,
+    out_q, out_k, out_v, out_u, out_o, out_d, x, xt, gp, gu, o, a,
     keep_a, give_a, yrecv_a, flow_a, last_a, keep_b, give_b, yrecv_b, flow_b, last_b,
-    line, flow_d, last_d, rest, yd, small, smalls, chain,
+    line, flow_d, last_d, rest, yd, small, smalls, chain, out_rows_a, out_rows_b,
     x_sem, g_sem, ys_sem, yr_sem, fs_sem, fr_sem, last_sem, ds_sem, dr_sem, last_d_sem,
-    yds_sem, ydr_sem, ss_sem, sr_sem, cs_sem, cr_sem, es_sem, er_sem,
+    yds_sem, ydr_sem, ss_sem, sr_sem, cs_sem, cr_sem, es_sem, er_sem, out_sem, rs_sem, hop_sem, here_sem,
 ):
     s, t, d = lax.axis_index("section"), lax.axis_index("tensor"), lax.axis_index("dp")
     n, chunk, _ = keep_a.shape
@@ -972,6 +1003,20 @@
     def operand(i):
         return pltpu.make_async_copy(*operands[i], g_sem.at[i])
 
+    section = (1 - s, t, d)
+    slanted = (1 - s, 1 - t, d)
+    barrier = pltpu.get_barrier_semaphore()
+    for device in (core, across, diagonal, up, down):
+        pl.semaphore_signal(barrier, inc=1, device_id=device, device_id_type=MESH)
+
+    @pl.when((s == 1) & (t != 1))
+    def _():
+        pl.semaphore_signal(barrier, inc=1, device_id=section, device_id_type=MESH)
+
+    @pl.when((s == 1) & (t == 1))
+    def _():
+        pl.semaphore_signal(barrier, inc=1, device_id=slanted, device_id_type=MESH)
+
     load(0).start()
     operand(0).start()
     load(1).start()
@@ -983,15 +1028,10 @@
     small[0:1, 2 * width : 2 * width + local] = ds[0:1]
     small[0:1, 2 * width + 384 : 2 * width + 384 + local] = ds[1:2]
 
-    greet([core, across, diagonal, up, down])
-
     partners = [core, across, diagonal]
 
     def share(i):
         return remote(small, smalls.at[i], ss_sem.at[i], sr_sem.at[i], partners[i])
-
-    for i in range(3):
-        share(i).start()
 
     def turn(i):
         load(i).wait()
@@ -1034,38 +1074,80 @@
         remote(piece, piece, ds_sem.at[e], dr_sem.at[e], up).wait_recv()
         line[e] = (line[e].astype(F32) + flow_d[e].astype(F32)).astype(BF16)
 
-    turn(0)
-    operand(0).wait()
-
-    def down_product(k, _):
+    def down_product(k):
         e = farthest_first(d, k, n)
         both = plain(xt[0, e], a[...]).astype(BF16)
         line[e] = jnp.concatenate([both[:, :split], both[:, local : local + split]], axis=1)
         for j in range(2):
             rest[j, e] = both[:, j * local + split : (j + 1) * local]
 
+    def first_d(k):
+        e = farthest_first(d, k, n)
+
         @pl.when(((d == 0) | (d == n - 1)) & (e != d))
         def _():
             send_d(e)
 
-        return 0
-
-    lax.fori_loop(0, n, down_product, 0)
-
+    def in_product(k, j):
+        e = farthest_first(d, k, n)
+        (keep_a, give_a)[j][e] = jnp.concatenate(
+            [plain(xt[1, e], gp[j]).astype(BF16), rest[j, e]], axis=1
+        )
+
+    turn(0)
+    operand(0).wait()
+    down_product(0)
     turn(1)
     operand(1).wait()
-
-    def in_product(k, _):
-        e = farthest_first(d, k, n)
-        for j, target in ((1, give_a), (0, keep_a)):
-            target[e] = jnp.concatenate(
-                [plain(xt[1, e], gp[j]).astype(BF16), rest[j, e]], axis=1
-            )
-            if j:
-                send_all(0, e)
+    in_product(0, 1)
+
+    heard = jnp.where(s == 0, jnp.where(t == 0, 2, jnp.where(t == 1, 0, 1)), 0)
+    pl.semaphore_wait(barrier, 5 + heard)
+
+    @pl.when((s == 0) & (t == 0))
+    def _():
+        pl.semaphore_signal(here_sem, inc=1, device_id=section, device_id_type=MESH)
+        pl.semaphore_signal(here_sem, inc=1, device_id=slanted, device_id_type=MESH)
+
+    send_all(0, farthest_first(d, 0, n))
+    first_d(0)
+    for i in range(3):
+        share(i).start()
+
+    half = final.shape[0]
+    owner = (s, 0, d)
+    spot = rows_out.at[y, pl.ds(pl.multiple_of(c * half, half), half)]
+
+    @pl.when(t == 0)
+    def _():
+        pltpu.make_async_copy(final, spot, er_sem.at[0]).start()
+
+    direct = (t == 1) | ((t > 1) & (s == 1))
+    aside = (t > 1) & (s == 0)
+
+    @pl.when(t == 1)
+    def _():
+        remote(final, spot, es_sem, er_sem.at[t], owner).start()
+
+    @pl.when(aside)
+    def _():
+        remote(final, out_rows_a, es_sem, rs_sem.at[0], section).start()
+
+    def more_down(k, _):
+        down_product(k)
+        first_d(k)
         return 0
 
-    lax.fori_loop(0, n, in_product, 0)
+    lax.fori_loop(1, n, more_down, 0)
+
+    def more_in(k, _):
+        in_product(k, 1)
+        send_all(0, farthest_first(d, k, n))
+        in_product(k, 0)
+        return 0
+
+    lax.fori_loop(1, n, more_in, 0)
+    in_product(0, 0)
 
     turn(2)
     turn(3)
@@ -1085,15 +1167,7 @@
 
     lax.fori_loop(0, n, other_product, 0)
 
-    half = final.shape[0]
-    owner = (s, 0, d)
-    spot = rows_out.at[y, pl.ds(pl.multiple_of(c * half, half), half)]
-
-    @pl.when(t == 0)
-    def _():
-        pltpu.make_async_copy(final, spot, er_sem.at[0]).start()
-
-    @pl.when(t != 0)
+    @pl.when((t > 1) & (s == 1))
     def _():
         remote(final, spot, es_sem, er_sem.at[t], owner).start()
 
@@ -1185,6 +1259,31 @@
 
     lax.fori_loop(0, n, flows_other, 0)
 
+    second = remote(out_rows_a, out_rows_b, hop_sem.at[0], rs_sem.at[1], across)
+    mine_half = pl.ds(pl.multiple_of(c * half, half), half)
+    third_dst = rows_out.at[1, mine_half]
+
+    def third(device):
+        return remote(out_rows_b, third_dst, hop_sem.at[1], er_sem.at[2 + c], device)
+
+    @pl.when((s == 1) & (t > 1))
+    def _():
+        remote(out_rows_a, out_rows_a, hop_sem.at[0], rs_sem.at[0], section).wait_recv()
+        second.start()
+
+    @pl.when((s == 1) & (t < 2))
+    def _():
+        second.wait_recv()
+        pl.semaphore_wait(here_sem, 1)
+
+    @pl.when((s == 1) & (t == 0))
+    def _():
+        third(section).start()
+
+    @pl.when((s == 1) & (t == 1))
+    def _():
+        third(slanted).start()
+
     def landed(which, i):
         keep, _, yrecv, flow, last = groups[which]
         at = pl.ds(i * step, step)
@@ -1207,6 +1306,12 @@
         below = jnp.where(d < n - 1, last[at].astype(F32), 0.0)
         return (keep[d, at].astype(F32) + yrecv[d, at].astype(F32)) + (above + below)
 
+    results = [
+        pltpu.make_async_copy(src, dst, out_sem.at[i])
+        for i, (src, dst) in enumerate(
+            ((out_q, q_out), (out_k, k_out), (out_v, v_out), (out_u, u_out), (out_o, o_out), (out_d, d_out))
+        )
+    ]
     rests = []
     for i in range(pieces):
         at = pl.ds(i * step, step)
@@ -1214,9 +1319,12 @@
         for j, ref in enumerate((out_q, out_k, out_v)):
             ref[at] = total[:, j * local : (j + 1) * local]
         rests.append(total[:, 3 * local :])
+    for i in range(3):
+        results[i].start()
     crossing.wait_recv()
     most = line[d, :, :split].astype(F32) + yd[...].astype(F32)
     out_d[...] = jnp.transpose(jnp.concatenate([most, jnp.concatenate(rests, axis=0)], axis=1))
+    results[5].start()
     found = smalls[0]
     out_g1[...] = found[0:1, :width]
     out_g2[...] = found[0:1, width : 2 * width]
@@ -1234,7 +1342,9 @@
         total = landed(1, i)
         out_u[pl.ds(i * step, step)] = total[:, :local]
         totals.append(total[:, local:])
+    results[3].start()
     out_o[...] = jnp.transpose(jnp.concatenate(totals, axis=0))
+    results[4].start()
 
     @pl.when(t == 0)
     def _():
@@ -1242,10 +1352,24 @@
             piece = rows_out.at[i // 2, pl.ds(i % 2 * half, half)]
             remote(piece, piece, es_sem, er_sem.at[i], owner).wait_recv()
 
-    @pl.when(t != 0)
+    @pl.when(direct)
     def _():
         remote(final, spot, es_sem, er_sem.at[t], owner).wait_send()
 
+    @pl.when(aside)
+    def _():
+        remote(final, out_rows_a, es_sem, rs_sem.at[0], section).wait_send()
+
+    @pl.when((s == 1) & (t > 1))
+    def _():
+        second.wait_send()
+
+    @pl.when((s == 1) & (t < 2))
+    def _():
+        third(section).wait_send()
+
+    for copy in results:
+        copy.wait()
     crossing.wait_send()
     for i in range(3):
         share(i).wait_send()
@@ -1302,9 +1426,11 @@
             jax.ShapeDtypeStruct(dim_scale.shape, F32),
         ],
         in_specs=[ANY] * 10 + [VMEM] * 4,
-        out_specs=[VMEM] * 6 + [ANY] + [VMEM] * 3,
+        out_specs=[ANY] * 7 + [VMEM] * 3,
         input_output_aliases={9: 6},
-        scratch_shapes=[
+        scratch_shapes=[pltpu.VMEM((chunk, local), F32)] * 4
+        + [pltpu.VMEM((local, chunk), F32)] * 2
+        + [
             pltpu.VMEM((2, length, width), BF16),
             pltpu.VMEM((4, n, chunk, length), BF16),
             pltpu.VMEM(gp.shape, BF16),
@@ -1322,6 +1448,8 @@
             pltpu.VMEM(small, F32),
             pltpu.VMEM((3,) + small, F32),
             pltpu.VMEM((4,) + small, F32),
+            pltpu.VMEM(final.shape, BF16),
+            pltpu.VMEM(final.shape, BF16),
             DMA((4,)),
             DMA((4,)),
         ]
@@ -1339,12 +1467,44 @@
             DMA((2,)),
             DMA,
             DMA((4,)),
+            DMA((6,)),
+            DMA((2,)),
+            DMA((2,)),
+            pltpu.SemaphoreType.REGULAR,
         ],
         compiler_params=pltpu.CompilerParams(
             collective_id=3, has_side_effects=True, vmem_limit_bytes=62 * MIB
         ),
         name="gradients",
     )(n1, n2, gy, g, gp, gu, o, a, final, rows, dg1, dg2, ds, dim_scale)
+
+
+def hand_over_kernel(*refs):
+    count = (len(refs) - 2) // 3
+    sources, results, kept = refs[:count], refs[count : 2 * count], refs[2 * count : 3 * count]
+    in_sem, out_sem = refs[3 * count :]
+    come = [pltpu.make_async_copy(sources[i], kept[i], in_sem.at[i]) for i in range(count)]
+    go = [pltpu.make_async_copy(kept[i], results[i], out_sem.at[i]) for i in range(count)]
+    for copy in come:
+        copy.start()
+    for i in range(count):
+        come[i].wait()
+        go[i].start()
+    for copy in go:
+        copy.wait()
+
+
+def hand_over(arrays):
+    count = len(arrays)
+    return pl.pallas_call(
+        hand_over_kernel,
+        out_shape=[jax.ShapeDtypeStruct(x.shape, x.dtype) for x in arrays],
+        in_specs=[ANY] * count,
+        out_specs=[ANY] * count,
+        scratch_shapes=[pltpu.VMEM(x.shape, x.dtype) for x in arrays] + [DMA((count,)), DMA((count,))],
+        compiler_params=pltpu.CompilerParams(vmem_limit_bytes=62 * MIB),
+        name="hand_over",
+    )(*arrays)
 
 
 def body(
@@ -1366,6 +1526,8 @@
     *pieces, input_grads, dg1, dg2, grad_scale = gradients(
         n1, n2, gy, g_all, gp, gu, o, a, final, input_grads, dg1, dg2, ds, dim_scale
     )
+    results = hand_over([layer_out, input_grads, dg1, *pieces, grad_scale, dg2])
+    layer_out, input_grads, dg1, *pieces, grad_scale, dg2 = results
     return (
         layer_out[None],
         input_grads[None],

time: 348 us -> 333 us (0.957)
  local copies, waits for them, and re-layouts: 9.24 us -> 0 us
  Pallas kernels: 338 us -> 331 us
    unnamed x33 -> x0, local copies, waits for them, and re-layouts: 9.24 us -> none
    pallas_call x1, Pallas kernels: 119 us -> 113 us  [gradients(): pl.pallas_call(gradient_kernel, out_shape=[jax.ShapeDtypeStruct((chunk, l...]
    pallas_call x1, Pallas kernels: 125 us -> 120 us  [backward(): pl.pallas_call(backward_kernel, out_shape=outs, in_specs=[ANY] * 14 + [VM...]
    pallas_call x0 -> x1, Pallas kernels: none -> 4.43 us  [hand_over(): pl.pallas_call(hand_over_kernel, out_shape=[jax.ShapeDtypeStruct(x.shape,...]
where the time goes in v5:
time: 333 us; the launch traced here: 332 us
  Pallas kernels  331 us (99%)
    pallas_call x1, Pallas kernels, backward(): pl.pallas_call(backward_kernel, out_shape=outs, in_specs=[ANY] * 14 + [VM...  120 us
    pallas_call x1, Pallas kernels, gradients(): pl.pallas_call(gradient_kernel, out_shape=[jax.ShapeDtypeStruct((chunk, l...  113 us
    pallas_call x1, Pallas kernels, forward(): pl.pallas_call(forward_kernel, out_shape=outs, in_specs=[ANY] * 8 + [VMEM...  93.4 us

profile of v5, /device:TPU:0, one launch (start us, length us, event | category | flops | bytes accessed | tf_op | source)
XLA Modules:
  0.0 331.9 jit_solution(3612671806536701393)
XLA Ops:
  0.6 93.4 %forward.1 = (bf16[4,128,1280]{2,1,0:T(8,128)(2,1)}, bf16[4,256,1280]{2,1,0:T(8,128)(2,1)}, bf16[1024,1280]{1,0:T(8,128)(2,1)}, bf16[8,1024,80]{2,1,0:T(8,128)(2...) custom-call(bf16[2,256,1280]{2,1,0:T(8,128)(2,1)} %inputs.1, ...), custom_call_target="tpu_custom_call" | custom-call | tf_op jit(solution)/shard_map/forward/pallas_call | solution.py:544
  94.1 120.0 %backward.1 = (bf16[2,256,1280]{2,1,0:T(8,128)(2,1)}, bf16[2,256,1280]{2,1,0:T(8,128)(2,1)}, bf16[128,1280]{1,0:T(8,128)(2,1)}, bf16[1024,1280]{1,0:T(8,128)(2,1...) custom-call(bf16[4,256,1280]{2,1,0:T(8,128)(2,1)} %get-tuple-element, ...), custom_call_target="tpu_custom_call" | custom-call | tf_op jit(solution)/shard_map/backward/pallas_call | solution.py:942
  214.1 113.2 %gradients.1 = (f32[320,320]{1,0:T(8,128)}, f32[320,320]{1,0:T(8,128)}, f32[320,320]{1,0:T(8,128)}, f32[320,320]{1,0:T(8,128)}, f32[320,320]{1,0:T(8,128)}, /*in...) custom-call(bf16[1024,1280]{1,0:T(8,128)(2,1)} %get-tuple-element.74, ...), custom_call_target="tpu_custom_call", output_to_operand_aliasing={{6}: (9, {})} | custom-call | tf_op jit(solution)/shard_map/gradients/pallas_call | solution.py:1418
  327.3 4.4 %hand_over.1 = (bf16[2,256,1280]{2,1,0:T(8,128)(2,1)}, bf16[2,256,1280]{2,1,0:T(8,128)(2,1)}, f32[1,1280]{1,0:T(1,128)}, f32[320,320]{1,0:T(8,128)}, f32[320,320...) custom-call(bf16[2,256,1280]{2,1,0:T(8,128)(2,1)} %get-tuple-element, ...), custom_call_target="tpu_custom_call" | custom-call | tf_op jit(solution)/shard_map/hand_over/pallas_call | solution.py:1499

commit v6 on v5

--- a/solution.py
+++ b/solution.py
@@ -337,17 +337,19 @@
 
         return 0
 
-    lax.fori_loop(0, 2 * blocks, attention, 0)
-
-    own(3).wait()
-    arrived(6)
-    arrived(7)
-
     def project(b, _):
+        @pl.when(b == 0)
+        def _():
+            own(3).wait()
+            arrived(6)
+            arrived(7)
+
         at = pl.ds(pl.multiple_of(b * rows, rows), rows)
         ysend[b] = plain(o[at], wo[...]).astype(BF16)
         remote(ysend.at[b], yrecv.at[b], ys_sem.at[b], yr_sem.at[b], core).start()
         return 0
+
+    lax.fori_loop(0, 2 * blocks, attention, 0)
 
     lax.fori_loop(0, blocks, project, 0)
 
@@ -614,6 +616,15 @@
     for device in (core, across, diagonal, section):
         pl.semaphore_signal(barrier, inc=1, device_id=device, device_id_type=MESH)
 
+    weight(2).start()
+    for kind in (2, 3, 6):
+        load(kind, last).start()
+    for bb in reversed(range(blocks)):
+        load(4, bb).start()
+        load(5, bb).start()
+    weight(3).start()
+    load(7, last).start()
+
     spot = out_rows.at[y, mine]
 
     def owner_copy(b, src, dst, send, receive, act):
@@ -637,13 +648,16 @@
     row_head = lax.broadcasted_iota(jnp.int32, (heads, width_two), 0)
     start = row_head * head
     place = lax.broadcasted_iota(jnp.int32, (heads, width_two), 1)
-    member = jnp.where((place >= start) & (place < start + head), 1.0, 0.0)
+    member = jnp.where((place >= start) & (place < start + head), 1.0, 0.0).astype(BF16)
 
     def save(kind, b, src, dst):
         pltpu.make_async_copy(src, dst, save_sem.at[kind, b]).start()
 
-    def neighbours_sum(b):
-        return remote(ysend.at[b], yrecv.at[b], ys_sem.at[b], yr_sem.at[b], core)
+    def neighbours_sum(b, i):
+        lanes = pl.ds(i * (width // 2), width // 2)
+        return remote(
+            ysend.at[b, :, lanes], yrecv.at[b, :, lanes], ys_sem.at[i, b], yr_sem.at[i, b], core
+        )
 
     def up_part(turn):
         b = last - turn
@@ -681,16 +695,12 @@
         @pl.when(turn == 0)
         def _():
             weight(1).wait()
-            weight(2).start()
-            for kind in (2, 3, 6):
-                load(kind, last).start()
-            for bb in reversed(range(blocks)):
-                load(4, bb).start()
-                load(5, bb).start()
 
         save(1, b, gu.at[at], gu_out.at[at])
-        ysend[b] = plain(grad_up, wu[...]).astype(BF16)
-        neighbours_sum(b).start()
+        for i in range(2):
+            lanes = slice(i * (width // 2), (i + 1) * (width // 2))
+            ysend[b, :, lanes] = plain(grad_up, wu[:, lanes]).astype(BF16)
+            neighbours_sum(b, i).start()
 
         @pl.when(turn == 0)
         def _():
@@ -703,7 +713,8 @@
         b = last - turn
         at = pl.ds(pl.multiple_of(b * rows, rows), rows)
         load(1, b).wait()
-        neighbours_sum(b).wait_recv()
+        for i in range(2):
+            neighbours_sum(b, i).wait_recv()
         grad = g[b]
         grad_normed = ysend[b].astype(F32) + yrecv[b].astype(F32)
         middle = m[b]
@@ -722,19 +733,13 @@
         @pl.when(turn == 0)
         def _():
             weight(2).wait()
-            weight(3).start()
-            load(7, last).start()
 
         load(2, b).wait()
         grad_mixed = by_last(grad_mid, wo[...]).astype(BF16)
         both = grad_mixed.astype(F32) * o[at].astype(F32)
-        delta[...] = lax.dot_general(
-            member,
-            both,
-            (((1,), (1,)), ((), ())),
-            precision=lax.Precision.HIGHEST,
-            preferred_element_type=F32,
-        )
+        high = both.astype(BF16)
+        low = (both - high.astype(F32)).astype(BF16)
+        delta[...] = by_last(member, high) + by_last(member, low)
         for i in range(heads):
             go_heads[i] = grad_mixed[:, i * head : (i + 1) * head]
 
@@ -851,7 +856,8 @@
     for b in range(blocks):
         at = pl.ds(b * rows, rows)
         piece = g.at[b, mine]
-        remote(ysend.at[b], yrecv.at[b], ys_sem.at[b], yr_sem.at[b], core).wait_send()
+        for i in range(2):
+            neighbours_sum(b, i).wait_send()
         here = x_rows.at[b // 2, pl.ds((b % 2) * half, half)]
         remote(here, here, xs_sem.at[b], xr_sem.at[b], core).wait_recv()
 
@@ -938,7 +944,7 @@
         DMA((8, blocks)),
         DMA((4,)),
     ]
-    scratch += [DMA((blocks,))] * 12 + [DMA((5, blocks))]
+    scratch += [DMA((blocks,))] * 4 + [DMA((2, blocks))] * 2 + [DMA((blocks,))] * 6 + [DMA((5, blocks))]
     return pl.pallas_call(
         backward_kernel,
         out_shape=outs,
@@ -1142,7 +1148,11 @@
 
     def more_in(k, _):
         in_product(k, 1)
-        send_all(0, farthest_first(d, k, n))
+
+        @pl.when(k < n - 1)
+        def _():
+            send_all(0, farthest_first(d, k, n))
+
         in_product(k, 0)
         return 0
 
@@ -1162,10 +1172,16 @@
             cut = slice(j * local, (j + 1) * local)
             target[e] = jnp.concatenate([ups[:, cut], outs[:, cut]], axis=1).astype(BF16)
             if j:
-                send_all(1, e)
+
+                @pl.when(k < n - 1)
+                def _():
+                    send_all(1, e)
+
         return 0
 
     lax.fori_loop(0, n, other_product, 0)
+    send_all(0, d)
+    send_all(1, d)
 
     @pl.when((t > 1) & (s == 1))
     def _():
@@ -1243,7 +1259,7 @@
         flows(1, k)
         return 0
 
-    lax.fori_loop(0, n, flows_in, 0)
+    lax.fori_loop(0, n - 1, flows_in, 0)
 
     @pl.when(d > 0)
     def _():
@@ -1257,7 +1273,7 @@
     crossing = remote(line.at[d, :, pl.ds(split, split)], yd, yds_sem, ydr_sem, across)
     crossing.start()
 
-    lax.fori_loop(0, n, flows_other, 0)
+    lax.fori_loop(0, n - 1, flows_other, 0)
 
     second = remote(out_rows_a, out_rows_b, hop_sem.at[0], rs_sem.at[1], across)
     mine_half = pl.ds(pl.multiple_of(c * half, half), half)
@@ -1287,6 +1303,7 @@
     def landed(which, i):
         keep, _, yrecv, flow, last = groups[which]
         at = pl.ds(i * step, step)
+        exchange(which, d, i).wait_recv()
 
         @pl.when(d > 0)
         def _():
@@ -1321,10 +1338,6 @@
         rests.append(total[:, 3 * local :])
     for i in range(3):
         results[i].start()
-    crossing.wait_recv()
-    most = line[d, :, :split].astype(F32) + yd[...].astype(F32)
-    out_d[...] = jnp.transpose(jnp.concatenate([most, jnp.concatenate(rests, axis=0)], axis=1))
-    results[5].start()
     found = smalls[0]
     out_g1[...] = found[0:1, :width]
     out_g2[...] = found[0:1, width : 2 * width]
@@ -1345,6 +1358,10 @@
     results[3].start()
     out_o[...] = jnp.transpose(jnp.concatenate(totals, axis=0))
     results[4].start()
+    crossing.wait_recv()
+    most = line[d, :, :split].astype(F32) + yd[...].astype(F32)
+    out_d[...] = jnp.transpose(jnp.concatenate([most, jnp.concatenate(rests, axis=0)], axis=1))
+    results[5].start()
 
     @pl.when(t == 0)
     def _():

time: 333 us -> 331 us (level)
  no operation moved by 1% of the time
where the time goes in v6:
time: 331 us; the launch traced here: 330 us
  Pallas kernels  329 us (99%)
    pallas_call x1, Pallas kernels, backward(): pl.pallas_call(backward_kernel, out_shape=outs, in_specs=[ANY] * 14 + [VM...  118 us
    pallas_call x1, Pallas kernels, gradients(): pl.pallas_call(gradient_kernel, out_shape=[jax.ShapeDtypeStruct((chunk, l...  113 us
    pallas_call x1, Pallas kernels, forward(): pl.pallas_call(forward_kernel, out_shape=outs, in_specs=[ANY] * 8 + [VMEM...  93.4 us

profile of v6, /device:TPU:0, one launch (start us, length us, event | category | flops | bytes accessed | tf_op | source)
XLA Modules:
  0.0 329.5 jit_solution(16308390764859362101)
XLA Ops:
  0.6 93.4 %forward.1 = (bf16[4,128,1280]{2,1,0:T(8,128)(2,1)}, bf16[4,256,1280]{2,1,0:T(8,128)(2,1)}, bf16[1024,1280]{1,0:T(8,128)(2,1)}, bf16[8,1024,80]{2,1,0:T(8,128)(2...) custom-call(bf16[2,256,1280]{2,1,0:T(8,128)(2,1)} %inputs.1, ...), custom_call_target="tpu_custom_call" | custom-call | tf_op jit(solution)/shard_map/forward/pallas_call | solution.py:546
  94.1 117.6 %backward.1 = (bf16[2,256,1280]{2,1,0:T(8,128)(2,1)}, bf16[2,256,1280]{2,1,0:T(8,128)(2,1)}, bf16[128,1280]{1,0:T(8,128)(2,1)}, bf16[1024,1280]{1,0:T(8,128)(2,1...) custom-call(bf16[4,256,1280]{2,1,0:T(8,128)(2,1)} %get-tuple-element, ...), custom_call_target="tpu_custom_call" | custom-call | tf_op jit(solution)/shard_map/backward/pallas_call | solution.py:948
  211.7 113.2 %gradients.1 = (f32[320,320]{1,0:T(8,128)}, f32[320,320]{1,0:T(8,128)}, f32[320,320]{1,0:T(8,128)}, f32[320,320]{1,0:T(8,128)}, f32[320,320]{1,0:T(8,128)}, /*in...) custom-call(bf16[1024,1280]{1,0:T(8,128)(2,1)} %get-tuple-element.74, ...), custom_call_target="tpu_custom_call", output_to_operand_aliasing={{6}: (9, {})} | custom-call | tf_op jit(solution)/shard_map/gradients/pallas_call | solution.py:1435
  324.9 4.4 %hand_over.1 = (bf16[2,256,1280]{2,1,0:T(8,128)(2,1)}, bf16[2,256,1280]{2,1,0:T(8,128)(2,1)}, f32[1,1280]{1,0:T(1,128)}, f32[320,320]{1,0:T(8,128)}, f32[320,320...) custom-call(bf16[2,256,1280]{2,1,0:T(8,128)(2,1)} %get-tuple-element, ...), custom_call_target="tpu_custom_call" | custom-call | tf_op jit(solution)/shard_map/hand_over/pallas_call | solution.py:1516

commit v7 on v6

--- a/solution.py
+++ b/solution.py
@@ -182,7 +182,6 @@
             remote(piece, piece, xfs_sem, xp_sem.at[i], core).wait_recv()
         piece = land.at[0, t_across]
         remote(piece, piece, xfs_sem, xr_sem.at[t_across], core).start()
-        block_wait(t_diagonal)
 
     def near_rows():
         block_wait(t)
@@ -252,6 +251,7 @@
             for i in range(4):
                 relay(i)
             far_rows()
+            block_wait(t_diagonal)
 
         @pl.when((s == 0) & (turn == blocks))
         def _():
@@ -399,6 +399,11 @@
         def _():
             finish(b - 1)
 
+        @pl.when((s == 1) & (b == blocks - 2))
+        def _():
+            near_rows()
+            far_rows()
+
         return 0
 
     def finish(b):
@@ -421,8 +426,7 @@
 
     @pl.when(s == 1)
     def _():
-        near_rows()
-        far_rows()
+        block_wait(t_diagonal)
 
     for b in range(blocks):
         pltpu.make_async_copy(land.at[0, b], g_out.at[b], save_sem.at[12, b]).start()

time: 331 us -> 329 us (level)
  no operation moved by 1% of the time
where the time goes in v7:
time: 329 us; the launch traced here: 328 us
  Pallas kernels  327 us (99%)
    pallas_call x1, Pallas kernels, backward(): pl.pallas_call(backward_kernel, out_shape=outs, in_specs=[ANY] * 14 + [VM...  116 us
    pallas_call x1, Pallas kernels, gradients(): pl.pallas_call(gradient_kernel, out_shape=[jax.ShapeDtypeStruct((chunk, l...  113 us
    pallas_call x1, Pallas kernels, forward(): pl.pallas_call(forward_kernel, out_shape=outs, in_specs=[ANY] * 8 + [VMEM...  93.4 us

profile of v7, /device:TPU:0, one launch (start us, length us, event | category | flops | bytes accessed | tf_op | source)
XLA Modules:
  0.0 327.9 jit_solution(2590014154628718806)
XLA Ops:
  0.6 93.4 %forward.1 = (bf16[4,128,1280]{2,1,0:T(8,128)(2,1)}, bf16[4,256,1280]{2,1,0:T(8,128)(2,1)}, bf16[1024,1280]{1,0:T(8,128)(2,1)}, bf16[8,1024,80]{2,1,0:T(8,128)(2...) custom-call(bf16[2,256,1280]{2,1,0:T(8,128)(2,1)} %inputs.1, ...), custom_call_target="tpu_custom_call" | custom-call | tf_op jit(solution)/shard_map/forward/pallas_call | solution.py:550
  94.1 116.0 %backward.1 = (bf16[2,256,1280]{2,1,0:T(8,128)(2,1)}, bf16[2,256,1280]{2,1,0:T(8,128)(2,1)}, bf16[128,1280]{1,0:T(8,128)(2,1)}, bf16[1024,1280]{1,0:T(8,128)(2,1...) custom-call(bf16[4,256,1280]{2,1,0:T(8,128)(2,1)} %get-tuple-element, ...), custom_call_target="tpu_custom_call" | custom-call | tf_op jit(solution)/shard_map/backward/pallas_call | solution.py:952
  210.0 113.2 %gradients.1 = (f32[320,320]{1,0:T(8,128)}, f32[320,320]{1,0:T(8,128)}, f32[320,320]{1,0:T(8,128)}, f32[320,320]{1,0:T(8,128)}, f32[320,320]{1,0:T(8,128)}, /*in...) custom-call(bf16[1024,1280]{1,0:T(8,128)(2,1)} %get-tuple-element.74, ...), custom_call_target="tpu_custom_call", output_to_operand_aliasing={{6}: (9, {})} | custom-call | tf_op jit(solution)/shard_map/gradients/pallas_call | solution.py:1439
  323.2 4.4 %hand_over.1 = (bf16[2,256,1280]{2,1,0:T(8,128)(2,1)}, bf16[2,256,1280]{2,1,0:T(8,128)(2,1)}, f32[1,1280]{1,0:T(1,128)}, f32[320,320]{1,0:T(8,128)}, f32[320,320...) custom-call(bf16[2,256,1280]{2,1,0:T(8,128)(2,1)} %get-tuple-element, ...), custom_call_target="tpu_custom_call" | custom-call | tf_op jit(solution)/shard_map/hand_over/pallas_call | solution.py:1520
